TPU v7x, 32 devices: a whole 2x2x4 slice. The times are simulated.
32 devices in a mesh: graph: 16 (over z, y, x), mp: 2 (over core).
Axes of the slice: x: 2, y: 2, z: 4, core: 2. Of those that a mesh axis runs over, the one named last changes fastest.
Arguments:
- messages: bfloat16 [16384, 512], P('graph', 'mp'), may hold values from -6 to 6
- basis_blocks: bfloat16 [1536, 128, 128], P('graph'), may hold values from -0.5 to 0.5
- source_block: int32 [1536], P('graph'), may hold values from 0 to 7
- target_owner: int32 [1536, 1], P('graph'), may hold values from 0 to 15; in each aligned block of 96 rows (0 to 95, 96 to 191, ...) at most 7 rows name the same one
- target_block: int32 [1536], P('graph'), may hold values from 0 to 7
- row_counts: int32 [1536], P('graph'), may hold values from 1 to 128
- reverse_block: int32 [128], P('graph'), may hold values from 0 to 127, as said below
- valid_edges: int32 [16], P('graph'), may hold values from 512 to 1024
- weight_in: bfloat16 [3, 512, 512], P(None, None, 'mp'), may hold values from -0.25 to 0.25
- weight_out: bfloat16 [3, 512, 512], P(None, 'mp'), may hold values from -0.25 to 0.25
Outputs:
- updated: bfloat16 [16384, 512], P('graph', 'mp')
Inputs may be any that keep to these rules, and one draw needn't show every extreme that they name: `target_owner`: among the 96 triplet blocks of one device, no owner is named more than 7 times, a bound that some block reaches. `reverse_block`: an involution on edge blocks. Of device g's 8 blocks, the first 2 pair with blocks 2 to 3 of device (g - 1) mod 16, blocks 2 to 3 pair with the first 2 of device (g + 1) mod 16, and the others pair with blocks of device g itself.
All inputs are finite; a program needn't handle non-finite values.
Results may differ from a plain program's by a relative error of at most 0.0073.
Values may be sent and summed in bfloat16 or wider, within the bound.
No kernel may reach another device: no remote copies, remote signals or barrier semaphores. Data moves between devices by JAX's collectives and lax.ppermute only.
A program may use at most 128 MiB of HBM per device.

v0:
```python
import jax
import jax.numpy as jnp
from jax import lax
from jax.sharding import PartitionSpec as P

MLPS = 3
BLK = 128


pair_scale = 0.7071067811865476


def padded_2(array, sides, width):
    for axis, dim in sides:
        size, length = (lax.axis_size(axis), array.shape[dim])
        up = [(i, (i + 1) % size) for i in range(size)]
        down = [(j, i) for i, j in up]
        last = lax.slice_in_dim(array, length - width, length, axis=dim)
        leading = lax.slice_in_dim(array, 0, width, axis=dim)
        before = lax.ppermute(last, axis, up)
        after = lax.ppermute(leading, axis, down)
        array = jnp.concatenate([before, array, after], axis=dim)
    return array


def place_slots(values, place, devices, capacity):
    shape_rest = values.shape[1:]
    padded = jnp.zeros((devices * capacity,) + shape_rest, values.dtype).at[place].set(values)
    return padded.reshape((devices, capacity) + shape_rest)


def sum_into_blocks(incoming, arrived, blocks):
    count_all = arrived.shape[0]
    rows, cols = (incoming.shape[1], incoming.shape[2])
    selector = (jnp.arange(blocks, dtype=jnp.int32)[:, None] == arrived[None, :]).astype(
        jnp.bfloat16
    )
    summed = jnp.dot(
        selector, incoming.reshape(count_all, rows * cols), preferred_element_type=jnp.float32
    )
    return summed.reshape(blocks, rows, cols)


def masked_products(basis_rows, source_data, own_rows, counts):
    products = jnp.einsum(
        "str,src->stc", basis_rows, source_data, preferred_element_type=jnp.float32
    )
    keep = own_rows[None, :] < counts[:, None]
    return jnp.where(keep[:, :, None], products, 0.0).astype(jnp.bfloat16)


def reverse_pairs(combined, reverse_block, this_device, devices, blocks, border):
    leading = combined[: 2 * border]
    extended = padded_2(leading, (("graph", 0),), border)
    lower_rim = extended[:border]
    upper_rim = extended[3 * border :]
    full = jnp.concatenate([lower_rim, combined, upper_rim], axis=0)
    holder = reverse_block // blocks
    within = reverse_block % blocks
    before = (this_device - 1) % devices
    local_index = jnp.where(
        holder == this_device,
        border + within,
        jnp.where(holder == before, within - border, border + blocks + within),
    )
    return full[local_index]


def local(
    messages,
    basis_blocks,
    source_block,
    target_owner,
    target_block,
    row_counts,
    reverse_block,
    valid_edges,
    weight_in,
    weight_out,
):
    devices = lax.axis_size("graph")
    this_device = lax.axis_index("graph")
    edge_rows, part_width = messages.shape
    blocks = edge_rows // BLK
    slots = source_block.shape[0]
    capacity = max(2, (slots + devices - 1) // devices + 1)
    border = blocks // 4
    owners = target_owner[:, 0]
    slot_index = jnp.arange(slots, dtype=jnp.int32)
    same_owner = (owners[:, None] == owners[None, :]) & (slot_index[None, :] < slot_index[:, None])
    earlier = jnp.sum(same_owner.astype(jnp.int32), axis=1)
    place = owners * capacity + earlier
    row_share = BLK // lax.axis_size("mp")
    first_row = lax.axis_index("mp") * row_share
    full_messages = lax.all_gather(messages, "mp", axis=1, tiled=True)
    full_blocks = full_messages.reshape(blocks, BLK, full_messages.shape[1])
    basis_rows = lax.dynamic_slice_in_dim(basis_blocks, first_row, row_share, 1)
    local_rows = lax.dynamic_slice_in_dim(full_blocks, first_row, row_share, 1)
    own_rows = first_row + jnp.arange(row_share, dtype=jnp.int32)
    source_data = full_blocks[source_block]
    products = masked_products(basis_rows, source_data, own_rows, row_counts)
    out_products = place_slots(products, place, devices, capacity)
    out_labels = place_slots(target_block, place, devices, capacity)
    incoming, arrived = (
        lax.all_to_all(out_products, "graph", split_axis=0, concat_axis=0, tiled=True),
        lax.all_to_all(out_labels, "graph", split_axis=0, concat_axis=0, tiled=True),
    )
    arrived_count = devices * capacity
    aggregate = sum_into_blocks(
        incoming.reshape((arrived_count,) + incoming.shape[2:]), arrived.reshape(-1), blocks
    )
    combined = (local_rows.astype(jnp.float32) + aggregate).astype(jnp.bfloat16)
    swapped = reverse_pairs(combined, reverse_block, this_device, devices, blocks, border)
    state = (combined.astype(jnp.float32) + swapped.astype(jnp.float32)) * pair_scale
    width_here = state.shape[2]
    state = state.reshape(blocks * row_share, width_here)
    position = (jnp.arange(blocks, dtype=jnp.int32)[:, None] * BLK + own_rows[None, :]).reshape(-1)
    keep_edge = position < valid_edges[0]
    weights_in, weights_out = (
        lax.all_gather(weight_in, "mp", axis=2, tiled=True),
        lax.all_gather(weight_out, "mp", axis=1, tiled=True),
    )
    for layer in range(MLPS):
        layer_input = state.astype(jnp.bfloat16)
        hidden = jax.nn.silu(
            jnp.dot(layer_input, weights_in[layer], preferred_element_type=jnp.float32)
        ).astype(jnp.bfloat16)
        state = state + jnp.dot(hidden, weights_out[layer], preferred_element_type=jnp.float32)
    final = jnp.where(keep_edge[:, None], state, 0.0).astype(jnp.bfloat16)
    final = final.reshape(blocks, row_share, width_here)
    columns = lax.all_to_all(final, "mp", split_axis=2, concat_axis=1, tiled=True)
    return columns.reshape(edge_rows, part_width)


def solution(mesh):
    in_specs = (
        P("graph", "mp"),
        P("graph", None, None),
        P("graph"),
        P("graph", None),
        P("graph"),
        P("graph"),
        P("graph"),
        P("graph"),
        P(None, None, "mp"),
        P(None, "mp", None),
    )
    out_specs = P("graph", "mp")
    return jax.shard_map(local, mesh=mesh, in_specs=in_specs, out_specs=out_specs, check_vma=False)
```

profile of v0, /device:TPU:25, one launch (start us, length us, event | category | flops | bytes accessed | tf_op | source)
XLA Modules:
  0.0 295.5 jit_solution(2174836113618519510)
XLA Ops:
  7.3 1.1 convert_reduce_fusion
  9.0 1.0 scatter_custom_fusion
  10.7 6.4 %all-to-all-start = ((s32[16,1,7]{2,1,0:T(1,128)}), s32[16,1,7]{2,1,0:T(1,128)S(1)}, u32[]{:S(2)}, u32[]{:S(2)}) async-start(s32[16,1,7]{2,1,0:T(1,128)} %bitcast.5), calls=%async_computation | async-start | bytes 16384 | tf_op jit(solution)/shard_map/all_to_all | solution.py:106
  17.8 0.7 broadcast_compare_fusion
  18.6 1.1 all-gather.4.cloned.1.call-done
  19.6 8.0 %gather_fusion = bf16[96,128,512]{2,1,0:T(8,128)(2,1)} fusion(bf16[8,128,512]{2,1,0:T(8,128)(2,1)} %bitcast.72, s32[1024]{0:T(1024)S(1)} %pad_clamp_fusion.1), kind=kCustom, calls=%fused_computation | custom fusion | bytes 25166208 | tf_op jit(solution)/shard_map/gather | solution.py:100
  27.7 7.2 %select_convert_fusion = bf16[96,64,512]{2,1,0:T(8,128)(2,1)} fusion(pred[96,64]{1,0:T(8,128)(4,1)S(1)} %broadcast_compare_fusion, bf16[96,128,512]{2,1,0:T(8,128)(2,1)} %gather_fusion, bf16[96,128,128]{2,1,0:T(8,128)(2,1)S(1)} %copy-done, s32[]{:T(128)S(6)} %select_n.47), kind=kOutput, calls=%fused_computation.4 | convolution fusion | flops 811597824 | bytes 20459524 | tf_op jit(solution)/shard_map/str,src->stc/dot_general | solution.py:45
  34.9 3.9 %broadcast_in_dim.49 = bf16[112,64,512]{2,1,0:T(8,128)(2,1)} broadcast(bf16[]{:T(256)} %constant.67.clone.1), dimensions={} | broadcast | bytes 7340034 | tf_op jit(solution)/shard_map/broadcast_in_dim | solution.py:28
  38.8 17.7 %scatter_fusion = bf16[112,64,512]{2,1,0:T(8,128)(2,1)} fusion(bf16[112,64,512]{2,1,0:T(8,128)(2,1)} %broadcast_in_dim.49, s32[96]{0:T(128)S(1)} %fusion.26, bf16[96,64,512]{2,1,0:T(8,128)(2,1)} %select_convert_fusion), kind=kCustom, calls=%fused_computation.3 | custom fusion | bytes 18874752 | tf_op jit(solution)/shard_map/scatter | solution.py:28
  56.6 6.4 %all-to-all-start.1 = ((bf16[16,7,64,512]{3,2,1,0:T(8,128)(2,1)}), bf16[16,7,64,512]{3,2,1,0:T(8,128)(2,1)}, u32[]{:S(2)}, u32[]{:S(2)}) async-start(bf16[16,7,64,512]{3,2,1,0:T(8,128)(2,1)} %bitcast.74), calls=%async_computation.1 | async-start | bytes 14680064 | tf_op jit(solution)/shard_map/all_to_all | solution.py:105
  66.5 1.9 constant_dynamic-slice_fusion
  68.3 151.3 %all-to-all-done.1 = bf16[16,7,64,512]{3,2,1,0:T(8,128)(2,1)} async-done(((bf16[16,7,64,512]{3,2,1,0:T(8,128)(2,1)}), bf16[16,7,64,512]{3,2,1,0:T(8,128)(2,1)}, u32[]{:S(2)}, u32[]{:S(2)}) %all-to-all-start.1) | async-done | bytes 7340064 | tf_op jit(solution)/shard_map/all_to_all | solution.py:105
  219.6 11.3 %fusion.8 = bf16[8,64,512]{2,0,1:T(8,128)(2,1)S(1)} fusion(bf16[8,64,512]{2,1,0:T(8,128)(2,1)} %constant_dynamic-slice_fusion, s32[112]{0:T(128)S(1)} %eq.51, bf16[14,8,64,512]{3,2,1,0:T(8,128)(2,1)} %bitcast.25), kind=kOutput, calls=%fused_computation.14 | convolution fusion | flops 59507584 | bytes 8389056 | tf_op jit(solution)/shard_map/dot_general | solution.py:38
  231.0 0.8 copy-done.1
  231.8 0.8 fusion.34
  232.6 7.9 %collective-permute-start.1 = (bf16[2,64,512]{2,0,1:T(2,128)(2,1)S(1)}, bf16[2,64,512]{2,0,1:T(2,128)(2,1)S(1)}, u32[]{:S(2)}, u32[]{:S(2)}) collective-permute-start(bf16[2,64,512]{2,0,1:T(2,128)(2,1)S(1)} %get-tuple-element.8), channel_id=1, source_target_pairs={{2,0},{4,2},{6,4},{8,6},{10,8},{12,10},{14,12},{16,14},{18,16},{20... | collective-permute-start | bytes 393224 | tf_op jit(solution)/shard_map/ppermute | solution.py:21
  240.6 2.5 collective-permute-done
  243.1 6.6 %collective-permute-done.1 = bf16[2,64,512]{2,0,1:T(2,128)(2,1)S(1)} collective-permute-done((bf16[2,64,512]{2,0,1:T(2,128)(2,1)S(1)}, bf16[2,64,512]{2,0,1:T(2,128)(2,1)S(1)}, u32[]{:S(2)}, u32[]{:S(2)}) %collective-permute-start.1) | collective-permute-done | bytes 131104 | tf_op jit(solution)/shard_map/ppermute | solution.py:21
  249.7 1.7 pad_maximum_fusion
  251.3 1.3 copy.32
  252.7 2.5 gather_fusion.1
  255.2 1.6 fusion.33
  256.8 1.6 copy.34
  258.4 0.9 copy.35
  259.3 3.6 %convolution_add_fusion.2 = f32[512,512]{1,0:T(8,128)} fusion(f32[512,512]{1,0:T(8,128)} %bitcast.77, bf16[3,512,512]{2,1,0:T(8,128)(2,1)} %all-gather.8.cloned.1.call-done, bf16[512,512]{1,0:T(8,128)(2,1)} %bitcast.79, bf16[3,512,512]{2,1,0:T(8,128)(2,1)} %all-gather.6.cloned.1.call-done), kind=kOutput, calls=%fused_computation.11 | convolution fusion | flops 538443776 | bytes 3670016 | tf_op jit(solution)/shard_map/dot_general | solution.py:128
  262.9 3.7 %convolution_add_fusion.1 = f32[512,512]{1,0:T(8,128)} fusion(f32[512,512]{1,0:T(8,128)} %convolution_add_fusion.2, bf16[3,512,512]{2,1,0:T(8,128)(2,1)} %all-gather.8.cloned.1.call-done, bf16[3,512,512]{2,1,0:T(8,128)(2,1)} %all-gather.6.cloned.1.call-done), kind=kOutput, calls=%fused_computation.10 | convolution fusion | flops 538705920 | bytes 4194304 | tf_op jit(solution)/shard_map/dot_general | solution.py:128
  266.6 3.6 %fusion.11 = bf16[512,512]{1,0:T(8,128)(2,1)} fusion(f32[512,512]{1,0:T(8,128)} %convolution_add_fusion.1, bf16[3,512,512]{2,1,0:T(8,128)(2,1)} %all-gather.8.cloned.1.call-done, bf16[3,512,512]{2,1,0:T(8,128)(2,1)} %all-gather.6.cloned.1.call-done, pred[512]{0:T(512)(128)(4,1)S(1)} %lt.72), kind=kOutput, calls=%fused_computation.15 | convolution fusion | flops 539230208 | bytes 3670528 | tf_op jit(solution)/shard_map/dot_general | solution.py:128
  270.2 2.7 copy.36
  272.9 2.6 reshape.131
  275.5 8.3 %all_to_all.29 = bf16[2,2,65536]{2,1,0:T(2,128)(2,1)} all-to-all(bf16[2,2,65536]{2,1,0:T(2,128)(2,1)} %reshape.131), channel_id=1, replica_groups=mesh['graph'=16,'mp'=2] {'mp'}, dimensions={0} | all-to-all | bytes 1048576 | tf_op jit(solution)/shard_map/all_to_all | solution.py:131
  283.8 2.5 reshape.132
  286.3 2.6 copy.37
  (28 shorter events, 5.7 us)
Async XLA Ops:
  6.5 21.1 %copy-start = (bf16[96,128,128]{2,1,0:T(8,128)(2,1)S(1)}, bf16[96,128,128]{2,1,0:T(8,128)(2,1)}, u32[]{:S(2)}) copy-start(bf16[96,128,128]{2,1,0:T(8,128)(2,1)} %param.11) | copy-start | bytes 9437188
  6.5 13.1 %all-gather.4.cloned.1.call-start = ((), (), s32[]{:S(2)}) async-start(), calls=%async_computation.3 | async-start | bytes 1572864 | tf_op jit(solution)/shard_map/all_gather | solution.py:95
  10.7 45.9 %all-to-all-start = ((s32[16,1,7]{2,1,0:T(1,128)}), s32[16,1,7]{2,1,0:T(1,128)S(1)}, u32[]{:S(2)}, u32[]{:S(2)}) async-start(s32[16,1,7]{2,1,0:T(1,128)} %bitcast.5), calls=%async_computation | async-start | bytes 16384 | tf_op jit(solution)/shard_map/all_to_all | solution.py:106
  56.6 163.1 %all-to-all-start.1 = ((bf16[16,7,64,512]{3,2,1,0:T(8,128)(2,1)}), bf16[16,7,64,512]{3,2,1,0:T(8,128)(2,1)}, u32[]{:S(2)}, u32[]{:S(2)}) async-start(bf16[16,7,64,512]{3,2,1,0:T(8,128)(2,1)} %bitcast.74), calls=%async_computation.1 | async-start | bytes 14680064 | tf_op jit(solution)/shard_map/all_to_all | solution.py:105
  62.9 196.4 %all-gather.6.cloned.1.call-start = ((), (), s32[]{:S(2)}) async-start(), calls=%async_computation.4 | async-start | bytes 2359296 | tf_op jit(solution)/shard_map/all_gather | solution.py:120
  63.7 195.7 %all-gather.8.cloned.1.call-start = ((), (), s32[]{:S(2)}) async-start(), calls=%async_computation.5 | async-start | bytes 2359296 | tf_op jit(solution)/shard_map/all_gather | solution.py:121
  219.6 20.9 %copy-start.2 = (s32[8]{0:T(128)S(1)}, s32[8]{0:T(128)}, u32[]{:S(2)}) copy-start(s32[8]{0:T(128)} %param.16) | copy-start | bytes 100
  231.0 0.8 copy-start.1
  232.6 10.5 %collective-permute-start = (bf16[2,64,512]{2,0,1:T(2,128)(2,1)}, bf16[2,64,512]{2,0,1:T(2,128)(2,1)S(1)}, u32[]{:S(2)}, u32[]{:S(2)}) collective-permute-start(bf16[2,64,512]{2,0,1:T(2,128)(2,1)} %get-tuple-element.7), channel_id=1, source_target_pairs={{0,2},{2,4},{4,6},{6,8},{8,10},{10,12},{12,14},{14,16},{16,18},{18... | collective-permute-start | bytes 393224 | tf_op jit(solution)/shard_map/ppermute | solution.py:20
  232.6 17.1 %collective-permute-start.1 = (bf16[2,64,512]{2,0,1:T(2,128)(2,1)S(1)}, bf16[2,64,512]{2,0,1:T(2,128)(2,1)S(1)}, u32[]{:S(2)}, u32[]{:S(2)}) collective-permute-start(bf16[2,64,512]{2,0,1:T(2,128)(2,1)S(1)} %get-tuple-element.8), channel_id=1, source_target_pairs={{2,0},{4,2},{6,4},{8,6},{10,8},{12,10},{14,12},{16,14},{18,16},{20... | collective-permute-start | bytes 393224 | tf_op jit(solution)/shard_map/ppermute | solution.py:21
Sparse Core Ops, SparseCore 0:
  8.9 10.6 all-gather.3
  65.3 11.3 all-gather.5
  78.3 10.9 all-gather.7
where the time goes:
time: 297 us; the launch traced here: 295 us
  waiting for transfers between devices  163 us (55%)
  local copies, waits for them, and re-layouts  52.4 us (18%)
  matrix products  29.4 us (10%)
  starting transfers between devices  21 us (7%)
  between operations  13.8 us (5%)
  blocking collectives  8.28 us (3%)
  other arithmetic  7.22 us (2%)
    all_to_all x1, waiting for transfers between devices, local(): lax.all_to_all(out_products, 'graph', split_axis=0, concat_axis=0, tiled=...  151 us
    scatter x2, local copies, waits for them, and re-layouts, place_slots(): jnp.zeros((devices * capacity,) + shape_rest, values.dtype).at[place]  18.7 us
    dot_general x1, matrix products, sum_into_blocks(): jnp.dot(selector, incoming.reshape(count_all, rows * cols), preferred_ele...  11.3 us
    dot_general x3, matrix products, local(): jnp.dot(hidden, weights_out[layer], preferred_element_type=jnp.float32)  10.8 us
    all_to_all x1, blocking collectives, local(): lax.all_to_all(final, 'mp', split_axis=2, concat_axis=1, tiled=True)  8.28 us
    gather x1, local copies, waits for them, and re-layouts, local(): source_data = full_blocks[source_block]  8.02 us
    ppermute x1, starting transfers between devices, padded_2(): after = lax.ppermute(leading, axis, down)  7.93 us
    dot_general x1, matrix products, masked_products(): jnp.einsum('str,src->stc', basis_rows, source_data, preferred_element_typ...  7.24 us
  transfers between devices with their start and end apart: 7, of which 4 were waited for; matrix products, arithmetic and copies ran while one was open for 22% of the time, Pallas kernels for 0%

commit v1 on v0

v1 whole, which is shorter than its diff:
```python
import functools

import jax
import jax.numpy as jnp
from jax import lax
from jax.experimental import pallas as pl
from jax.experimental.pallas import tpu as pltpu
from jax.sharding import PartitionSpec as P

MLPS = 3
BLK = 128
CHUNKS = 2
UNROLL = 4
VMEM_LIMIT = 56 * 1024 * 1024

pair_scale = 0.7071067811865476


def split_bits(devices):
    count = devices.bit_length() - 1
    near = [bit for bit in (0, 2) if bit < count]
    far = [bit for bit in range(count) if bit not in near]
    return near, far


def xor_pairs(devices, mask):
    return [(i, i ^ mask) for i in range(devices)]


def near_mask(near, k):
    return sum(((k >> i) & 1) << bit for i, bit in enumerate(near))


def full(shape):
    return pl.BlockSpec(memory_space=pltpu.VMEM)


def smem():
    return pl.BlockSpec(memory_space=pltpu.SMEM)


def pack_kernel(near, far, room, rows, blocks, owner, source, target, counts, basis, *refs):
    groups = 1 << len(near)
    packed = [refs[k * CHUNKS : (k + 1) * CHUNKS] for k in range(groups)]
    metas = refs[groups * CHUNKS : groups * (CHUNKS + 1)]
    table, fill = refs[groups * (CHUNKS + 1) :]
    slots = basis.shape[0]
    me = lax.axis_index("graph")
    core = lax.axis_index("mp")
    for k in range(groups):
        fill[k] = 0

    def clear(i, carry):
        table[i] = -1
        return carry

    lax.fori_loop(0, groups * room, clear, 0)

    def route(t, carry):
        rel = owner[t] ^ me
        k = 0
        for i, bit in enumerate(near):
            k = k + (((rel >> bit) & 1) << i)
        p = fill[k]
        fill[k] = p + 1
        table[k * room + p] = t
        return carry

    lax.fori_loop(0, slots, route, 0)

    row = lax.broadcasted_iota(jnp.int32, (rows, BLK), 0)
    for k in range(groups):

        def one(p, carry):
            t = table[k * room + p]
            there = t >= 0
            s = jnp.maximum(t, 0)
            rel = owner[s] ^ me
            b = 0
            for i, bit in enumerate(far):
                b = b + (((rel >> bit) & 1) << (len(far) - 1 - i))
            label = (b * blocks + target[s]) * blocks + source[s]
            metas[k][p] = jnp.where(there, label, 0)
            count = jnp.where(there, counts[s], 0)
            for j in range(CHUNKS):
                first = core * (rows * CHUNKS) + j * rows
                block = basis[s, pl.ds(pl.multiple_of(first, rows), rows), :]
                packed[k][j][p] = jnp.where(row + first < count, block, jnp.zeros_like(block))
            return carry

        lax.fori_loop(0, room, one, 0)


def product_kernel(groups, room, blocks, rows, *refs):
    metas = refs[:groups]
    basis = refs[groups : 2 * groups]
    mine = refs[2 * groups : 3 * groups]
    other = refs[3 * groups : 4 * groups]
    keep, send, acc = refs[4 * groups :]
    core = lax.axis_index("mp")
    width = mine[0].shape[1]
    own_cols = pl.ds(pl.multiple_of(core * width, width), width)
    other_cols = pl.ds(pl.multiple_of((1 - core) * width, width), width)
    acc[...] = jnp.zeros_like(acc)
    for k in range(groups):

        def some(step, carry):
            sums = []
            for u in range(UNROLL):
                p = step * UNROLL + u
                label = metas[k][p]
                s = label % blocks
                at = pl.ds(pl.multiple_of(s * BLK, BLK), BLK)
                left = basis[k][p]
                a = jnp.dot(left, mine[k][at, :], preferred_element_type=jnp.float32)
                b = jnp.dot(left, other[k][at, :], preferred_element_type=jnp.float32)
                sums.append((label // blocks, a, b))
            for at, a, b in sums:
                acc[at, :, own_cols] += a
                acc[at, :, other_cols] += b
            return carry

        lax.fori_loop(0, room // UNROLL, some, 0)
    half = keep.shape[0]
    for o in range(half):
        keep[o] = acc[o * blocks : (o + 1) * blocks].astype(keep.dtype)
        send[o] = acc[(half + o) * blocks : (half + o + 1) * blocks].astype(send.dtype)


def combine_kernel(chunk, rows, border, count, *refs):
    mine, other = refs[:2]
    addends = refs[2 : 2 + count]
    combined, low, high = refs[2 + count :]
    blocks = combined.shape[0]
    core = lax.axis_index("mp")
    width = mine.shape[1]
    own_cols = pl.ds(pl.multiple_of(core * width, width), width)
    other_cols = pl.ds(pl.multiple_of((1 - core) * width, width), width)
    first = core * (rows * CHUNKS) + chunk * rows
    for b in range(blocks):
        at = pl.ds(pl.multiple_of(b * BLK + first, rows), rows)
        for cols, held in ((own_cols, mine), (other_cols, other)):
            total = held[at, :].astype(jnp.float32)
            for part in addends:
                total = total + part[0, b, :, cols].astype(jnp.float32)
            combined[b, :, cols] = total.astype(combined.dtype)
    low[...] = combined[:border]
    high[...] = combined[border : 2 * border]


def mlp_kernel(chunk, rows, border, reverse, valid, combined, before, after, *refs):
    in_own, in_other, out_own, out_other, final_own, final_other, state = refs
    blocks, _, width = combined.shape
    core = lax.axis_index("mp")
    first = core * (rows * CHUNKS) + chunk * rows
    for b in range(blocks):
        within = reverse[b] % blocks
        if b < border:
            pair = before[jnp.clip(within - border, 0, border - 1)]
        elif b < 2 * border:
            pair = after[jnp.clip(within, 0, border - 1)]
        else:
            pair = combined[within]
        state[b * rows : (b + 1) * rows] = (
            combined[b].astype(jnp.float32) + pair.astype(jnp.float32)
        ) * pair_scale
    for layer in range(MLPS):
        layer_input = state[...].astype(jnp.bfloat16)
        total = state[...]
        for w_in, w_out in ((in_own, out_own), (in_other, out_other)):
            value = jnp.dot(layer_input, w_in[layer], preferred_element_type=jnp.float32)
            hidden = (value / (1.0 + jnp.exp(-value))).astype(jnp.bfloat16)
            total = total + jnp.dot(hidden, w_out[layer], preferred_element_type=jnp.float32)
        state[...] = total
    half = width // 2
    own_cols = pl.ds(pl.multiple_of(core * half, half), half)
    other_cols = pl.ds(pl.multiple_of((1 - core) * half, half), half)
    row = lax.broadcasted_iota(jnp.int32, (rows, half), 0) + first
    limit = valid[0]
    for b in range(blocks):
        keep = row + b * BLK < limit
        at = slice(b * rows, (b + 1) * rows)
        final_own[b] = jnp.where(keep, state[at, own_cols], 0.0).astype(final_own.dtype)
        final_other[b] = jnp.where(keep, state[at, other_cols], 0.0).astype(final_other.dtype)


def join_kernel(rows, *refs):
    own, came, out = refs[:CHUNKS], refs[CHUNKS : 2 * CHUNKS], refs[2 * CHUNKS]
    blocks = own[0].shape[0]
    core = lax.axis_index("mp")
    for b in range(blocks):
        for j in range(CHUNKS):
            here = b * BLK + core * (rows * CHUNKS) + j * rows
            there = b * BLK + (1 - core) * (rows * CHUNKS) + j * rows
            out[pl.ds(pl.multiple_of(here, rows), rows), :] = own[j][b]
            out[pl.ds(pl.multiple_of(there, rows), rows), :] = came[j][b]


def local(
    messages,
    basis_blocks,
    source_block,
    target_owner,
    target_block,
    row_counts,
    reverse_block,
    valid_edges,
    weight_in,
    weight_out,
):
    devices = lax.axis_size("graph")
    edge_rows, part_width = messages.shape
    width = part_width * lax.axis_size("mp")
    blocks = edge_rows // BLK
    slots = source_block.shape[0]
    capacity = max(2, (slots + devices - 1) // devices + 1)
    border = blocks // 4
    near, far = split_bits(devices)
    groups = 1 << len(near)
    owners = devices // groups
    room = min(slots, capacity * owners)
    room = -(-room // UNROLL) * UNROLL
    rows = BLK // lax.axis_size("mp") // CHUNKS
    params = pltpu.CompilerParams(vmem_limit_bytes=VMEM_LIMIT)
    bf16 = jnp.bfloat16

    def near_send(array, k):
        return lax.ppermute(array, "graph", xor_pairs(devices, near_mask(near, k)))

    def swap(array):
        return lax.ppermute(array, "mp", [(0, 1), (1, 0)])

    mine = [messages] + [near_send(messages, k) for k in range(1, groups)]

    packed_shape = jax.ShapeDtypeStruct((room, rows, BLK), bf16)
    meta_shape = jax.ShapeDtypeStruct((room,), jnp.int32)
    packed = pl.pallas_call(
        functools.partial(pack_kernel, near, far, room, rows, blocks),
        out_shape=[packed_shape] * (groups * CHUNKS) + [meta_shape] * groups,
        in_specs=[smem()] * 4 + [full(None)],
        out_specs=[full(None)] * (groups * CHUNKS) + [smem()] * groups,
        scratch_shapes=[pltpu.SMEM((groups * room,), jnp.int32), pltpu.SMEM((groups,), jnp.int32)],
        compiler_params=params,
        name="pack",
    )(target_owner[:, 0], source_block, target_block, row_counts, basis_blocks)
    sent_basis = [packed[k * CHUNKS : (k + 1) * CHUNKS] for k in range(groups)]
    sent_meta = packed[groups * CHUNKS :]
    metas = [sent_meta[0]] + [near_send(sent_meta[k], k) for k in range(1, groups)]
    basis = [
        [sent_basis[0][j]] + [near_send(sent_basis[k][j], k) for k in range(1, groups)]
        for j in range(CHUNKS)
    ]
    other = [swap(array) for array in mine]
    in_other, out_other = swap(weight_in), swap(weight_out)

    half_shape = jax.ShapeDtypeStruct((owners // 2, blocks, rows, width), bf16)
    block_shape = jax.ShapeDtypeStruct((blocks, rows, width), bf16)
    border_shape = jax.ShapeDtypeStruct((border, rows, width), bf16)
    part_shape = jax.ShapeDtypeStruct((blocks, rows, part_width), bf16)
    up = [(i, (i + 1) % devices) for i in range(devices)]
    down = [(j, i) for i, j in up]
    finals = []
    for chunk in range(CHUNKS):
        keep, send = pl.pallas_call(
            functools.partial(product_kernel, groups, room, blocks, rows),
            out_shape=[half_shape] * 2,
            in_specs=[smem()] * groups + [full(None)] * (3 * groups),
            out_specs=[full(None)] * 2,
            scratch_shapes=[pltpu.VMEM((owners * blocks, rows, width), jnp.float32)],
            compiler_params=params,
            name="product",
        )(*metas, *basis[chunk], *mine, *other)
        addends = [keep]
        size = owners // 2
        for index, bit in enumerate(far):
            addends.append(lax.ppermute(send, "graph", xor_pairs(devices, 1 << bit)))
            if index + 1 < len(far):
                size = size // 2
                total = sum(part[size : 2 * size].astype(jnp.float32) for part in addends)
                send = total.astype(bf16)
        first_owner = pl.BlockSpec((1, blocks, rows, width), lambda i: (0, 0, 0, 0))

        def whole(*shape):
            return pl.BlockSpec(shape, lambda i: (0,) * len(shape))

        combined, low, high = pl.pallas_call(
            functools.partial(combine_kernel, chunk, rows, border, len(addends)),
            grid=(1,),
            out_shape=[block_shape, border_shape, border_shape],
            in_specs=[whole(edge_rows, part_width)] * 2 + [first_owner] * len(addends),
            out_specs=[whole(blocks, rows, width)] + [whole(border, rows, width)] * 2,
            compiler_params=params,
            name="combine",
        )(mine[0], other[0], *addends)
        before = lax.ppermute(high, "graph", up)
        after = lax.ppermute(low, "graph", down)
        own, theirs = pl.pallas_call(
            functools.partial(mlp_kernel, chunk, rows, border),
            out_shape=[part_shape] * 2,
            in_specs=[smem()] * 2 + [full(None)] * 7,
            out_specs=[full(None)] * 2,
            scratch_shapes=[pltpu.VMEM((blocks * rows, width), jnp.float32)],
            compiler_params=params,
            name="mlp",
        )(
            reverse_block,
            valid_edges,
            combined,
            before,
            after,
            weight_in,
            in_other,
            weight_out,
            out_other,
        )
        finals.append((own, swap(theirs)))

    return pl.pallas_call(
        functools.partial(join_kernel, rows),
        out_shape=jax.ShapeDtypeStruct(messages.shape, bf16),
        in_specs=[full(None)] * (2 * CHUNKS),
        out_specs=full(None),
        compiler_params=params,
        name="join",
    )(*[own for own, _ in finals], *[came for _, came in finals])


def solution(mesh):
    in_specs = (
        P("graph", "mp"),
        P("graph", None, None),
        P("graph"),
        P("graph", None),
        P("graph"),
        P("graph"),
        P("graph"),
        P("graph"),
        P(None, None, "mp"),
        P(None, "mp", None),
    )
    out_specs = P("graph", "mp")
    return jax.shard_map(local, mesh=mesh, in_specs=in_specs, out_specs=out_specs, check_vma=False)
```

time: 297 us -> 146 us (0.49)
  the two profiles are of different devices: /device:TPU:25 before, /device:TPU:0 now
where the time goes in v1:
time: 146 us
  waiting for transfers between devices  56.5 us (39%)
  Pallas kernels  41.9 us (29%)
  starting transfers between devices  39.7 us (27%)
  local copies, waits for them, and re-layouts  5.54 us (4%)
    ppermute x12, waiting for transfers between devices, near_send(): return lax.ppermute(array, 'graph', xor_pairs(devices, near_mask(near, k)))  40.5 us
    pallas_call x2, Pallas kernels, local(): pl.pallas_call(functools.partial(product_kernel, groups, room, blocks, ro...  19.4 us
    ppermute x12, starting transfers between devices, near_send(): return lax.ppermute(array, 'graph', xor_pairs(devices, near_mask(near, k)))  19 us
    ppermute x4, waiting for transfers between devices, local(): addends.append(lax.ppermute(send, 'graph', xor_pairs(devices, 1 << bit)))  14.8 us
    ppermute x2, starting transfers between devices, local(): after = lax.ppermute(low, 'graph', down)  9.63 us
    pallas_call x2, Pallas kernels, local(): pl.pallas_call(functools.partial(mlp_kernel, chunk, rows, border), out_sh...  8.68 us
    ppermute x4, starting transfers between devices, local(): addends.append(lax.ppermute(send, 'graph', xor_pairs(devices, 1 << bit)))  7.53 us
    pallas_call x1, Pallas kernels, local(): pl.pallas_call(functools.partial(pack_kernel, near, far, room, rows, bloc...  7.42 us
  transfers between devices with their start and end apart: 28, of which 11 were waited for; matrix products, arithmetic and copies ran while one was open for 1% of the time, Pallas kernels for 21%

profile of v1, /device:TPU:0, one launch (start us, length us, event | category | flops | bytes accessed | tf_op | source)
XLA Modules:
  0.0 146.0 jit_solution(387637007956639728)
XLA Ops:
  0.0 2.9 %collective-permute-start.7 = (bf16[1024,256]{1,0:T(8,128)(2,1)}, bf16[1024,256]{1,0:T(8,128)(2,1)S(1)}, u32[]{:S(2)}, u32[]{:S(2)}) collective-permute-start(bf16[1024,256]{1,0:T(8,128)(2,1)} %refs_0_.6), channel_id=1, source_target_pairs={{0,2},{2,0},{4,6},{6,4},{8,10},{10,8},{12,14},{14,12},{16,18},{18,... | collective-permute-start | bytes 1572872 | tf_op jit(solution)/shard_map/ppermute | solution.py:228
  2.9 1.6 %collective-permute-start.8 = (bf16[1024,256]{1,0:T(8,128)(2,1)}, bf16[1024,256]{1,0:T(8,128)(2,1)S(1)}, u32[]{:S(2)}, u32[]{:S(2)}) collective-permute-start(bf16[1024,256]{1,0:T(8,128)(2,1)} %refs_0_.6), channel_id=1, source_target_pairs={{0,8},{2,10},{4,12},{6,14},{8,0},{10,2},{12,4},{14,6},{16,24},{18,... | collective-permute-start | bytes 1572872 | tf_op jit(solution)/shard_map/ppermute | solution.py:228
  4.5 7.4 %pack.1 = (bf16[28,32,128]{2,1,0:T(8,128)(2,1)}, bf16[28,32,128]{2,1,0:T(8,128)(2,1)}, bf16[28,32,128]{2,1,0:T(8,128)(2,1)}, bf16[28,32,128]{2,1,0:T(8,128)(2,1)...) custom-call(s32[96]{0:T(128)} %bitcast.1, ...), custom_call_target="tpu_custom_call" | custom-call | tf_op jit(solution)/shard_map/pack/pallas_call | solution.py:237
  12.0 2.0 %collective-permute-start.19 = (bf16[28,32,128]{2,1,0:T(8,128)(2,1)}, bf16[28,32,128]{2,1,0:T(8,128)(2,1)S(1)}, u32[]{:S(2)}, u32[]{:S(2)}) collective-permute-start(bf16[28,32,128]{2,1,0:T(8,128)(2,1)} %get-tuple-element.46), channel_id=1, source_target_pairs={{0,2},{2,0},{4,6},{6,4},{8,10},{10,8},{12,14},{14,12},{16,18},{18,... | collective-permute-start | bytes 688136 | tf_op jit(solution)/shard_map/ppermute | solution.py:228
  14.1 17.3 %collective-permute-done.1.refs_1_ = s32[28]{0:T(128)S(1)} collective-permute-done((s32[28]{0:T(128)}, s32[28]{0:T(128)S(1)}, u32[]{:S(2)}, u32[]{:S(2)}) %collective-permute-start.1) | collective-permute-done | bytes 144 | tf_op jit(solution)/shard_map/ppermute | solution.py:228
  31.4 1.8 %collective-permute-start.2 = (s32[28]{0:T(128)}, s32[28]{0:T(128)S(1)}, u32[]{:S(2)}, u32[]{:S(2)}) collective-permute-start(s32[28]{0:T(128)} %get-tuple-element.33), channel_id=1, source_target_pairs={{0,8},{2,10},{4,12},{6,14},{8,0},{10,2},{12,4},{14,6},{16,24},{18,... | collective-permute-start | bytes 344 | tf_op jit(solution)/shard_map/ppermute | solution.py:228
  33.1 2.0 %collective-permute-done.2.refs_2_ = s32[28]{0:T(128)S(1)} collective-permute-done((s32[28]{0:T(128)}, s32[28]{0:T(128)S(1)}, u32[]{:S(2)}, u32[]{:S(2)}) %collective-permute-start.2) | collective-permute-done | bytes 144 | tf_op jit(solution)/shard_map/ppermute | solution.py:228
  35.1 2.7 %collective-permute-start.3 = (s32[28]{0:T(128)}, s32[28]{0:T(128)S(1)}, u32[]{:S(2)}, u32[]{:S(2)}) collective-permute-start(s32[28]{0:T(128)} %get-tuple-element.34), channel_id=1, source_target_pairs={{0,10},{2,8},{4,14},{6,12},{8,2},{10,0},{12,6},{14,4},{16,26},{18,... | collective-permute-start | bytes 344 | tf_op jit(solution)/shard_map/ppermute | solution.py:228
  37.8 1.8 %collective-permute-done.3.refs_3_ = s32[28]{0:T(128)S(1)} collective-permute-done((s32[28]{0:T(128)}, s32[28]{0:T(128)S(1)}, u32[]{:S(2)}, u32[]{:S(2)}) %collective-permute-start.3) | collective-permute-done | bytes 144 | tf_op jit(solution)/shard_map/ppermute | solution.py:228
  40.7 1.8 %collective-permute-start.20 = (bf16[28,32,128]{2,1,0:T(8,128)(2,1)}, bf16[28,32,128]{2,1,0:T(8,128)(2,1)S(1)}, u32[]{:S(2)}, u32[]{:S(2)}) collective-permute-start(bf16[28,32,128]{2,1,0:T(8,128)(2,1)} %get-tuple-element.47), channel_id=1, source_target_pairs={{0,8},{2,10},{4,12},{6,14},{8,0},{10,2},{12,4},{14,6},{16,24},{18,... | collective-permute-start | bytes 688136 | tf_op jit(solution)/shard_map/ppermute | solution.py:228
  42.4 6.1 %collective-permute-done.20.refs_6_ = bf16[28,32,128]{2,1,0:T(8,128)(2,1)S(1)} collective-permute-done((bf16[28,32,128]{2,1,0:T(8,128)(2,1)}, bf16[28,32,128]{2,1,0:T(8,128)(2,1)S(1)}, u32[]{:S(2)}, u32[]{:S(2)}) %collective-permute-start.20) | collective-permute-done | bytes 229408 | tf_op jit(solution)/shard_map/ppermute | solution.py:228
  48.5 2.7 %collective-permute-start.21 = (bf16[28,32,128]{2,1,0:T(8,128)(2,1)}, bf16[28,32,128]{2,1,0:T(8,128)(2,1)S(1)}, u32[]{:S(2)}, u32[]{:S(2)}) collective-permute-start(bf16[28,32,128]{2,1,0:T(8,128)(2,1)} %get-tuple-element.48), channel_id=1, source_target_pairs={{0,10},{2,8},{4,14},{6,12},{8,2},{10,0},{12,6},{14,4},{16,26},{18,... | collective-permute-start | bytes 688136 | tf_op jit(solution)/shard_map/ppermute | solution.py:228
  51.2 5.2 %collective-permute-done.21.refs_7_ = bf16[28,32,128]{2,1,0:T(8,128)(2,1)S(1)} collective-permute-done((bf16[28,32,128]{2,1,0:T(8,128)(2,1)}, bf16[28,32,128]{2,1,0:T(8,128)(2,1)S(1)}, u32[]{:S(2)}, u32[]{:S(2)}) %collective-permute-start.21) | collective-permute-done | bytes 229408 | tf_op jit(solution)/shard_map/ppermute | solution.py:228
  57.8 9.7 %product.3 = (bf16[2,8,32,512]{3,2,1,0:T(8,128)(2,1)}, bf16[2,8,32,512]{3,2,1,0:T(8,128)(2,1)}) custom-call(s32[28]{0:T(128)} %get-tuple-element.31.refs_0_, s32[28]{0:T(128)} %copy-done.29, s32[28]{0:T(128)} %copy-done.30, s32[28]{0:T(128)} %copy-done.31, bf16[28,32,128]{2,1,0:T(8,128)(2,1)} %get-tuple-element.45.refs_4_, bf16[28,32,128]{2,1,0:T(8,128)(2,1)} %copy-done.17, ...), custom_call_target="tpu_custom_call" | custom-call | tf_op jit(solution)/shard_map/product/pallas_call | solution.py:264
  67.5 1.7 %collective-permute-start.22 = (bf16[2,8,32,512]{3,2,1,0:T(8,128)(2,1)}, bf16[2,8,32,512]{3,2,1,0:T(8,128)(2,1)S(1)}, u32[]{:S(2)}, u32[]{:S(2)}) collective-permute-start(bf16[2,8,32,512]{3,2,1,0:T(8,128)(2,1)} %get-tuple-element.50), channel_id=1, source_target_pairs={{0,4},{2,6},{4,0},{6,2},{8,12},{10,14},{12,8},{14,10},{16,20},{18,... | collective-permute-start | bytes 1572872 | tf_op jit(solution)/shard_map/ppermute | solution.py:276
  69.2 1.5 %collective-permute-start.4 = (bf16[28,32,128]{2,1,0:T(8,128)(2,1)S(1)}, bf16[28,32,128]{2,1,0:T(8,128)(2,1)S(1)}, u32[]{:S(2)}, u32[]{:S(2)}) collective-permute-start(bf16[28,32,128]{2,1,0:T(8,128)(2,1)S(1)} %copy-done.34), channel_id=1, source_target_pairs={{0,2},{2,0},{4,6},{6,4},{8,10},{10,8},{12,14},{14,12},{16,18},{18,... | collective-permute-start | bytes 688136 | tf_op jit(solution)/shard_map/ppermute | solution.py:228
  70.7 1.6 %collective-permute-start.5 = (bf16[28,32,128]{2,1,0:T(8,128)(2,1)S(1)}, bf16[28,32,128]{2,1,0:T(8,128)(2,1)S(1)}, u32[]{:S(2)}, u32[]{:S(2)}) collective-permute-start(bf16[28,32,128]{2,1,0:T(8,128)(2,1)S(1)} %copy-done.33), channel_id=1, source_target_pairs={{0,8},{2,10},{4,12},{6,14},{8,0},{10,2},{12,4},{14,6},{16,24},{18,... | collective-permute-start | bytes 688136 | tf_op jit(solution)/shard_map/ppermute | solution.py:228
  72.7 5.0 %collective-permute-done.4.refs_5_ = bf16[28,32,128]{2,1,0:T(8,128)(2,1)S(1)} collective-permute-done((bf16[28,32,128]{2,1,0:T(8,128)(2,1)S(1)}, bf16[28,32,128]{2,1,0:T(8,128)(2,1)S(1)}, u32[]{:S(2)}, u32[]{:S(2)}) %collective-permute-start.4) | collective-permute-done | bytes 229408 | tf_op jit(solution)/shard_map/ppermute | solution.py:228
  78.4 2.4 %collective-permute-done.6.refs_7_ = bf16[28,32,128]{2,1,0:T(8,128)(2,1)S(1)} collective-permute-done((bf16[28,32,128]{2,1,0:T(8,128)(2,1)S(1)}, bf16[28,32,128]{2,1,0:T(8,128)(2,1)S(1)}, u32[]{:S(2)}, u32[]{:S(2)}) %collective-permute-start.6) | collective-permute-done | bytes 229408 | tf_op jit(solution)/shard_map/ppermute | solution.py:228
  81.6 9.7 %product.2 = (bf16[2,8,32,512]{3,2,1,0:T(8,128)(2,1)}, bf16[2,8,32,512]{3,2,1,0:T(8,128)(2,1)}) custom-call(s32[28]{0:T(128)} %get-tuple-element.31.refs_0_, s32[28]{0:T(128)} %copy-done.29, s32[28]{0:T(128)} %copy-done.30, s32[28]{0:T(128)} %copy-done.31, bf16[28,32,128]{2,1,0:T(8,128)(2,1)} %get-tuple-element.35.refs_4_, bf16[28,32,128]{2,1,0:T(8,128)(2,1)} %copy-done.18, ...), custom_call_target="tpu_custom_call" | custom-call | tf_op jit(solution)/shard_map/product/pallas_call | solution.py:264
  92.3 2.8 %collective-permute-start.23 = (bf16[1,8,32,512]{3,2,1,0:T(8,128)(2,1)S(1)}, bf16[1,8,32,512]{3,2,1,0:T(8,128)(2,1)S(1)}, u32[]{:S(2)}, u32[]{:S(2)}) collective-permute-start(bf16[1,8,32,512]{3,2,1,0:T(8,128)(2,1)S(1)} %add_convert_fusion), channel_id=1, source_target_pairs={{0,16},{2,18},{4,20},{6,22},{8,24},{10,26},{12,28},{14,30},{16,0},... | collective-permute-start | bytes 786440 | tf_op jit(solution)/shard_map/ppermute | solution.py:276
  95.0 6.8 %collective-permute-done.13.refs_3_ = bf16[2,8,32,512]{3,2,1,0:T(8,128)(2,1)S(1)} collective-permute-done((bf16[2,8,32,512]{3,2,1,0:T(8,128)(2,1)}, bf16[2,8,32,512]{3,2,1,0:T(8,128)(2,1)S(1)}, u32[]{:S(2)}, u32[]{:S(2)}) %collective-permute-start.13) | collective-permute-done | bytes 524320 | tf_op jit(solution)/shard_map/ppermute | solution.py:276
  103.0 2.6 %collective-permute-start.14 = (bf16[1,8,32,512]{3,2,1,0:T(8,128)(2,1)S(1)}, bf16[1,8,32,512]{3,2,1,0:T(8,128)(2,1)S(1)}, u32[]{:S(2)}, u32[]{:S(2)}) collective-permute-start(bf16[1,8,32,512]{3,2,1,0:T(8,128)(2,1)S(1)} %add_convert_fusion.1), channel_id=1, source_target_pairs={{0,16},{2,18},{4,20},{6,22},{8,24},{10,26},{12,28},{14,30},{16,0},... | collective-permute-start | bytes 786440 | tf_op jit(solution)/shard_map/ppermute | solution.py:276
  105.7 7.9 %collective-permute-done.23.refs_4_ = bf16[1,8,32,512]{3,2,1,0:T(8,128)(2,1)S(1)} collective-permute-done((bf16[1,8,32,512]{3,2,1,0:T(8,128)(2,1)S(1)}, bf16[1,8,32,512]{3,2,1,0:T(8,128)(2,1)S(1)}, u32[]{:S(2)}, u32[]{:S(2)}) %collective-permute-start.23) | collective-permute-done | bytes 262176 | tf_op jit(solution)/shard_map/ppermute | solution.py:276
  114.3 2.3 %combine.3 = (bf16[8,32,512]{2,1,0:T(8,128)(2,1)}, bf16[2,32,512]{2,1,0:T(8,128)(2,1)}, bf16[2,32,512]{2,1,0:T(8,128)(2,1)}) custom-call(bf16[1024,256]{1,0:T(8,128)(2,1)} %refs_0_.6, bf16[1024,256]{1,0:T(8,128)(2,1)} %copy-done.1, bf16[2,8,32,512]{3,2,1,0:T(8,128)(2,1)} %get-tuple-element.49.refs_2_, bf16[2,8,32,512]{3,2,1,0:T(8,128)(2,1)} %copy-done.13, ...), custom_call_target="tpu_custom_call" | custom-call | tf_op jit(solution)/shard_map/combine/pallas_call | solution.py:286
  116.6 1.6 %collective-permute-start.24 = (bf16[2,32,512]{2,1,0:T(8,128)(2,1)}, bf16[2,32,512]{2,1,0:T(8,128)(2,1)S(1)}, u32[]{:S(2)}, u32[]{:S(2)}) collective-permute-start(bf16[2,32,512]{2,1,0:T(8,128)(2,1)} %get-tuple-element.52), channel_id=1, source_target_pairs={{0,2},{2,4},{4,6},{6,8},{8,10},{10,12},{12,14},{14,16},{16,18},{18... | collective-permute-start | bytes 196616 | tf_op jit(solution)/shard_map/ppermute | solution.py:295
  118.2 4.0 %collective-permute-start.25 = (bf16[2,32,512]{2,1,0:T(8,128)(2,1)}, bf16[2,32,512]{2,1,0:T(8,128)(2,1)S(1)}, u32[]{:S(2)}, u32[]{:S(2)}) collective-permute-start(bf16[2,32,512]{2,1,0:T(8,128)(2,1)} %get-tuple-element.53), channel_id=1, source_target_pairs={{2,0},{4,2},{6,4},{8,6},{10,8},{12,10},{14,12},{16,14},{18,16},{20... | collective-permute-start | bytes 196616 | tf_op jit(solution)/shard_map/ppermute | solution.py:296
  122.9 2.3 %combine.2 = (bf16[8,32,512]{2,1,0:T(8,128)(2,1)}, bf16[2,32,512]{2,1,0:T(8,128)(2,1)}, bf16[2,32,512]{2,1,0:T(8,128)(2,1)}) custom-call(bf16[1024,256]{1,0:T(8,128)(2,1)} %refs_0_.6, bf16[1024,256]{1,0:T(8,128)(2,1)} %copy-done.1, bf16[2,8,32,512]{3,2,1,0:T(8,128)(2,1)} %get-tuple-element.39.refs_2_, bf16[2,8,32,512]{3,2,1,0:T(8,128)(2,1)} %copy-done.14, ...), custom_call_target="tpu_custom_call" | custom-call | tf_op jit(solution)/shard_map/combine/pallas_call | solution.py:286
  125.2 5.6 %collective-permute-start.16 = (bf16[2,32,512]{2,1,0:T(8,128)(2,1)}, bf16[2,32,512]{2,1,0:T(8,128)(2,1)S(1)}, u32[]{:S(2)}, u32[]{:S(2)}) collective-permute-start(bf16[2,32,512]{2,1,0:T(8,128)(2,1)} %get-tuple-element.43), channel_id=1, source_target_pairs={{2,0},{4,2},{6,4},{8,6},{10,8},{12,10},{14,12},{16,14},{18,16},{20... | collective-permute-start | bytes 196616 | tf_op jit(solution)/shard_map/ppermute | solution.py:296
  132.4 4.3 %mlp.3 = (bf16[8,32,256]{2,1,0:T(8,128)(2,1)}, bf16[8,32,256]{2,1,0:T(8,128)(2,1)}) custom-call(s32[8]{0:T(128)} %reverse.3, s32[1]{0:T(128)S(6)} %copy.11.valid, bf16[8,32,512]{2,1,0:T(8,128)(2,1)} %get-tuple-element.51.combined, bf16[2,32,512]{2,1,0:T(8,128)(2,1)} %copy-done.26, bf16[2,32,512]{2,1,0:T(8,128)(2,1)} %copy-done.27, ...), custom_call_target="tpu_custom_call" | custom-call | tf_op jit(solution)/shard_map/mlp/pallas_call | solution.py:297
  137.4 4.3 %mlp.2 = (bf16[8,32,256]{2,1,0:T(8,128)(2,1)}, bf16[8,32,256]{2,1,0:T(8,128)(2,1)}) custom-call(s32[8]{0:T(128)} %reverse.3, s32[1]{0:T(128)S(6)} %copy.11.valid, bf16[8,32,512]{2,1,0:T(8,128)(2,1)} %get-tuple-element.41.combined, bf16[2,32,512]{2,1,0:T(8,128)(2,1)} %copy-done.25, bf16[2,32,512]{2,1,0:T(8,128)(2,1)} %copy-done.28, ...), custom_call_target="tpu_custom_call" | custom-call | tf_op jit(solution)/shard_map/mlp/pallas_call | solution.py:297
  144.0 1.9 %join.1 = bf16[1024,256]{1,0:T(8,128)(2,1)} custom-call(bf16[8,32,256]{2,1,0:T(8,128)(2,1)} %get-tuple-element.44.refs_0_, bf16[8,32,256]{2,1,0:T(8,128)(2,1)} %get-tuple-element.54.refs_1_, bf16[8,32,256]{2,1,0:T(8,128)(2,1)} %copy-done.24, bf16[8,32,256]{2,1,0:T(8,128)(2,1)} %copy-done.23), custom_call_target="tpu_custom_call" | custom-call | tf_op jit(solution)/shard_map/join/pallas_call | solution.py:318
  (104 shorter events, 11.7 us)
Async XLA Ops:
  0.0 39.6 %copy-start = (bf16[1024,256]{1,0:T(8,128)(2,1)S(1)}, bf16[1024,256]{1,0:T(8,128)(2,1)}, u32[]{:S(2)}) copy-start(bf16[1024,256]{1,0:T(8,128)(2,1)} %refs_0_.6) | copy-start | bytes 1572868
  0.0 39.6 %collective-permute-start.7 = (bf16[1024,256]{1,0:T(8,128)(2,1)}, bf16[1024,256]{1,0:T(8,128)(2,1)S(1)}, u32[]{:S(2)}, u32[]{:S(2)}) collective-permute-start(bf16[1024,256]{1,0:T(8,128)(2,1)} %refs_0_.6), channel_id=1, source_target_pairs={{0,2},{2,0},{4,6},{6,4},{8,10},{10,8},{12,14},{14,12},{16,18},{18,... | collective-permute-start | bytes 1572872 | tf_op jit(solution)/shard_map/ppermute | solution.py:228
  2.9 37.2 %collective-permute-start.8 = (bf16[1024,256]{1,0:T(8,128)(2,1)}, bf16[1024,256]{1,0:T(8,128)(2,1)S(1)}, u32[]{:S(2)}, u32[]{:S(2)}) collective-permute-start(bf16[1024,256]{1,0:T(8,128)(2,1)} %refs_0_.6), channel_id=1, source_target_pairs={{0,8},{2,10},{4,12},{6,14},{8,0},{10,2},{12,4},{14,6},{16,24},{18,... | collective-permute-start | bytes 1572872 | tf_op jit(solution)/shard_map/ppermute | solution.py:228
  4.5 35.7 %collective-permute-start.9 = (bf16[1024,256]{1,0:T(8,128)(2,1)}, bf16[1024,256]{1,0:T(8,128)(2,1)S(1)}, u32[]{:S(2)}, u32[]{:S(2)}) collective-permute-start(bf16[1024,256]{1,0:T(8,128)(2,1)} %refs_0_.6), channel_id=1, source_target_pairs={{0,10},{2,8},{4,14},{6,12},{8,2},{10,0},{12,6},{14,4},{16,26},{18,... | collective-permute-start | bytes 1572872 | tf_op jit(solution)/shard_map/ppermute | solution.py:228
  11.9 57.3 %copy-start.34 = (bf16[28,32,128]{2,1,0:T(8,128)(2,1)S(1)}, bf16[28,32,128]{2,1,0:T(8,128)(2,1)}, u32[]{:S(2)}) copy-start(bf16[28,32,128]{2,1,0:T(8,128)(2,1)} %get-tuple-element.36) | copy-start | bytes 688132
  12.0 58.7 %copy-start.33 = (bf16[28,32,128]{2,1,0:T(8,128)(2,1)S(1)}, bf16[28,32,128]{2,1,0:T(8,128)(2,1)}, u32[]{:S(2)}) copy-start(bf16[28,32,128]{2,1,0:T(8,128)(2,1)} %get-tuple-element.37) | copy-start | bytes 688132
  12.0 60.3 %copy-start.32 = (bf16[28,32,128]{2,1,0:T(8,128)(2,1)S(1)}, bf16[28,32,128]{2,1,0:T(8,128)(2,1)}, u32[]{:S(2)}) copy-start(bf16[28,32,128]{2,1,0:T(8,128)(2,1)} %get-tuple-element.38) | copy-start | bytes 688132
  12.0 28.7 %collective-permute-start.19 = (bf16[28,32,128]{2,1,0:T(8,128)(2,1)}, bf16[28,32,128]{2,1,0:T(8,128)(2,1)S(1)}, u32[]{:S(2)}, u32[]{:S(2)}) collective-permute-start(bf16[28,32,128]{2,1,0:T(8,128)(2,1)} %get-tuple-element.46), channel_id=1, source_target_pairs={{0,2},{2,0},{4,6},{6,4},{8,10},{10,8},{12,14},{14,12},{16,18},{18,... | collective-permute-start | bytes 688136 | tf_op jit(solution)/shard_map/ppermute | solution.py:228
  14.0 17.4 %collective-permute-start.1 = (s32[28]{0:T(128)}, s32[28]{0:T(128)S(1)}, u32[]{:S(2)}, u32[]{:S(2)}) collective-permute-start(s32[28]{0:T(128)} %get-tuple-element.32), channel_id=1, source_target_pairs={{0,2},{2,0},{4,6},{6,4},{8,10},{10,8},{12,14},{14,12},{16,18},{18,... | collective-permute-start | bytes 344 | tf_op jit(solution)/shard_map/ppermute | solution.py:228
  31.4 3.8 %collective-permute-start.2 = (s32[28]{0:T(128)}, s32[28]{0:T(128)S(1)}, u32[]{:S(2)}, u32[]{:S(2)}) collective-permute-start(s32[28]{0:T(128)} %get-tuple-element.33), channel_id=1, source_target_pairs={{0,8},{2,10},{4,12},{6,14},{8,0},{10,2},{12,4},{14,6},{16,24},{18,... | collective-permute-start | bytes 344 | tf_op jit(solution)/shard_map/ppermute | solution.py:228
  35.1 4.5 %collective-permute-start.3 = (s32[28]{0:T(128)}, s32[28]{0:T(128)S(1)}, u32[]{:S(2)}, u32[]{:S(2)}) collective-permute-start(s32[28]{0:T(128)} %get-tuple-element.34), channel_id=1, source_target_pairs={{0,10},{2,8},{4,14},{6,12},{8,2},{10,0},{12,6},{14,4},{16,26},{18,... | collective-permute-start | bytes 344 | tf_op jit(solution)/shard_map/ppermute | solution.py:228
  39.6 16.8 %collective-permute-start = (bf16[1024,256]{1,0:T(8,128)(2,1)S(1)}, bf16[1024,256]{1,0:T(8,128)(2,1)S(1)}, u32[]{:S(2)}, u32[]{:S(2)}) collective-permute-start(bf16[1024,256]{1,0:T(8,128)(2,1)S(1)} %copy-done), channel_id=1, source_target_pairs={{0,1},{1,0},{2,3},{3,2},{4,5},{5,4},{6,7},{7,6},{8,9},{9,8},{10,11... | collective-permute-start | bytes 1572872 | tf_op jit(solution)/shard_map/ppermute | solution.py:231
  39.6 16.7 %collective-permute-start.10 = (bf16[1024,256]{1,0:T(8,128)(2,1)S(1)}, bf16[1024,256]{1,0:T(8,128)(2,1)S(1)}, u32[]{:S(2)}, u32[]{:S(2)}) collective-permute-start(bf16[1024,256]{1,0:T(8,128)(2,1)S(1)} %collective-permute-done.7.refs_9_), channel_id=1, source_target_pairs={{0,1},{1,0},{2,3},{3,2},{4,5},{5,4},{6,7},{7,6},{8,9},{9,8},{10,11... | collective-permute-start | bytes 1572872 | tf_op jit(solution)/shard_map/ppermute | solution.py:231
  40.1 16.3 %collective-permute-start.11 = (bf16[1024,256]{1,0:T(8,128)(2,1)S(1)}, bf16[1024,256]{1,0:T(8,128)(2,1)S(1)}, u32[]{:S(2)}, u32[]{:S(2)}) collective-permute-start(bf16[1024,256]{1,0:T(8,128)(2,1)S(1)} %collective-permute-done.8.refs_10_), channel_id=1, source_target_pairs={{0,1},{1,0},{2,3},{3,2},{4,5},{5,4},{6,7},{7,6},{8,9},{9,8},{10,11... | collective-permute-start | bytes 1572872 | tf_op jit(solution)/shard_map/ppermute | solution.py:231
  40.2 16.2 %collective-permute-start.12 = (bf16[1024,256]{1,0:T(8,128)(2,1)S(1)}, bf16[1024,256]{1,0:T(8,128)(2,1)S(1)}, u32[]{:S(2)}, u32[]{:S(2)}) collective-permute-start(bf16[1024,256]{1,0:T(8,128)(2,1)S(1)} %collective-permute-done.9.refs_11_), channel_id=1, source_target_pairs={{0,1},{1,0},{2,3},{3,2},{4,5},{5,4},{6,7},{7,6},{8,9},{9,8},{10,11... | collective-permute-start | bytes 1572872 | tf_op jit(solution)/shard_map/ppermute | solution.py:231
  40.7 7.8 %collective-permute-start.20 = (bf16[28,32,128]{2,1,0:T(8,128)(2,1)}, bf16[28,32,128]{2,1,0:T(8,128)(2,1)S(1)}, u32[]{:S(2)}, u32[]{:S(2)}) collective-permute-start(bf16[28,32,128]{2,1,0:T(8,128)(2,1)} %get-tuple-element.47), channel_id=1, source_target_pairs={{0,8},{2,10},{4,12},{6,14},{8,0},{10,2},{12,4},{14,6},{16,24},{18,... | collective-permute-start | bytes 688136 | tf_op jit(solution)/shard_map/ppermute | solution.py:228
  48.5 7.9 %collective-permute-start.21 = (bf16[28,32,128]{2,1,0:T(8,128)(2,1)}, bf16[28,32,128]{2,1,0:T(8,128)(2,1)S(1)}, u32[]{:S(2)}, u32[]{:S(2)}) collective-permute-start(bf16[28,32,128]{2,1,0:T(8,128)(2,1)} %get-tuple-element.48), channel_id=1, source_target_pairs={{0,10},{2,8},{4,14},{6,12},{8,2},{10,0},{12,6},{14,4},{16,26},{18,... | collective-permute-start | bytes 688136 | tf_op jit(solution)/shard_map/ppermute | solution.py:228
  67.5 24.7 %collective-permute-start.22 = (bf16[2,8,32,512]{3,2,1,0:T(8,128)(2,1)}, bf16[2,8,32,512]{3,2,1,0:T(8,128)(2,1)S(1)}, u32[]{:S(2)}, u32[]{:S(2)}) collective-permute-start(bf16[2,8,32,512]{3,2,1,0:T(8,128)(2,1)} %get-tuple-element.50), channel_id=1, source_target_pairs={{0,4},{2,6},{4,0},{6,2},{8,12},{10,14},{12,8},{14,10},{16,20},{18,... | collective-permute-start | bytes 1572872 | tf_op jit(solution)/shard_map/ppermute | solution.py:276
  69.2 8.5 %collective-permute-start.4 = (bf16[28,32,128]{2,1,0:T(8,128)(2,1)S(1)}, bf16[28,32,128]{2,1,0:T(8,128)(2,1)S(1)}, u32[]{:S(2)}, u32[]{:S(2)}) collective-permute-start(bf16[28,32,128]{2,1,0:T(8,128)(2,1)S(1)} %copy-done.34), channel_id=1, source_target_pairs={{0,2},{2,0},{4,6},{6,4},{8,10},{10,8},{12,14},{14,12},{16,18},{18,... | collective-permute-start | bytes 688136 | tf_op jit(solution)/shard_map/ppermute | solution.py:228
  70.7 7.7 %collective-permute-start.5 = (bf16[28,32,128]{2,1,0:T(8,128)(2,1)S(1)}, bf16[28,32,128]{2,1,0:T(8,128)(2,1)S(1)}, u32[]{:S(2)}, u32[]{:S(2)}) collective-permute-start(bf16[28,32,128]{2,1,0:T(8,128)(2,1)S(1)} %copy-done.33), channel_id=1, source_target_pairs={{0,8},{2,10},{4,12},{6,14},{8,0},{10,2},{12,4},{14,6},{16,24},{18,... | collective-permute-start | bytes 688136 | tf_op jit(solution)/shard_map/ppermute | solution.py:228
  72.3 8.6 %collective-permute-start.6 = (bf16[28,32,128]{2,1,0:T(8,128)(2,1)S(1)}, bf16[28,32,128]{2,1,0:T(8,128)(2,1)S(1)}, u32[]{:S(2)}, u32[]{:S(2)}) collective-permute-start(bf16[28,32,128]{2,1,0:T(8,128)(2,1)S(1)} %copy-done.32), channel_id=1, source_target_pairs={{0,10},{2,8},{4,14},{6,12},{8,2},{10,0},{12,6},{14,4},{16,26},{18,... | collective-permute-start | bytes 688136 | tf_op jit(solution)/shard_map/ppermute | solution.py:228
  91.3 10.6 %collective-permute-start.13 = (bf16[2,8,32,512]{3,2,1,0:T(8,128)(2,1)}, bf16[2,8,32,512]{3,2,1,0:T(8,128)(2,1)S(1)}, u32[]{:S(2)}, u32[]{:S(2)}) collective-permute-start(bf16[2,8,32,512]{3,2,1,0:T(8,128)(2,1)} %get-tuple-element.40), channel_id=1, source_target_pairs={{0,4},{2,6},{4,0},{6,2},{8,12},{10,14},{12,8},{14,10},{16,20},{18,... | collective-permute-start | bytes 1572872 | tf_op jit(solution)/shard_map/ppermute | solution.py:276
  91.7 33.5 %collective-permute-start.17 = (bf16[3,512,256]{2,1,0:T(8,128)(2,1)S(1)}, bf16[3,512,256]{2,1,0:T(8,128)(2,1)S(1)}, u32[]{:S(2)}, u32[]{:S(2)}) collective-permute-start(bf16[3,512,256]{2,1,0:T(8,128)(2,1)S(1)} %copy-done.2), channel_id=1, source_target_pairs={{0,1},{1,0},{2,3},{3,2},{4,5},{5,4},{6,7},{7,6},{8,9},{9,8},{10,11... | collective-permute-start | bytes 2359304 | tf_op jit(solution)/shard_map/ppermute | solution.py:231
  91.7 39.8 %collective-permute-start.18 = (bf16[3,256,512]{2,1,0:T(8,128)(2,1)S(1)}, bf16[3,256,512]{2,1,0:T(8,128)(2,1)S(1)}, u32[]{:S(2)}, u32[]{:S(2)}) collective-permute-start(bf16[3,256,512]{2,1,0:T(8,128)(2,1)S(1)} %copy-done.3), channel_id=1, source_target_pairs={{0,1},{1,0},{2,3},{3,2},{4,5},{5,4},{6,7},{7,6},{8,9},{9,8},{10,11... | collective-permute-start | bytes 2359304 | tf_op jit(solution)/shard_map/ppermute | solution.py:231
  92.3 21.4 %collective-permute-start.23 = (bf16[1,8,32,512]{3,2,1,0:T(8,128)(2,1)S(1)}, bf16[1,8,32,512]{3,2,1,0:T(8,128)(2,1)S(1)}, u32[]{:S(2)}, u32[]{:S(2)}) collective-permute-start(bf16[1,8,32,512]{3,2,1,0:T(8,128)(2,1)S(1)} %add_convert_fusion), channel_id=1, source_target_pairs={{0,16},{2,18},{4,20},{6,22},{8,24},{10,26},{12,28},{14,30},{16,0},... | collective-permute-start | bytes 786440 | tf_op jit(solution)/shard_map/ppermute | solution.py:276
  103.0 19.2 %collective-permute-start.14 = (bf16[1,8,32,512]{3,2,1,0:T(8,128)(2,1)S(1)}, bf16[1,8,32,512]{3,2,1,0:T(8,128)(2,1)S(1)}, u32[]{:S(2)}, u32[]{:S(2)}) collective-permute-start(bf16[1,8,32,512]{3,2,1,0:T(8,128)(2,1)S(1)} %add_convert_fusion.1), channel_id=1, source_target_pairs={{0,16},{2,18},{4,20},{6,22},{8,24},{10,26},{12,28},{14,30},{16,0},... | collective-permute-start | bytes 786440 | tf_op jit(solution)/shard_map/ppermute | solution.py:276
  116.6 14.9 %collective-permute-start.24 = (bf16[2,32,512]{2,1,0:T(8,128)(2,1)}, bf16[2,32,512]{2,1,0:T(8,128)(2,1)S(1)}, u32[]{:S(2)}, u32[]{:S(2)}) collective-permute-start(bf16[2,32,512]{2,1,0:T(8,128)(2,1)} %get-tuple-element.52), channel_id=1, source_target_pairs={{0,2},{2,4},{4,6},{6,8},{8,10},{10,12},{12,14},{14,16},{16,18},{18... | collective-permute-start | bytes 196616 | tf_op jit(solution)/shard_map/ppermute | solution.py:295
  118.2 13.3 %collective-permute-start.25 = (bf16[2,32,512]{2,1,0:T(8,128)(2,1)}, bf16[2,32,512]{2,1,0:T(8,128)(2,1)S(1)}, u32[]{:S(2)}, u32[]{:S(2)}) collective-permute-start(bf16[2,32,512]{2,1,0:T(8,128)(2,1)} %get-tuple-element.53), channel_id=1, source_target_pairs={{2,0},{4,2},{6,4},{8,6},{10,8},{12,10},{14,12},{16,14},{18,16},{20... | collective-permute-start | bytes 196616 | tf_op jit(solution)/shard_map/ppermute | solution.py:296
  125.2 11.5 %collective-permute-start.15 = (bf16[2,32,512]{2,1,0:T(8,128)(2,1)}, bf16[2,32,512]{2,1,0:T(8,128)(2,1)S(1)}, u32[]{:S(2)}, u32[]{:S(2)}) collective-permute-start(bf16[2,32,512]{2,1,0:T(8,128)(2,1)} %get-tuple-element.42), channel_id=1, source_target_pairs={{0,2},{2,4},{4,6},{6,8},{8,10},{10,12},{12,14},{14,16},{16,18},{18... | collective-permute-start | bytes 196616 | tf_op jit(solution)/shard_map/ppermute | solution.py:295
  125.2 11.5 %collective-permute-start.16 = (bf16[2,32,512]{2,1,0:T(8,128)(2,1)}, bf16[2,32,512]{2,1,0:T(8,128)(2,1)S(1)}, u32[]{:S(2)}, u32[]{:S(2)}) collective-permute-start(bf16[2,32,512]{2,1,0:T(8,128)(2,1)} %get-tuple-element.43), channel_id=1, source_target_pairs={{2,0},{4,2},{6,4},{8,6},{10,8},{12,10},{14,12},{16,14},{18,16},{20... | collective-permute-start | bytes 196616 | tf_op jit(solution)/shard_map/ppermute | solution.py:296
  136.7 5.5 %collective-permute-start.27 = (bf16[8,32,256]{2,1,0:T(8,128)(2,1)}, bf16[8,32,256]{2,1,0:T(8,128)(2,1)S(1)}, u32[]{:S(2)}, u32[]{:S(2)}) collective-permute-start(bf16[8,32,256]{2,1,0:T(8,128)(2,1)} %get-tuple-element.56), channel_id=1, source_target_pairs={{0,1},{1,0},{2,3},{3,2},{4,5},{5,4},{6,7},{7,6},{8,9},{9,8},{10,11... | collective-permute-start | bytes 393224 | tf_op jit(solution)/shard_map/ppermute | solution.py:231
  141.7 1.7 %collective-permute-start.26 = (bf16[8,32,256]{2,1,0:T(8,128)(2,1)}, bf16[8,32,256]{2,1,0:T(8,128)(2,1)S(1)}, u32[]{:S(2)}, u32[]{:S(2)}) collective-permute-start(bf16[8,32,256]{2,1,0:T(8,128)(2,1)} %get-tuple-element.55), channel_id=1, source_target_pairs={{0,1},{1,0},{2,3},{3,2},{4,5},{5,4},{6,7},{7,6},{8,9},{9,8},{10,11... | collective-permute-start | bytes 393224 | tf_op jit(solution)/shard_map/ppermute | solution.py:231
  (31 other events, 276.4 us)

commit v2 on v1

v2 whole, which is shorter than its diff:
```python
import functools

import jax
import jax.numpy as jnp
from jax import lax
from jax.experimental import pallas as pl
from jax.experimental.pallas import tpu as pltpu
from jax.sharding import PartitionSpec as P

MLPS = 3
BLK = 128
CHUNKS = 2
UNROLL = 14
GRANT = 12 * 1024 * 1024

pair_scale = 0.7071067811865476


def split_bits(devices):
    count = devices.bit_length() - 1
    near = [bit for bit in (0, 2) if bit < count]
    far = [bit for bit in range(count) if bit not in near]
    return near, far


def xor_pairs(devices, mask):
    return [(i, i ^ mask) for i in range(devices)]


def near_mask(near, k):
    return sum(((k >> i) & 1) << bit for i, bit in enumerate(near))


def grant(extra=0):
    return pltpu.CompilerParams(vmem_limit_bytes=GRANT + extra)


def spent(microseconds):
    return pl.CostEstimate(
        flops=0, bytes_accessed=int(microseconds * 3.69e6), transcendentals=0
    )


def after_all(value, *others):
    if not others:
        return value
    return lax.optimization_barrier((value, *others))[0]


def full(shape):
    return pl.BlockSpec(memory_space=pltpu.VMEM)


def smem():
    return pl.BlockSpec(memory_space=pltpu.SMEM)


def pack_kernel(near, far, room, rows, blocks, owner, source, target, counts, basis, *refs):
    groups = 1 << len(near)
    packed = refs[:groups]
    table, fill = refs[groups:]
    slots = basis.shape[0]
    me = lax.axis_index("graph")
    core = lax.axis_index("mp")
    for k in range(groups):
        fill[k] = 0

    def clear(i, carry):
        table[i] = -1
        return carry

    lax.fori_loop(0, groups * room, clear, 0, unroll=4)

    def route(t, carry):
        rel = owner[t] ^ me
        k = 0
        for i, bit in enumerate(near):
            k = k + (((rel >> bit) & 1) << i)
        p = fill[k]
        fill[k] = p + 1
        table[k * room + p] = t
        return carry

    lax.fori_loop(0, slots, route, 0)

    share = rows * CHUNKS
    first = core * share
    row = lax.broadcasted_iota(jnp.int32, (share, BLK), 0)
    label_row = lax.broadcasted_iota(jnp.int32, (rows, BLK), 0)
    lane = lax.broadcasted_iota(jnp.int32, (rows, BLK), 1)
    for k in range(groups):

        def one(p, labels):
            t = table[k * room + p]
            there = t >= 0
            s = jnp.maximum(t, 0)
            rel = owner[s] ^ me
            b = 0
            for i, bit in enumerate(far):
                b = b + (((rel >> bit) & 1) << (len(far) - 1 - i))
            place = jnp.where(there, b * blocks + target[s], 0)
            place = jnp.where(label_row == 0, place, source[s])
            labels = jnp.where(lane == p, place, labels)
            count = jnp.where(there, counts[s], 0)
            block = basis[s, pl.ds(pl.multiple_of(first, share), share), :]
            block = jnp.where(row + first < count, block, jnp.zeros_like(block))
            packed[k][p] = block
            return labels

        labels = lax.fori_loop(0, room, one, jnp.zeros((rows, BLK), jnp.int32), unroll=2)
        labels = labels.astype(jnp.float32).astype(jnp.bfloat16)
        packed[k][room, :rows] = labels


def add_products(room, held, basis, mine, other, acc, staged, metas, sem):
    sources = len(basis)
    core = lax.axis_index("mp")
    width = mine[0].shape[1]
    own_cols = pl.ds(pl.multiple_of(core * width, width), width)
    other_cols = pl.ds(pl.multiple_of((1 - core) * width, width), width)
    for k in range(sources):
        staged[k] = basis[k][room, :16, :].astype(jnp.float32).astype(jnp.int32)
    copy = pltpu.make_async_copy(staged, metas, sem)
    copy.start()
    acc[...] = jnp.zeros_like(acc)
    copy.wait()
    for k in range(sources):

        def some(step, carry):
            sums = []
            for u in range(UNROLL):
                p = step * UNROLL + u
                s = metas[k, 1, p]
                at = pl.ds(pl.multiple_of(s * BLK, BLK), BLK)
                left = basis[k][p, held]
                a = jnp.dot(left, mine[k][at, :], preferred_element_type=jnp.float32)
                b = jnp.dot(left, other[k][at, :], preferred_element_type=jnp.float32)
                sums.append((metas[k, 0, p], a, b))
            for at, a, b in sums:
                acc[at, :, own_cols] += a
                acc[at, :, other_cols] += b
            return carry

        lax.fori_loop(0, room // UNROLL, some, 0)


def first_kernel(sources, room, *refs):
    basis, mine, other = (refs[i * sources : (i + 1) * sources] for i in range(3))
    acc, staged, metas, sem = refs[3 * sources :]
    add_products(room, slice(None), basis, mine, other, acc, staged, metas, sem)


def last_kernel(sources, room, blocks, rows, chunk, *refs):
    basis, mine, other = (refs[i * sources : (i + 1) * sources] for i in range(3))
    before = refs[3 * sources]
    keep_low, keep_high, send_low, send_high, acc, staged, metas, sem = refs[3 * sources + 1 :]
    held = slice(chunk * rows, (chunk + 1) * rows)
    add_products(room, held, basis, mine, other, acc, staged, metas, sem)
    part = keep_low.shape[0]
    for i, out in enumerate((keep_low, keep_high, send_low, send_high)):
        for o in range(part):
            at = slice((i * part + o) * blocks, (i * part + o + 1) * blocks)
            out[o] = (before[at, held] + acc[at]).astype(out.dtype)


def combine_kernel(chunk, rows, border, count, *refs):
    mine, other = refs[:2]
    addends = refs[2 : 2 + count]
    combined, even_send, odd_send = refs[2 + count :]
    blocks = combined.shape[0]
    core = lax.axis_index("mp")
    width = mine.shape[1]
    own_cols = pl.ds(pl.multiple_of(core * width, width), width)
    other_cols = pl.ds(pl.multiple_of((1 - core) * width, width), width)
    first = core * (rows * CHUNKS) + chunk * rows
    for b in range(blocks):
        at = pl.ds(pl.multiple_of(b * BLK + first, rows), rows)
        for cols, held in ((own_cols, mine), (other_cols, other)):
            total = held[at, :].astype(jnp.float32)
            for part in addends:
                total = total + part[0, b, :, cols].astype(jnp.float32)
            combined[b, :, cols] = total.astype(combined.dtype)
    odd = lax.axis_index("graph") % 2
    even_send[...] = combined[pl.ds((1 - odd) * border, border)]
    odd_send[...] = combined[pl.ds(odd * border, border)]


def mlp_kernel(chunk, rows, border, reverse, valid, combined, even_came, odd_came, *refs):
    in_own, in_other, out_own, out_other, final_own, final_other, state = refs
    blocks, _, width = combined.shape
    core = lax.axis_index("mp")
    odd = lax.axis_index("graph") % 2 == 1
    first = core * (rows * CHUNKS) + chunk * rows
    for b in range(blocks):
        within = reverse[b] % blocks
        if b >= 2 * border:
            pair = combined[within]
        else:
            w = jnp.clip(within - (border if b < border else 0), 0, border - 1)
            pair = jnp.where(odd == (b < border), even_came[w], odd_came[w])
        state[b * rows : (b + 1) * rows] = (
            combined[b].astype(jnp.float32) + pair.astype(jnp.float32)
        ) * pair_scale
    for layer in range(MLPS):
        layer_input = state[...].astype(jnp.bfloat16)
        total = state[...]
        for w_in, w_out in ((in_own, out_own), (in_other, out_other)):
            value = jnp.dot(layer_input, w_in[layer], preferred_element_type=jnp.float32)
            hidden = (value / (1.0 + jnp.exp(-value))).astype(jnp.bfloat16)
            total = total + jnp.dot(hidden, w_out[layer], preferred_element_type=jnp.float32)
        state[...] = total
    half = width // 2
    own_cols = pl.ds(pl.multiple_of(core * half, half), half)
    other_cols = pl.ds(pl.multiple_of((1 - core) * half, half), half)
    row = lax.broadcasted_iota(jnp.int32, (rows, half), 0) + first
    limit = valid[0]
    for b in range(blocks):
        keep = row + b * BLK < limit
        at = slice(b * rows, (b + 1) * rows)
        final_own[b] = jnp.where(keep, state[at, own_cols], 0.0).astype(final_own.dtype)
        final_other[b] = jnp.where(keep, state[at, other_cols], 0.0).astype(final_other.dtype)


def join_kernel(rows, *refs):
    own, came, out = refs[:CHUNKS], refs[CHUNKS : 2 * CHUNKS], refs[2 * CHUNKS]
    core = lax.axis_index("mp")
    for chunk in range(CHUNKS):
        for b in range(own[chunk].shape[0]):
            base = b * BLK + chunk * rows
            here = base + core * (rows * CHUNKS)
            there = base + (1 - core) * (rows * CHUNKS)
            out[pl.ds(pl.multiple_of(here, rows), rows), :] = own[chunk][b]
            out[pl.ds(pl.multiple_of(there, rows), rows), :] = came[chunk][b]


def local(
    messages,
    basis_blocks,
    source_block,
    target_owner,
    target_block,
    row_counts,
    reverse_block,
    valid_edges,
    weight_in,
    weight_out,
):
    devices = lax.axis_size("graph")
    edge_rows, part_width = messages.shape
    width = part_width * lax.axis_size("mp")
    blocks = edge_rows // BLK
    slots = source_block.shape[0]
    capacity = max(2, (slots + devices - 1) // devices + 1)
    border = blocks // 4
    near, far = split_bits(devices)
    groups = 1 << len(near)
    owners = devices // groups
    room = min(slots, capacity * owners)
    room = -(-room // UNROLL) * UNROLL
    rows = BLK // lax.axis_size("mp") // CHUNKS
    bf16 = jnp.bfloat16

    def near_send(array, k):
        return lax.ppermute(array, "graph", xor_pairs(devices, near_mask(near, k)))

    def far_send(array, bit):
        return lax.ppermute(array, "graph", xor_pairs(devices, 1 << bit))

    def swap(array):
        return lax.ppermute(array, "mp", [(0, 1), (1, 0)])

    def swap_halves(array):
        middle = array.shape[0] // 2
        return jnp.concatenate([swap(array[:middle]), swap(array[middle:])], axis=0)

    mine = [messages, near_send(messages, 1), near_send(messages, 2)]
    other = [swap(messages)]
    in_other, out_other = swap(weight_in), swap(weight_out)

    share = rows * CHUNKS
    whole_shape = jax.ShapeDtypeStruct((room + 1, share, BLK), bf16)
    packed = pl.pallas_call(
        functools.partial(pack_kernel, near, far, room, rows, blocks),
        out_shape=[whole_shape] * groups,
        in_specs=[smem()] * 4 + [full(None)],
        out_specs=[full(None)] * groups,
        scratch_shapes=[pltpu.SMEM((groups * room,), jnp.int32), pltpu.SMEM((groups,), jnp.int32)],
        compiler_params=grant(),
        cost_estimate=spent(6),
        name="pack",
    )(
        target_owner[:, 0],
        source_block,
        target_block,
        row_counts,
        after_all(basis_blocks, other[0], in_other, out_other),
    )
    last = groups - 1
    middle = edge_rows // 2
    acc_shape = (owners * blocks, rows, width)
    acc_bytes = owners * blocks * rows * width * 4
    partial = pl.pallas_call(
        functools.partial(first_kernel, 1, room),
        out_shape=jax.ShapeDtypeStruct((owners * blocks, share, width), jnp.float32),
        in_specs=[full(None)] * 3,
        out_specs=full(None),
        scratch_shapes=[
            pltpu.VMEM((1, 16, BLK), jnp.int32),
            pltpu.SMEM((1, 16, BLK), jnp.int32),
            pltpu.SemaphoreType.DMA,
        ],
        compiler_params=grant(CHUNKS * acc_bytes),
        cost_estimate=spent(2),
        name="own_products",
    )(packed[0], messages, other[0])

    basis = [packed[0]]
    for k in range(1, groups):
        basis.append(near_send(after_all(packed[k], partial), k))
    mine = [messages] + [after_all(array, partial) for array in mine[1:]]
    onward = [near_send(mine[1][:middle], 2), near_send(mine[2][middle:], 1)]
    mine.append(jnp.concatenate(onward, axis=0))
    other.extend(swap_halves(mine[k]) for k in range(1, groups))

    part_owners_shape = jax.ShapeDtypeStruct((owners // 4, blocks, rows, width), bf16)
    block_shape = jax.ShapeDtypeStruct((blocks, rows, width), bf16)
    part_shape = jax.ShapeDtypeStruct((blocks, rows, part_width), bf16)
    border_shape = jax.ShapeDtypeStruct((border, rows, width), bf16)
    even_pairs = [(i, i ^ 1) for i in range(devices)]
    odd_pairs = [(i, (i + 1 if i % 2 else i - 1) % devices) for i in range(devices)]
    summed = []
    for chunk in range(CHUNKS):
        summed.append(
            pl.pallas_call(
                functools.partial(last_kernel, last, room, blocks, rows, chunk),
                out_shape=[part_owners_shape] * 4,
                in_specs=[full(None)] * (3 * last + 1),
                out_specs=[full(None)] * 4,
                scratch_shapes=[
                    pltpu.VMEM(acc_shape, jnp.float32),
                    pltpu.VMEM((last, 16, BLK), jnp.int32),
                    pltpu.SMEM((last, 16, BLK), jnp.int32),
                    pltpu.SemaphoreType.DMA,
                ],
                compiler_params=grant(4 * acc_bytes),
                cost_estimate=spent(2),
                name="came_products",
            )(*basis[1:], *mine[1:], *other[1:], partial)
        )
    came_high = [far_send(parts[3], far[0]) for parts in summed]
    came_low = [far_send(after_all(parts[2], came_high[-1]), far[0]) for parts in summed]
    finals = []
    for chunk in range(CHUNKS):
        keep_low, keep_high = summed[chunk][:2]
        send = (keep_high.astype(jnp.float32) + came_high[chunk].astype(jnp.float32)).astype(bf16)
        addends = [keep_low, came_low[chunk]]
        size = owners // 4
        for index, bit in enumerate(far[1:]):
            addends.append(far_send(send, bit))
            if index + 2 < len(far):
                size = size // 2
                total = sum(part[size : 2 * size].astype(jnp.float32) for part in addends)
                send = total.astype(bf16)
        combined, even_send, odd_send = pl.pallas_call(
            functools.partial(combine_kernel, chunk, rows, border, len(addends)),
            out_shape=[block_shape, border_shape, border_shape],
            in_specs=[full(None)] * (2 + len(addends)),
            out_specs=[full(None)] * 3,
            compiler_params=grant(acc_bytes),
            cost_estimate=spent(0.5),
            name="combine",
        )(mine[0], other[0], *addends)
        came = [
            lax.ppermute(even_send, "graph", even_pairs),
            lax.ppermute(odd_send, "graph", odd_pairs),
        ]
        own, theirs = pl.pallas_call(
            functools.partial(mlp_kernel, chunk, rows, border),
            out_shape=[part_shape] * 2,
            in_specs=[smem()] * 2 + [full(None)] * 7,
            out_specs=[full(None)] * 2,
            scratch_shapes=[pltpu.VMEM((blocks * rows, width), jnp.float32)],
            compiler_params=grant(),
            cost_estimate=spent(2),
            name="mlp",
        )(
            reverse_block,
            valid_edges,
            combined,
            *came,
            weight_in,
            in_other,
            weight_out,
            out_other,
        )
        finals.append((own, swap(theirs)))

    return pl.pallas_call(
        functools.partial(join_kernel, rows),
        out_shape=jax.ShapeDtypeStruct(messages.shape, bf16),
        in_specs=[full(None)] * (2 * CHUNKS),
        out_specs=full(None),
        compiler_params=grant(),
        cost_estimate=spent(1),
        name="join",
    )(*[own for own, _ in finals], *[came for _, came in finals])


def solution(mesh):
    in_specs = (
        P("graph", "mp"),
        P("graph", None, None),
        P("graph"),
        P("graph", None),
        P("graph"),
        P("graph"),
        P("graph"),
        P("graph"),
        P(None, None, "mp"),
        P(None, "mp", None),
    )
    out_specs = P("graph", "mp")
    return jax.shard_map(local, mesh=mesh, in_specs=in_specs, out_specs=out_specs, check_vma=False)
```

time: 146 us -> 101 us (0.69)
  Pallas kernels: 41.9 us -> 18.1 us
  waiting for transfers between devices: 56.5 us -> 40.4 us
  starting transfers between devices: 39.7 us -> 35.5 us
    ppermute x12 -> x7, waiting for transfers between devices: 40.5 us -> 23.7 us  [near_send(): return lax.ppermute(array, 'graph', xor_pairs(devices, near_mask(near, k)))]
    pallas_call x2 -> x3, Pallas kernels: 19.4 us -> 8.97 us  [the longest x2 7.18 us: local(): pl.pallas_call(functools.partial(last_kernel, last, room, blocks, rows, c...]
    ppermute x12 -> x7, starting transfers between devices: 19 us -> 11.4 us  [near_send(): return lax.ppermute(array, 'graph', xor_pairs(devices, near_mask(near, k)))]
    pallas_call x2, Pallas kernels: 8.68 us -> 4.4 us  [local(): pl.pallas_call(functools.partial(mlp_kernel, chunk, rows, border), out_sh...]
    pallas_call x2, Pallas kernels: 4.52 us -> 0.27 us  [local(): pl.pallas_call(functools.partial(combine_kernel, chunk, rows, border, len...]
    pallas_call x1, Pallas kernels: 7.42 us -> 3.59 us  [local(): pl.pallas_call(functools.partial(pack_kernel, near, far, room, rows, bloc...]
    ppermute x8 -> x10, starting transfers between devices: 18.8 us -> 21.8 us  [the longest x6 11.6 us: far_send(): return lax.ppermute(array, 'graph', xor_pairs(devices, 1 << bit))]
    ppermute x8 -> x10, waiting for transfers between devices: 14.8 us -> 14.1 us  [the longest x6 13.6 us: far_send(): return lax.ppermute(array, 'graph', xor_pairs(devices, 1 << bit))]
  transfers between devices with their start and end apart: 28 -> 28, of which waited for: 11 -> 11; matrix products, arithmetic and copies ran while one was open for 1% -> 0% of each run, Pallas kernels for 21% -> 14%
where the time goes in v2:
time: 101 us
  waiting for transfers between devices  40.4 us (40%)
  starting transfers between devices  35.5 us (35%)
  Pallas kernels  18.1 us (18%)
  local copies, waits for them, and re-layouts  5.78 us (6%)
    ppermute x7, waiting for transfers between devices, near_send(): return lax.ppermute(array, 'graph', xor_pairs(devices, near_mask(near, k)))  23.7 us
    ppermute x6, waiting for transfers between devices, far_send(): return lax.ppermute(array, 'graph', xor_pairs(devices, 1 << bit))  13.6 us
    ppermute x6, starting transfers between devices, far_send(): return lax.ppermute(array, 'graph', xor_pairs(devices, 1 << bit))  11.6 us
    ppermute x7, starting transfers between devices, near_send(): return lax.ppermute(array, 'graph', xor_pairs(devices, near_mask(near, k)))  11.4 us
    ppermute x2, starting transfers between devices, local(): lax.ppermute(odd_send, 'graph', odd_pairs)  7.64 us
    pallas_call x2, Pallas kernels, local(): pl.pallas_call(functools.partial(last_kernel, last, room, blocks, rows, c...  7.18 us
    unnamed x24, local copies, waits for them, and re-layouts  5.64 us
    pallas_call x2, Pallas kernels, local(): pl.pallas_call(functools.partial(mlp_kernel, chunk, rows, border), out_sh...  4.4 us
  transfers between devices with their start and end apart: 28, of which 11 were waited for; matrix products, arithmetic and copies ran while one was open for 0% of the time, Pallas kernels for 14%

profile of v2, /device:TPU:0, one launch (start us, length us, event | category | flops | bytes accessed | tf_op | source)
XLA Modules:
  0.0 100.9 jit_solution(1066531518375192542)
XLA Ops:
  1.0 2.5 %collective-permute-start.6 = (bf16[1024,256]{1,0:T(8,128)(2,1)}, bf16[1024,256]{1,0:T(8,128)(2,1)S(1)}, u32[]{:S(2)}, u32[]{:S(2)}) collective-permute-start(bf16[1024,256]{1,0:T(8,128)(2,1)} %refs_0_.6), channel_id=1, source_target_pairs={{0,2},{2,0},{4,6},{6,4},{8,10},{10,8},{12,14},{14,12},{16,18},{18,... | collective-permute-start | bytes 1572872 | tf_op jit(solution)/shard_map/ppermute | solution.py:264
  3.5 1.6 %collective-permute-start.7 = (bf16[1024,256]{1,0:T(8,128)(2,1)}, bf16[1024,256]{1,0:T(8,128)(2,1)S(1)}, u32[]{:S(2)}, u32[]{:S(2)}) collective-permute-start(bf16[1024,256]{1,0:T(8,128)(2,1)} %refs_0_.6), channel_id=1, source_target_pairs={{0,8},{2,10},{4,12},{6,14},{8,0},{10,2},{12,4},{14,6},{16,24},{18,... | collective-permute-start | bytes 1572872 | tf_op jit(solution)/shard_map/ppermute | solution.py:264
  5.1 1.9 %copy-done.2 = bf16[96,128,128]{2,1,0:T(8,128)(2,1)S(1)} copy-done((bf16[96,128,128]{2,1,0:T(8,128)(2,1)S(1)}, bf16[96,128,128]{2,1,0:T(8,128)(2,1)}, u32[]{:S(2)}) %copy-start.2) | copy-done | bytes 3145752
  6.9 0.7 copy-done.6
  9.6 3.6 %pack.1 = (bf16[29,64,128]{2,1,0:T(8,128)(2,1)S(1)}, bf16[29,64,128]{2,1,0:T(8,128)(2,1)S(1)}, bf16[29,64,128]{2,1,0:T(8,128)(2,1)S(1)}, bf16[29,64,128]{2,1,0:T(8,128)(2,1)S(1)}) custom-call(s32[96]{0:T(128)S(1)} %bitcast.1, s32[96]{0:T(128)S(1)} %copy-done.7, s32[96]{0:T(128)S(1)} %copy-done.8, s32[96]{0:T(128)S(1)} %copy-done.9, ...), custom_call_target="tpu_custom_call" | custom-call | bytes 22140000 | tf_op jit(solution)/shard_map/pack/pallas_call | solution.py:282
  13.2 1.0 %copy-done = bf16[1024,256]{1,0:T(8,128)(2,1)S(1)} copy-done((bf16[1024,256]{1,0:T(8,128)(2,1)S(1)}, bf16[1024,256]{1,0:T(8,128)(2,1)}, u32[]{:S(2)}) %copy-start) | copy-done | bytes 524312
  14.2 1.8 %own_products.1.refs_9_ = f32[32,64,512]{2,1,0:T(8,128)S(1)} custom-call(bf16[29,64,128]{2,1,0:T(8,128)(2,1)S(1)} %get-tuple-element.37.refs_0_, bf16[1024,256]{1,0:T(8,128)(2,1)S(1)} %copy-done, bf16[1024,256]{1,0:T(8,128)(2,1)S(1)} %collective-permute-done.refs_2_.refs_1_), custom_call_target="tpu_custom_call" | custom-call | bytes 7380000 | tf_op jit(solution)/shard_map/own_products/pallas_call | solution.py:302
  16.3 2.2 %collective-permute-start.8 = (bf16[512,256]{1,0:T(8,128)(2,1)S(1)}, bf16[512,256]{1,0:T(8,128)(2,1)S(1)}, u32[]{:S(2)}, u32[]{:S(2)}) collective-permute-start(bf16[512,256]{1,0:T(8,128)(2,1)S(1)} %get-tuple-element.68), channel_id=1, source_target_pairs={{0,8},{2,10},{4,12},{6,14},{8,0},{10,2},{12,4},{14,6},{16,24},{18,... | collective-permute-start | bytes 786440 | tf_op jit(solution)/shard_map/ppermute | solution.py:264
  19.1 1.5 %collective-permute-start.9 = (bf16[512,256]{1,0:T(8,128)(2,1)S(1)}, bf16[512,256]{1,0:T(8,128)(2,1)S(1)}, u32[]{:S(2)}, u32[]{:S(2)}) collective-permute-start(bf16[512,256]{1,0:T(8,128)(2,1)S(1)} %get-tuple-element.66), channel_id=1, source_target_pairs={{0,2},{2,0},{4,6},{6,4},{8,10},{10,8},{12,14},{14,12},{16,18},{18,... | collective-permute-start | bytes 786440 | tf_op jit(solution)/shard_map/ppermute | solution.py:264
  20.6 4.5 %collective-permute-done.8 = bf16[512,256]{1,0:T(8,128)(2,1)S(1)} collective-permute-done((bf16[512,256]{1,0:T(8,128)(2,1)S(1)}, bf16[512,256]{1,0:T(8,128)(2,1)S(1)}, u32[]{:S(2)}, u32[]{:S(2)}) %collective-permute-start.8) | collective-permute-done | bytes 262176 | tf_op jit(solution)/shard_map/ppermute | solution.py:264
  25.1 2.7 %collective-permute-start.5 = (bf16[29,64,128]{2,1,0:T(8,128)(2,1)S(1)}, bf16[29,64,128]{2,1,0:T(8,128)(2,1)S(1)}, u32[]{:S(2)}, u32[]{:S(2)}) collective-permute-start(bf16[29,64,128]{2,1,0:T(8,128)(2,1)S(1)} %get-tuple-element.42), channel_id=1, source_target_pairs={{0,10},{2,8},{4,14},{6,12},{8,2},{10,0},{12,6},{14,4},{16,26},{18,... | collective-permute-start | bytes 1425416 | tf_op jit(solution)/shard_map/ppermute | solution.py:264
  29.5 0.9 collective-permute-done.14
  30.8 9.0 %collective-permute-done.5.refs_2_ = bf16[29,64,128]{2,1,0:T(8,128)(2,1)S(1)} collective-permute-done((bf16[29,64,128]{2,1,0:T(8,128)(2,1)S(1)}, bf16[29,64,128]{2,1,0:T(8,128)(2,1)S(1)}, u32[]{:S(2)}, u32[]{:S(2)}) %collective-permute-start.5) | collective-permute-done | bytes 475168 | tf_op jit(solution)/shard_map/ppermute | solution.py:264
  39.8 10.0 %collective-permute-done.4.refs_1_ = bf16[29,64,128]{2,1,0:T(8,128)(2,1)S(1)} collective-permute-done((bf16[29,64,128]{2,1,0:T(8,128)(2,1)S(1)}, bf16[29,64,128]{2,1,0:T(8,128)(2,1)S(1)}, u32[]{:S(2)}, u32[]{:S(2)}) %collective-permute-start.4) | collective-permute-done | bytes 475168 | tf_op jit(solution)/shard_map/ppermute | solution.py:264
  49.8 3.6 %came_products.3 = (bf16[1,8,32,512]{3,2,1,0:T(8,128)(2,1)S(1)}, bf16[1,8,32,512]{3,2,1,0:T(8,128)(2,1)S(1)}, bf16[1,8,32,512]{3,2,1,0:T(8,128)(2,1)S(1)}, bf16[1,8,32,512]{3,2,1,0:T(8,128)(2,1)S(1)}) custom-call(bf16[29,64,128]{2,1,0:T(8,128)(2,1)S(1)} %collective-permute-done.3.refs_0_, bf16[29,64,128]{2,1,0:T(8,128)(2,1)S(1)} %collective-permute-done.4.refs_1_, ...), custom_call_target="tpu_custom_call" | custom-call | bytes 7380000 | tf_op jit(solution)/shard_map/came_products/pallas_call | solution.py:334
  53.4 1.6 %collective-permute-start.16 = (bf16[1,8,32,512]{3,2,1,0:T(8,128)(2,1)S(1)}, bf16[1,8,32,512]{3,2,1,0:T(8,128)(2,1)S(1)}, u32[]{:S(2)}, u32[]{:S(2)}) collective-permute-start(bf16[1,8,32,512]{3,2,1,0:T(8,128)(2,1)S(1)} %get-tuple-element.47), channel_id=1, source_target_pairs={{0,4},{2,6},{4,0},{6,2},{8,12},{10,14},{12,8},{14,10},{16,20},{18,... | collective-permute-start | bytes 786440 | tf_op jit(solution)/shard_map/ppermute | solution.py:267
  55.0 3.6 %came_products.2 = (bf16[1,8,32,512]{3,2,1,0:T(8,128)(2,1)S(1)}, bf16[1,8,32,512]{3,2,1,0:T(8,128)(2,1)S(1)}, bf16[1,8,32,512]{3,2,1,0:T(8,128)(2,1)S(1)}, bf16[1,8,32,512]{3,2,1,0:T(8,128)(2,1)S(1)}) custom-call(bf16[29,64,128]{2,1,0:T(8,128)(2,1)S(1)} %collective-permute-done.3.refs_0_, bf16[29,64,128]{2,1,0:T(8,128)(2,1)S(1)} %collective-permute-done.4.refs_1_, ...), custom_call_target="tpu_custom_call" | custom-call | bytes 7380000 | tf_op jit(solution)/shard_map/came_products/pallas_call | solution.py:334
  59.2 2.8 %collective-permute-done.16 = bf16[1,8,32,512]{3,2,1,0:T(8,128)(2,1)S(1)} collective-permute-done((bf16[1,8,32,512]{3,2,1,0:T(8,128)(2,1)S(1)}, bf16[1,8,32,512]{3,2,1,0:T(8,128)(2,1)S(1)}, u32[]{:S(2)}, u32[]{:S(2)}) %collective-permute-start.16) | collective-permute-done | bytes 262176 | tf_op jit(solution)/shard_map/ppermute | solution.py:267
  62.0 2.9 %collective-permute-start.23 = (bf16[1,8,32,512]{3,2,1,0:T(8,128)(2,1)S(1)}, bf16[1,8,32,512]{3,2,1,0:T(8,128)(2,1)S(1)}, u32[]{:S(2)}, u32[]{:S(2)}) collective-permute-start(bf16[1,8,32,512]{3,2,1,0:T(8,128)(2,1)S(1)} %add_convert_fusion), channel_id=1, source_target_pairs={{0,16},{2,18},{4,20},{6,22},{8,24},{10,26},{12,28},{14,30},{16,0},... | collective-permute-start | bytes 786440 | tf_op jit(solution)/shard_map/ppermute | solution.py:267
  65.0 2.0 %collective-permute-start.22 = (bf16[1,8,32,512]{3,2,1,0:T(8,128)(2,1)S(1)}, bf16[1,8,32,512]{3,2,1,0:T(8,128)(2,1)S(1)}, u32[]{:S(2)}, u32[]{:S(2)}) collective-permute-start(bf16[1,8,32,512]{3,2,1,0:T(8,128)(2,1)S(1)} %get-tuple-element.57), channel_id=1, source_target_pairs={{0,4},{2,6},{4,0},{6,2},{8,12},{10,14},{12,8},{14,10},{16,20},{18,... | collective-permute-start | bytes 786440 | tf_op jit(solution)/shard_map/ppermute | solution.py:267
  66.9 1.0 %collective-permute-done.18 = bf16[1,8,32,512]{3,2,1,0:T(8,128)(2,1)S(1)} collective-permute-done((bf16[1,8,32,512]{3,2,1,0:T(8,128)(2,1)S(1)}, bf16[1,8,32,512]{3,2,1,0:T(8,128)(2,1)S(1)}, u32[]{:S(2)}, u32[]{:S(2)}) %collective-permute-start.18) | collective-permute-done | bytes 262176 | tf_op jit(solution)/shard_map/ppermute | solution.py:267
  68.0 2.6 %collective-permute-start.19 = (bf16[1,8,32,512]{3,2,1,0:T(8,128)(2,1)S(1)}, bf16[1,8,32,512]{3,2,1,0:T(8,128)(2,1)S(1)}, u32[]{:S(2)}, u32[]{:S(2)}) collective-permute-start(bf16[1,8,32,512]{3,2,1,0:T(8,128)(2,1)S(1)} %add_convert_fusion.1), channel_id=1, source_target_pairs={{0,16},{2,18},{4,20},{6,22},{8,24},{10,26},{12,28},{14,30},{16,0},... | collective-permute-start | bytes 786440 | tf_op jit(solution)/shard_map/ppermute | solution.py:267
  70.6 1.9 %collective-permute-start.17 = (bf16[1,8,32,512]{3,2,1,0:T(8,128)(2,1)S(1)}, bf16[1,8,32,512]{3,2,1,0:T(8,128)(2,1)S(1)}, u32[]{:S(2)}, u32[]{:S(2)}) collective-permute-start(bf16[1,8,32,512]{3,2,1,0:T(8,128)(2,1)S(1)} %get-tuple-element.48), channel_id=1, source_target_pairs={{0,4},{2,6},{4,0},{6,2},{8,12},{10,14},{12,8},{14,10},{16,20},{18,... | collective-permute-start | bytes 786440 | tf_op jit(solution)/shard_map/ppermute | solution.py:267
  72.5 9.8 %collective-permute-done.23.refs_4_ = bf16[1,8,32,512]{3,2,1,0:T(8,128)(2,1)S(1)} collective-permute-done((bf16[1,8,32,512]{3,2,1,0:T(8,128)(2,1)S(1)}, bf16[1,8,32,512]{3,2,1,0:T(8,128)(2,1)S(1)}, u32[]{:S(2)}, u32[]{:S(2)}) %collective-permute-start.23) | collective-permute-done | bytes 262176 | tf_op jit(solution)/shard_map/ppermute | solution.py:267
  82.4 1.6 %collective-permute-start.24 = (bf16[2,32,512]{2,1,0:T(8,128)(2,1)S(1)}, bf16[2,32,512]{2,1,0:T(8,128)(2,1)S(1)}, u32[]{:S(2)}, u32[]{:S(2)}) collective-permute-start(bf16[2,32,512]{2,1,0:T(8,128)(2,1)S(1)} %get-tuple-element.60), channel_id=1, source_target_pairs={{0,2},{2,0},{4,6},{6,4},{8,10},{10,8},{12,14},{14,12},{16,18},{18,... | collective-permute-start | bytes 196616 | tf_op jit(solution)/shard_map/ppermute | solution.py:374
  84.1 3.3 %collective-permute-start.25 = (bf16[2,32,512]{2,1,0:T(8,128)(2,1)S(1)}, bf16[2,32,512]{2,1,0:T(8,128)(2,1)S(1)}, u32[]{:S(2)}, u32[]{:S(2)}) collective-permute-start(bf16[2,32,512]{2,1,0:T(8,128)(2,1)S(1)} %get-tuple-element.61), channel_id=1, source_target_pairs={{0,30},{2,4},{4,2},{6,8},{8,6},{10,12},{12,10},{14,16},{16,14},{18... | collective-permute-start | bytes 196616 | tf_op jit(solution)/shard_map/ppermute | solution.py:375
  87.6 1.0 collective-permute-start.20
  88.5 4.3 %collective-permute-start.21 = (bf16[2,32,512]{2,1,0:T(8,128)(2,1)S(1)}, bf16[2,32,512]{2,1,0:T(8,128)(2,1)S(1)}, u32[]{:S(2)}, u32[]{:S(2)}) collective-permute-start(bf16[2,32,512]{2,1,0:T(8,128)(2,1)S(1)} %get-tuple-element.53), channel_id=1, source_target_pairs={{0,30},{2,4},{4,2},{6,8},{8,6},{10,12},{12,10},{14,16},{16,14},{18... | collective-permute-start | bytes 196616 | tf_op jit(solution)/shard_map/ppermute | solution.py:375
  93.6 2.2 %mlp.3 = (bf16[8,32,256]{2,1,0:T(8,128)(2,1)S(1)}, bf16[8,32,256]{2,1,0:T(8,128)(2,1)S(1)}) custom-call(s32[8]{0:T(128)S(1)} %copy-done.5, s32[1]{0:T(128)S(6)} %copy.15.valid, bf16[8,32,512]{2,1,0:T(8,128)(2,1)S(1)} %get-tuple-element.59.combined, bf16[2,32,512]{2,1,0:T(8,128)(2,1)S(1)} %collective-permute-done.24.even_came, ...), custom_call_target="tpu_custom_call" | custom-call | bytes 7380000 | tf_op jit(solution)/shard_map/mlp/pallas_call | solution.py:377
  96.4 2.2 %mlp.2 = (bf16[8,32,256]{2,1,0:T(8,128)(2,1)S(1)}, bf16[8,32,256]{2,1,0:T(8,128)(2,1)S(1)}) custom-call(s32[8]{0:T(128)S(1)} %copy-done.5, s32[1]{0:T(128)S(6)} %copy.15.valid, bf16[8,32,512]{2,1,0:T(8,128)(2,1)S(1)} %get-tuple-element.51.combined, bf16[2,32,512]{2,1,0:T(8,128)(2,1)S(1)} %collective-permute-done.20.even_came, ...), custom_call_target="tpu_custom_call" | custom-call | bytes 7380000 | tf_op jit(solution)/shard_map/mlp/pallas_call | solution.py:377
  98.7 1.3 %collective-permute-done.26.refs_2_ = bf16[8,32,256]{2,1,0:T(8,128)(2,1)S(1)} collective-permute-done((bf16[8,32,256]{2,1,0:T(8,128)(2,1)S(1)}, bf16[8,32,256]{2,1,0:T(8,128)(2,1)S(1)}, u32[]{:S(2)}, u32[]{:S(2)}) %collective-permute-start.26) | collective-permute-done | bytes 131104 | tf_op jit(solution)/shard_map/ppermute | solution.py:270
  100.0 0.8 join.1
  (65 shorter events, 7.6 us)
Async XLA Ops:
  0.0 5.0 %collective-permute-start.1 = (bf16[3,512,256]{2,1,0:T(8,128)(2,1)}, bf16[3,512,256]{2,1,0:T(8,128)(2,1)S(1)}, u32[]{:S(2)}, u32[]{:S(2)}) collective-permute-start(bf16[3,512,256]{2,1,0:T(8,128)(2,1)} %refs_0_.7), channel_id=1, source_target_pairs={{0,1},{1,0},{2,3},{3,2},{4,5},{5,4},{6,7},{7,6},{8,9},{9,8},{10,11... | collective-permute-start | bytes 2359304 | tf_op jit(solution)/shard_map/ppermute | solution.py:270
  0.5 4.6 %collective-permute-start.2 = (bf16[3,256,512]{2,1,0:T(8,128)(2,1)}, bf16[3,256,512]{2,1,0:T(8,128)(2,1)S(1)}, u32[]{:S(2)}, u32[]{:S(2)}) collective-permute-start(bf16[3,256,512]{2,1,0:T(8,128)(2,1)} %refs_2_.3), channel_id=1, source_target_pairs={{0,1},{1,0},{2,3},{3,2},{4,5},{5,4},{6,7},{7,6},{8,9},{9,8},{10,11... | collective-permute-start | bytes 2359304 | tf_op jit(solution)/shard_map/ppermute | solution.py:270
  0.5 4.5 %collective-permute-start = (bf16[1024,256]{1,0:T(8,128)(2,1)}, bf16[1024,256]{1,0:T(8,128)(2,1)S(1)}, u32[]{:S(2)}, u32[]{:S(2)}) collective-permute-start(bf16[1024,256]{1,0:T(8,128)(2,1)} %refs_0_.6), channel_id=1, source_target_pairs={{0,1},{1,0},{2,3},{3,2},{4,5},{5,4},{6,7},{7,6},{8,9},{9,8},{10,11... | collective-permute-start | bytes 1572872 | tf_op jit(solution)/shard_map/ppermute | solution.py:270
  1.0 15.3 %collective-permute-start.6 = (bf16[1024,256]{1,0:T(8,128)(2,1)}, bf16[1024,256]{1,0:T(8,128)(2,1)S(1)}, u32[]{:S(2)}, u32[]{:S(2)}) collective-permute-start(bf16[1024,256]{1,0:T(8,128)(2,1)} %refs_0_.6), channel_id=1, source_target_pairs={{0,2},{2,0},{4,6},{6,4},{8,10},{10,8},{12,14},{14,12},{16,18},{18,... | collective-permute-start | bytes 1572872 | tf_op jit(solution)/shard_map/ppermute | solution.py:264
  3.5 15.0 %collective-permute-start.7 = (bf16[1024,256]{1,0:T(8,128)(2,1)}, bf16[1024,256]{1,0:T(8,128)(2,1)S(1)}, u32[]{:S(2)}, u32[]{:S(2)}) collective-permute-start(bf16[1024,256]{1,0:T(8,128)(2,1)} %refs_0_.6), channel_id=1, source_target_pairs={{0,8},{2,10},{4,12},{6,14},{8,0},{10,2},{12,4},{14,6},{16,24},{18,... | collective-permute-start | bytes 1572872 | tf_op jit(solution)/shard_map/ppermute | solution.py:264
  16.3 8.8 %collective-permute-start.8 = (bf16[512,256]{1,0:T(8,128)(2,1)S(1)}, bf16[512,256]{1,0:T(8,128)(2,1)S(1)}, u32[]{:S(2)}, u32[]{:S(2)}) collective-permute-start(bf16[512,256]{1,0:T(8,128)(2,1)S(1)} %get-tuple-element.68), channel_id=1, source_target_pairs={{0,8},{2,10},{4,12},{6,14},{8,0},{10,2},{12,4},{14,6},{16,24},{18,... | collective-permute-start | bytes 786440 | tf_op jit(solution)/shard_map/ppermute | solution.py:264
  18.5 6.6 %collective-permute-start.12 = (bf16[512,256]{1,0:T(8,128)(2,1)S(1)}, bf16[512,256]{1,0:T(8,128)(2,1)S(1)}, u32[]{:S(2)}, u32[]{:S(2)}) collective-permute-start(bf16[512,256]{1,0:T(8,128)(2,1)S(1)} %get-tuple-element.65), channel_id=1, source_target_pairs={{0,1},{1,0},{2,3},{3,2},{4,5},{5,4},{6,7},{7,6},{8,9},{9,8},{10,11... | collective-permute-start | bytes 786440 | tf_op jit(solution)/shard_map/ppermute | solution.py:270
  18.6 9.3 %collective-permute-start.10 = (bf16[512,256]{1,0:T(8,128)(2,1)S(1)}, bf16[512,256]{1,0:T(8,128)(2,1)S(1)}, u32[]{:S(2)}, u32[]{:S(2)}) collective-permute-start(bf16[512,256]{1,0:T(8,128)(2,1)S(1)} %get-tuple-element.68), channel_id=1, source_target_pairs={{0,1},{1,0},{2,3},{3,2},{4,5},{5,4},{6,7},{7,6},{8,9},{9,8},{10,11... | collective-permute-start | bytes 786440 | tf_op jit(solution)/shard_map/ppermute | solution.py:270
  19.1 9.3 %collective-permute-start.9 = (bf16[512,256]{1,0:T(8,128)(2,1)S(1)}, bf16[512,256]{1,0:T(8,128)(2,1)S(1)}, u32[]{:S(2)}, u32[]{:S(2)}) collective-permute-start(bf16[512,256]{1,0:T(8,128)(2,1)S(1)} %get-tuple-element.66), channel_id=1, source_target_pairs={{0,2},{2,0},{4,6},{6,4},{8,10},{10,8},{12,14},{14,12},{16,18},{18,... | collective-permute-start | bytes 786440 | tf_op jit(solution)/shard_map/ppermute | solution.py:264
  20.6 8.3 %collective-permute-start.13 = (bf16[512,256]{1,0:T(8,128)(2,1)S(1)}, bf16[512,256]{1,0:T(8,128)(2,1)S(1)}, u32[]{:S(2)}, u32[]{:S(2)}) collective-permute-start(bf16[512,256]{1,0:T(8,128)(2,1)S(1)} %get-tuple-element.66), channel_id=1, source_target_pairs={{0,1},{1,0},{2,3},{3,2},{4,5},{5,4},{6,7},{7,6},{8,9},{9,8},{10,11... | collective-permute-start | bytes 786440 | tf_op jit(solution)/shard_map/ppermute | solution.py:270
  25.1 3.8 %collective-permute-start.11 = (bf16[512,256]{1,0:T(8,128)(2,1)S(1)}, bf16[512,256]{1,0:T(8,128)(2,1)S(1)}, u32[]{:S(2)}, u32[]{:S(2)}) collective-permute-start(bf16[512,256]{1,0:T(8,128)(2,1)S(1)} %get-tuple-element.67), channel_id=1, source_target_pairs={{0,1},{1,0},{2,3},{3,2},{4,5},{5,4},{6,7},{7,6},{8,9},{9,8},{10,11... | collective-permute-start | bytes 786440 | tf_op jit(solution)/shard_map/ppermute | solution.py:270
  25.1 14.7 %collective-permute-start.5 = (bf16[29,64,128]{2,1,0:T(8,128)(2,1)S(1)}, bf16[29,64,128]{2,1,0:T(8,128)(2,1)S(1)}, u32[]{:S(2)}, u32[]{:S(2)}) collective-permute-start(bf16[29,64,128]{2,1,0:T(8,128)(2,1)S(1)} %get-tuple-element.42), channel_id=1, source_target_pairs={{0,10},{2,8},{4,14},{6,12},{8,2},{10,0},{12,6},{14,4},{16,26},{18,... | collective-permute-start | bytes 1425416 | tf_op jit(solution)/shard_map/ppermute | solution.py:264
  27.9 21.9 %collective-permute-start.4 = (bf16[29,64,128]{2,1,0:T(8,128)(2,1)S(1)}, bf16[29,64,128]{2,1,0:T(8,128)(2,1)S(1)}, u32[]{:S(2)}, u32[]{:S(2)}) collective-permute-start(bf16[29,64,128]{2,1,0:T(8,128)(2,1)S(1)} %get-tuple-element.40), channel_id=1, source_target_pairs={{0,8},{2,10},{4,12},{6,14},{8,0},{10,2},{12,4},{14,6},{16,24},{18,... | collective-permute-start | bytes 1425416 | tf_op jit(solution)/shard_map/ppermute | solution.py:264
  28.4 21.4 %collective-permute-start.3 = (bf16[29,64,128]{2,1,0:T(8,128)(2,1)S(1)}, bf16[29,64,128]{2,1,0:T(8,128)(2,1)S(1)}, u32[]{:S(2)}, u32[]{:S(2)}) collective-permute-start(bf16[29,64,128]{2,1,0:T(8,128)(2,1)S(1)} %get-tuple-element.38), channel_id=1, source_target_pairs={{0,2},{2,0},{4,6},{6,4},{8,10},{10,8},{12,14},{14,12},{16,18},{18,... | collective-permute-start | bytes 1425416 | tf_op jit(solution)/shard_map/ppermute | solution.py:264
  28.9 1.5 %collective-permute-start.14 = (bf16[512,256]{1,0:T(8,128)(2,1)S(1)}, bf16[512,256]{1,0:T(8,128)(2,1)S(1)}, u32[]{:S(2)}, u32[]{:S(2)}) collective-permute-start(bf16[512,256]{1,0:T(8,128)(2,1)S(1)} %collective-permute-done.8), channel_id=1, source_target_pairs={{0,1},{1,0},{2,3},{3,2},{4,5},{5,4},{6,7},{7,6},{8,9},{9,8},{10,11... | collective-permute-start | bytes 786440 | tf_op jit(solution)/shard_map/ppermute | solution.py:270
  28.9 1.9 %collective-permute-start.15 = (bf16[512,256]{1,0:T(8,128)(2,1)S(1)}, bf16[512,256]{1,0:T(8,128)(2,1)S(1)}, u32[]{:S(2)}, u32[]{:S(2)}) collective-permute-start(bf16[512,256]{1,0:T(8,128)(2,1)S(1)} %collective-permute-done.9), channel_id=1, source_target_pairs={{0,1},{1,0},{2,3},{3,2},{4,5},{5,4},{6,7},{7,6},{8,9},{9,8},{10,11... | collective-permute-start | bytes 786440 | tf_op jit(solution)/shard_map/ppermute | solution.py:270
  53.4 28.9 %copy-start.1 = (bf16[1024,256]{1,0:T(8,128)(2,1)S(1)}, bf16[1024,256]{1,0:T(8,128)(2,1)}, u32[]{:S(2)}) copy-start(bf16[1024,256]{1,0:T(8,128)(2,1)} %refs_0_.6) | copy-start | bytes 1572868
  53.4 8.6 %collective-permute-start.16 = (bf16[1,8,32,512]{3,2,1,0:T(8,128)(2,1)S(1)}, bf16[1,8,32,512]{3,2,1,0:T(8,128)(2,1)S(1)}, u32[]{:S(2)}, u32[]{:S(2)}) collective-permute-start(bf16[1,8,32,512]{3,2,1,0:T(8,128)(2,1)S(1)} %get-tuple-element.47), channel_id=1, source_target_pairs={{0,4},{2,6},{4,0},{6,2},{8,12},{10,14},{12,8},{14,10},{16,20},{18,... | collective-permute-start | bytes 786440 | tf_op jit(solution)/shard_map/ppermute | solution.py:267
  58.6 34.9 %copy-start.3 = (bf16[3,512,256]{2,1,0:T(8,128)(2,1)S(1)}, bf16[3,512,256]{2,1,0:T(8,128)(2,1)}, u32[]{:S(2)}) copy-start(bf16[3,512,256]{2,1,0:T(8,128)(2,1)} %refs_0_.7) | copy-start | bytes 2359300
  58.6 34.9 %copy-start.4 = (bf16[3,256,512]{2,1,0:T(8,128)(2,1)S(1)}, bf16[3,256,512]{2,1,0:T(8,128)(2,1)}, u32[]{:S(2)}) copy-start(bf16[3,256,512]{2,1,0:T(8,128)(2,1)} %refs_2_.3) | copy-start | bytes 2359300
  58.6 34.9 %copy-start.5 = (s32[8]{0:T(128)S(1)}, s32[8]{0:T(128)}, u32[]{:S(2)}) copy-start(s32[8]{0:T(128)} %reverse.3) | copy-start | bytes 100
  58.6 9.3 %collective-permute-start.18 = (bf16[1,8,32,512]{3,2,1,0:T(8,128)(2,1)S(1)}, bf16[1,8,32,512]{3,2,1,0:T(8,128)(2,1)S(1)}, u32[]{:S(2)}, u32[]{:S(2)}) collective-permute-start(bf16[1,8,32,512]{3,2,1,0:T(8,128)(2,1)S(1)} %get-tuple-element.50), channel_id=1, source_target_pairs={{0,4},{2,6},{4,0},{6,2},{8,12},{10,14},{12,8},{14,10},{16,20},{18,... | collective-permute-start | bytes 786440 | tf_op jit(solution)/shard_map/ppermute | solution.py:267
  62.0 20.3 %collective-permute-start.23 = (bf16[1,8,32,512]{3,2,1,0:T(8,128)(2,1)S(1)}, bf16[1,8,32,512]{3,2,1,0:T(8,128)(2,1)S(1)}, u32[]{:S(2)}, u32[]{:S(2)}) collective-permute-start(bf16[1,8,32,512]{3,2,1,0:T(8,128)(2,1)S(1)} %add_convert_fusion), channel_id=1, source_target_pairs={{0,16},{2,18},{4,20},{6,22},{8,24},{10,26},{12,28},{14,30},{16,0},... | collective-permute-start | bytes 786440 | tf_op jit(solution)/shard_map/ppermute | solution.py:267
  65.0 17.3 %collective-permute-start.22 = (bf16[1,8,32,512]{3,2,1,0:T(8,128)(2,1)S(1)}, bf16[1,8,32,512]{3,2,1,0:T(8,128)(2,1)S(1)}, u32[]{:S(2)}, u32[]{:S(2)}) collective-permute-start(bf16[1,8,32,512]{3,2,1,0:T(8,128)(2,1)S(1)} %get-tuple-element.57), channel_id=1, source_target_pairs={{0,4},{2,6},{4,0},{6,2},{8,12},{10,14},{12,8},{14,10},{16,20},{18,... | collective-permute-start | bytes 786440 | tf_op jit(solution)/shard_map/ppermute | solution.py:267
  68.0 19.4 %collective-permute-start.19 = (bf16[1,8,32,512]{3,2,1,0:T(8,128)(2,1)S(1)}, bf16[1,8,32,512]{3,2,1,0:T(8,128)(2,1)S(1)}, u32[]{:S(2)}, u32[]{:S(2)}) collective-permute-start(bf16[1,8,32,512]{3,2,1,0:T(8,128)(2,1)S(1)} %add_convert_fusion.1), channel_id=1, source_target_pairs={{0,16},{2,18},{4,20},{6,22},{8,24},{10,26},{12,28},{14,30},{16,0},... | collective-permute-start | bytes 786440 | tf_op jit(solution)/shard_map/ppermute | solution.py:267
  70.6 16.8 %collective-permute-start.17 = (bf16[1,8,32,512]{3,2,1,0:T(8,128)(2,1)S(1)}, bf16[1,8,32,512]{3,2,1,0:T(8,128)(2,1)S(1)}, u32[]{:S(2)}, u32[]{:S(2)}) collective-permute-start(bf16[1,8,32,512]{3,2,1,0:T(8,128)(2,1)S(1)} %get-tuple-element.48), channel_id=1, source_target_pairs={{0,4},{2,6},{4,0},{6,2},{8,12},{10,14},{12,8},{14,10},{16,20},{18,... | collective-permute-start | bytes 786440 | tf_op jit(solution)/shard_map/ppermute | solution.py:267
  82.4 11.1 %collective-permute-start.24 = (bf16[2,32,512]{2,1,0:T(8,128)(2,1)S(1)}, bf16[2,32,512]{2,1,0:T(8,128)(2,1)S(1)}, u32[]{:S(2)}, u32[]{:S(2)}) collective-permute-start(bf16[2,32,512]{2,1,0:T(8,128)(2,1)S(1)} %get-tuple-element.60), channel_id=1, source_target_pairs={{0,2},{2,0},{4,6},{6,4},{8,10},{10,8},{12,14},{14,12},{16,18},{18,... | collective-permute-start | bytes 196616 | tf_op jit(solution)/shard_map/ppermute | solution.py:374
  84.1 9.4 %collective-permute-start.25 = (bf16[2,32,512]{2,1,0:T(8,128)(2,1)S(1)}, bf16[2,32,512]{2,1,0:T(8,128)(2,1)S(1)}, u32[]{:S(2)}, u32[]{:S(2)}) collective-permute-start(bf16[2,32,512]{2,1,0:T(8,128)(2,1)S(1)} %get-tuple-element.61), channel_id=1, source_target_pairs={{0,30},{2,4},{4,2},{6,8},{8,6},{10,12},{12,10},{14,16},{16,14},{18... | collective-permute-start | bytes 196616 | tf_op jit(solution)/shard_map/ppermute | solution.py:375
  87.6 8.3 %collective-permute-start.20 = (bf16[2,32,512]{2,1,0:T(8,128)(2,1)S(1)}, bf16[2,32,512]{2,1,0:T(8,128)(2,1)S(1)}, u32[]{:S(2)}, u32[]{:S(2)}) collective-permute-start(bf16[2,32,512]{2,1,0:T(8,128)(2,1)S(1)} %get-tuple-element.52), channel_id=1, source_target_pairs={{0,2},{2,0},{4,6},{6,4},{8,10},{10,8},{12,14},{14,12},{16,18},{18,... | collective-permute-start | bytes 196616 | tf_op jit(solution)/shard_map/ppermute | solution.py:374
  88.5 7.9 %collective-permute-start.21 = (bf16[2,32,512]{2,1,0:T(8,128)(2,1)S(1)}, bf16[2,32,512]{2,1,0:T(8,128)(2,1)S(1)}, u32[]{:S(2)}, u32[]{:S(2)}) collective-permute-start(bf16[2,32,512]{2,1,0:T(8,128)(2,1)S(1)} %get-tuple-element.53), channel_id=1, source_target_pairs={{0,30},{2,4},{4,2},{6,8},{8,6},{10,12},{12,10},{14,16},{16,14},{18... | collective-permute-start | bytes 196616 | tf_op jit(solution)/shard_map/ppermute | solution.py:375
  95.8 2.9 %collective-permute-start.27 = (bf16[8,32,256]{2,1,0:T(8,128)(2,1)S(1)}, bf16[8,32,256]{2,1,0:T(8,128)(2,1)S(1)}, u32[]{:S(2)}, u32[]{:S(2)}) collective-permute-start(bf16[8,32,256]{2,1,0:T(8,128)(2,1)S(1)} %get-tuple-element.64), channel_id=1, source_target_pairs={{0,1},{1,0},{2,3},{3,2},{4,5},{5,4},{6,7},{7,6},{8,9},{9,8},{10,11... | collective-permute-start | bytes 393224 | tf_op jit(solution)/shard_map/ppermute | solution.py:270
  98.6 1.4 %collective-permute-start.26 = (bf16[8,32,256]{2,1,0:T(8,128)(2,1)S(1)}, bf16[8,32,256]{2,1,0:T(8,128)(2,1)S(1)}, u32[]{:S(2)}, u32[]{:S(2)}) collective-permute-start(bf16[8,32,256]{2,1,0:T(8,128)(2,1)S(1)} %get-tuple-element.63), channel_id=1, source_target_pairs={{0,1},{1,0},{2,3},{3,2},{4,5},{5,4},{6,7},{7,6},{8,9},{9,8},{10,11... | collective-permute-start | bytes 393224 | tf_op jit(solution)/shard_map/ppermute | solution.py:270
  (6 other events, 5.6 us)

commit v3 on v2

v3 whole, which is shorter than its diff:
```python
import functools

import jax
import jax.numpy as jnp
from jax import lax
from jax.experimental import pallas as pl
from jax.experimental.pallas import tpu as pltpu
from jax.sharding import PartitionSpec as P

MLPS = 3
BLK = 128
CHUNKS = 2
UNROLL = 14
GRANT = 12 * 1024 * 1024

pair_scale = 0.7071067811865476


def split_bits(devices):
    count = devices.bit_length() - 1
    near = [bit for bit in (0, 2) if bit < count]
    far = [bit for bit in range(count) if bit not in near]
    return near, far


def xor_pairs(devices, mask):
    return [(i, i ^ mask) for i in range(devices)]


def near_mask(near, k):
    return sum(((k >> i) & 1) << bit for i, bit in enumerate(near))


def grant(extra=0):
    return pltpu.CompilerParams(vmem_limit_bytes=GRANT + extra)


def spent(microseconds):
    return pl.CostEstimate(
        flops=0, bytes_accessed=int(microseconds * 3.69e6), transcendentals=0
    )


def after_all(value, *others):
    if not others:
        return value
    return lax.optimization_barrier((value, *others))[0]


def full(shape):
    return pl.BlockSpec(memory_space=pltpu.VMEM)


def smem():
    return pl.BlockSpec(memory_space=pltpu.SMEM)


def pack_kernel(near, far, room, rows, blocks, owner, source, target, counts, basis, *refs):
    groups = 1 << len(near)
    whole, cut = refs[: groups - 1], refs[groups - 1 : groups - 1 + CHUNKS]
    table, fill = refs[groups - 1 + CHUNKS :]
    slots = basis.shape[0]
    me = lax.axis_index("graph")
    core = lax.axis_index("mp")
    for k in range(groups):
        fill[k] = 0

    def clear(i, carry):
        table[i] = -1
        return carry

    lax.fori_loop(0, groups * room, clear, 0, unroll=4)

    def route(t, carry):
        rel = owner[t] ^ me
        k = 0
        for i, bit in enumerate(near):
            k = k + (((rel >> bit) & 1) << i)
        p = fill[k]
        fill[k] = p + 1
        table[k * room + p] = t
        return carry

    lax.fori_loop(0, slots, route, 0)

    share = rows * CHUNKS
    first = core * share
    row = lax.broadcasted_iota(jnp.int32, (share, BLK), 0)
    label_row = lax.broadcasted_iota(jnp.int32, (rows, BLK), 0)
    lane = lax.broadcasted_iota(jnp.int32, (rows, BLK), 1)
    for k in range(groups):

        def one(p, labels):
            t = table[k * room + p]
            there = t >= 0
            s = jnp.maximum(t, 0)
            rel = owner[s] ^ me
            b = 0
            for i, bit in enumerate(far):
                b = b + (((rel >> bit) & 1) << (len(far) - 1 - i))
            place = jnp.where(there, b * blocks + target[s], 0)
            place = jnp.where(label_row == 0, place, source[s])
            labels = jnp.where(lane == p, place, labels)
            count = jnp.where(there, counts[s], 0)
            block = basis[s, pl.ds(pl.multiple_of(first, share), share), :]
            block = jnp.where(row + first < count, block, jnp.zeros_like(block))
            if k < groups - 1:
                whole[k][p] = block
            else:
                for j in range(CHUNKS):
                    cut[j][p] = block[j * rows : (j + 1) * rows]
            return labels

        labels = lax.fori_loop(0, room, one, jnp.zeros((rows, BLK), jnp.int32), unroll=2)
        labels = labels.astype(jnp.float32).astype(jnp.bfloat16)
        if k < groups - 1:
            whole[k][room, :rows] = labels
        else:
            cut[0][room] = labels


def add_products(room, labels, basis, mine, other, acc, staged, metas, sem):
    sources = len(basis)
    core = lax.axis_index("mp")
    width = mine[0].shape[1]
    own_cols = pl.ds(pl.multiple_of(core * width, width), width)
    other_cols = pl.ds(pl.multiple_of((1 - core) * width, width), width)
    for k in range(sources):
        staged[k] = labels[k][room, :16, :].astype(jnp.float32).astype(jnp.int32)
    copy = pltpu.make_async_copy(staged, metas, sem)
    copy.start()
    acc[...] = jnp.zeros_like(acc)
    copy.wait()
    for k in range(sources):

        def some(step, carry):
            sums = []
            for u in range(UNROLL):
                p = step * UNROLL + u
                s = metas[k, 1, p]
                at = pl.ds(pl.multiple_of(s * BLK, BLK), BLK)
                left = basis[k][p]
                a = jnp.dot(left, mine[k][at, :], preferred_element_type=jnp.float32)
                b = jnp.dot(left, other[k][at, :], preferred_element_type=jnp.float32)
                sums.append((metas[k, 0, p], a, b))
            for at, a, b in sums:
                acc[at, :, own_cols] += a
                acc[at, :, other_cols] += b
            return carry

        lax.fori_loop(0, room // UNROLL, some, 0)


def first_kernel(sources, room, *refs):
    basis, mine, other = (refs[i * sources : (i + 1) * sources] for i in range(3))
    acc, staged, metas, sem = refs[3 * sources :]
    add_products(room, basis, basis, mine, other, acc, staged, metas, sem)


def last_kernel(room, blocks, rows, chunk, labels, basis, mine, other, before, *refs):
    keep_low, keep_high, send_low, send_high, acc, staged, metas, sem = refs
    held = slice(chunk * rows, (chunk + 1) * rows)
    add_products(room, [labels], [basis], [mine], [other], acc, staged, metas, sem)
    part = keep_low.shape[0]
    for i, out in enumerate((keep_low, keep_high, send_low, send_high)):
        for o in range(part):
            at = slice((i * part + o) * blocks, (i * part + o + 1) * blocks)
            out[o] = (before[at, held] + acc[at]).astype(out.dtype)


def combine_kernel(rows, border, start, bases, *refs):
    mine, other = refs[:2]
    counts = [len(each) for each in bases]
    addends, outs = refs[2 : 2 + sum(counts)], refs[2 + sum(counts) :]
    combined, sends = outs[0], outs[1:]
    core = lax.axis_index("mp")
    width = mine.shape[1]
    own_cols = pl.ds(pl.multiple_of(core * width, width), width)
    other_cols = pl.ds(pl.multiple_of((1 - core) * width, width), width)
    for chunk in range(CHUNKS):
        parts = addends[sum(counts[:chunk]) : sum(counts[: chunk + 1])]
        first = core * (rows * CHUNKS) + chunk * rows
        held_rows = slice(chunk * rows, (chunk + 1) * rows)
        for i in range(combined.shape[0]):
            b = start + i
            at = pl.ds(pl.multiple_of(b * BLK + first, rows), rows)
            for cols, held in ((own_cols, mine), (other_cols, other)):
                total = held[at, :].astype(jnp.float32)
                for part, base in zip(parts, bases[chunk]):
                    total = total + part[0, b - base, :, cols].astype(jnp.float32)
                combined[i, held_rows, cols] = total.astype(combined.dtype)
    if sends:
        odd = lax.axis_index("graph") % 2
        even_send, odd_send = sends
        even_send[...] = combined[pl.ds((1 - odd) * border, border)]
        odd_send[...] = combined[pl.ds(odd * border, border)]


def mlp_kernel(border, start, blocks, reverse, valid, combined, *refs):
    came, refs = (refs[:2], refs[2:]) if start == 0 else (None, refs)
    in_own, in_other, out_own, out_other, final_own, final_other, state = refs
    count, share, width = combined.shape
    core = lax.axis_index("mp")
    odd = lax.axis_index("graph") % 2 == 1
    first = core * share
    for i in range(count):
        b = start + i
        within = reverse[b] % blocks
        if came is None:
            pair = combined[within - start]
        else:
            w = jnp.clip(within - (border if b < border else 0), 0, border - 1)
            pair = jnp.where(odd == (b < border), came[0][w], came[1][w])
        state[i * share : (i + 1) * share] = (
            combined[i].astype(jnp.float32) + pair.astype(jnp.float32)
        ) * pair_scale
    for layer in range(MLPS):
        layer_input = state[...].astype(jnp.bfloat16)
        total = state[...]
        for w_in, w_out in ((in_own, out_own), (in_other, out_other)):
            value = jnp.dot(layer_input, w_in[layer], preferred_element_type=jnp.float32)
            hidden = (value / (1.0 + jnp.exp(-value))).astype(jnp.bfloat16)
            total = total + jnp.dot(hidden, w_out[layer], preferred_element_type=jnp.float32)
        state[...] = total
    half = width // 2
    own_cols = pl.ds(pl.multiple_of(core * half, half), half)
    other_cols = pl.ds(pl.multiple_of((1 - core) * half, half), half)
    row = lax.broadcasted_iota(jnp.int32, (share, half), 0) + first
    limit = valid[0]
    for i in range(count):
        keep = row + (start + i) * BLK < limit
        at = slice(i * share, (i + 1) * share)
        final_own[i] = jnp.where(keep, state[at, own_cols], 0.0).astype(final_own.dtype)
        final_other[i] = jnp.where(keep, state[at, other_cols], 0.0).astype(final_other.dtype)


def join_kernel(starts, *refs):
    parts = len(starts)
    own, came, out = refs[:parts], refs[parts : 2 * parts], refs[2 * parts]
    core = lax.axis_index("mp")
    for i, start in enumerate(starts):
        count, share, _ = own[i].shape
        for b in range(count):
            here = (start + b) * BLK + core * share
            there = (start + b) * BLK + (1 - core) * share
            out[pl.ds(pl.multiple_of(here, share), share), :] = own[i][b]
            out[pl.ds(pl.multiple_of(there, share), share), :] = came[i][b]


def local(
    messages,
    basis_blocks,
    source_block,
    target_owner,
    target_block,
    row_counts,
    reverse_block,
    valid_edges,
    weight_in,
    weight_out,
):
    devices = lax.axis_size("graph")
    edge_rows, part_width = messages.shape
    width = part_width * lax.axis_size("mp")
    blocks = edge_rows // BLK
    slots = source_block.shape[0]
    capacity = max(2, (slots + devices - 1) // devices + 1)
    border = blocks // 4
    near, far = split_bits(devices)
    groups = 1 << len(near)
    owners = devices // groups
    room = min(slots, capacity * owners)
    room = -(-room // UNROLL) * UNROLL
    rows = BLK // lax.axis_size("mp") // CHUNKS
    bf16 = jnp.bfloat16

    def near_send(array, k):
        return lax.ppermute(array, "graph", xor_pairs(devices, near_mask(near, k)))

    def far_send(array, bit):
        return lax.ppermute(array, "graph", xor_pairs(devices, 1 << bit))

    def swap(array):
        return lax.ppermute(array, "mp", [(0, 1), (1, 0)])

    mine = [messages, near_send(messages, 1), near_send(messages, 2)]
    other = [swap(messages)]
    in_other, out_other = swap(weight_in), swap(weight_out)

    share = rows * CHUNKS
    whole_shape = jax.ShapeDtypeStruct((room + 1, share, BLK), bf16)
    cut_shapes = [
        jax.ShapeDtypeStruct((room + (j == 0), rows, BLK), bf16) for j in range(CHUNKS)
    ]
    packed = pl.pallas_call(
        functools.partial(pack_kernel, near, far, room, rows, blocks),
        out_shape=[whole_shape] * (groups - 1) + cut_shapes,
        in_specs=[smem()] * 4 + [full(None)],
        out_specs=[full(None)] * (groups - 1 + CHUNKS),
        scratch_shapes=[pltpu.SMEM((groups * room,), jnp.int32), pltpu.SMEM((groups,), jnp.int32)],
        compiler_params=grant(),
        cost_estimate=spent(6),
        name="pack",
    )(
        target_owner[:, 0],
        source_block,
        target_block,
        row_counts,
        after_all(basis_blocks, other[0], in_other, out_other),
    )
    last = groups - 1
    middle = edge_rows // 2
    basis = [packed[0]]
    for k in range(1, last):
        basis.append(near_send(after_all(packed[k], *mine[1:]), k))
    ready = [after_all(array, packed[0]) for array in mine[1:]]
    onward = [near_send(ready[0][:middle], 2), near_send(ready[1][middle:], 1)]
    mine.append(jnp.concatenate(onward, axis=0))
    other.extend(swap(after_all(array, *basis[1:])) for array in mine[1:])
    acc_shape = (owners * blocks, rows, width)
    acc_bytes = owners * blocks * rows * width * 4
    partial = pl.pallas_call(
        functools.partial(first_kernel, last, room),
        out_shape=jax.ShapeDtypeStruct((owners * blocks, share, width), jnp.float32),
        in_specs=[full(None)] * (3 * last),
        out_specs=full(None),
        scratch_shapes=[
            pltpu.VMEM((last, 16, BLK), jnp.int32),
            pltpu.SMEM((last, 16, BLK), jnp.int32),
            pltpu.SemaphoreType.DMA,
        ],
        compiler_params=grant(CHUNKS * acc_bytes),
        cost_estimate=spent(4),
        name="first_products",
    )(*basis[:last], *mine[:last], *other[:last])

    part_owners_shape = jax.ShapeDtypeStruct((owners // 4, blocks, rows, width), bf16)
    border_shape = jax.ShapeDtypeStruct((border, share, width), bf16)
    even_pairs = [(i, i ^ 1) for i in range(devices)]
    odd_pairs = [(i, (i + 1 if i % 2 else i - 1) % devices) for i in range(devices)]
    cut, waited, came_first = [], basis[1:], None
    sums, lows, highs = [], [], []
    for chunk in range(CHUNKS):
        cut.append(near_send(after_all(packed[last + chunk], *waited), last))
        waits = [] if came_first is None else [came_first]
        keep_low, keep_high, send_low, send_high = pl.pallas_call(
            functools.partial(last_kernel, room, blocks, rows, chunk),
            out_shape=[part_owners_shape] * 4,
            in_specs=[full(None)] * 5,
            out_specs=[full(None)] * 4,
            scratch_shapes=[
                pltpu.VMEM(acc_shape, jnp.float32),
                pltpu.VMEM((1, 16, BLK), jnp.int32),
                pltpu.SMEM((1, 16, BLK), jnp.int32),
                pltpu.SemaphoreType.DMA,
            ],
            compiler_params=grant(4 * acc_bytes),
            cost_estimate=spent(2),
            name="last_products",
        )(cut[0], after_all(cut[chunk], *waits), mine[last], other[last], partial)
        waited = [keep_low]
        came = far_send(send_high, far[0])
        came_first = (keep_high.astype(jnp.float32) + came.astype(jnp.float32)).astype(bf16)
        sums.append(came_first)
        highs.append(came)
        lows.append((keep_low, send_low))
    lows = [
        (keep_low, far_send(after_all(send_low, came), far[0]))
        for (keep_low, send_low), came in zip(lows, highs)
    ]
    starts = [0, 2 * border]
    stops = [2 * border, blocks]
    arrived = []
    for chunk in range(CHUNKS):
        pieces = [(0, blocks)] if chunk < CHUNKS - 1 else list(zip(starts, stops))
        found = []
        for start, stop in pieces:
            send, addends, bases = sums[chunk][:, start:stop], list(lows[chunk]), [0, 0]
            size = owners // 4
            for index, bit in enumerate(far[1:]):
                addends.append(far_send(send, bit))
                bases.append(start)
                if index + 2 < len(far):
                    size = size // 2
                    send = sum(
                        part[size : 2 * size, start - base : stop - base].astype(jnp.float32)
                        for part, base in zip(addends, bases)
                    ).astype(bf16)
            found.append((addends, tuple(bases)))
        arrived.append(found if len(found) > 1 else found * 2)
    finals, came = [], []
    for index, (start, stop) in enumerate(zip(starts, stops)):
        addends = [array for found in arrived for array in found[index][0]]
        bases = tuple(found[index][1] for found in arrived)
        piece_shape = jax.ShapeDtypeStruct((stop - start, share, width), bf16)
        part_shape = jax.ShapeDtypeStruct((stop - start, share, part_width), bf16)
        outs = pl.pallas_call(
            functools.partial(combine_kernel, rows, border, start, bases),
            out_shape=[piece_shape] + [border_shape] * (2 if start == 0 else 0),
            in_specs=[full(None)] * (2 + len(addends)),
            out_specs=[full(None)] * (3 if start == 0 else 1),
            compiler_params=grant(acc_bytes),
            cost_estimate=spent(0.5),
            name="combine",
        )(mine[0], other[0], *addends)
        if start == 0:
            came = [
                lax.ppermute(outs[2], "graph", odd_pairs),
                lax.ppermute(outs[1], "graph", even_pairs),
            ][::-1]
        operands = [outs[0]] + (came if start == 0 else [])
        own, theirs = pl.pallas_call(
            functools.partial(mlp_kernel, border, start, blocks),
            out_shape=[part_shape] * 2,
            in_specs=[smem()] * 2 + [full(None)] * (4 + len(operands)),
            out_specs=[full(None)] * 2,
            scratch_shapes=[pltpu.VMEM(((stop - start) * share, width), jnp.float32)],
            compiler_params=grant(),
            cost_estimate=spent(2),
            name="mlp",
        )(reverse_block, valid_edges, *operands, weight_in, in_other, weight_out, out_other)
        finals.append((own, swap(theirs)))

    return pl.pallas_call(
        functools.partial(join_kernel, starts),
        out_shape=jax.ShapeDtypeStruct(messages.shape, bf16),
        in_specs=[full(None)] * (2 * len(finals)),
        out_specs=full(None),
        compiler_params=grant(),
        cost_estimate=spent(1),
        name="join",
    )(*[own for own, _ in finals], *[theirs for _, theirs in finals])


def solution(mesh):
    in_specs = (
        P("graph", "mp"),
        P("graph", None, None),
        P("graph"),
        P("graph", None),
        P("graph"),
        P("graph"),
        P("graph"),
        P("graph"),
        P(None, None, "mp"),
        P(None, "mp", None),
    )
    out_specs = P("graph", "mp")
    return jax.shard_map(local, mesh=mesh, in_specs=in_specs, out_specs=out_specs, check_vma=False)
```

time: 101 us -> 95.8 us (0.949)
  starting transfers between devices: 35.5 us -> 28.7 us
  waiting for transfers between devices: 40.4 us -> 44.6 us
  Pallas kernels: 18.1 us -> 16.7 us
  local copies, waits for them, and re-layouts: 5.78 us -> 4.62 us
    ppermute x6 -> x7, waiting for transfers between devices: 13.6 us -> 19.5 us  [far_send(): return lax.ppermute(array, 'graph', xor_pairs(devices, 1 << bit))]
    ppermute x4 -> x2, starting transfers between devices: 10.3 us -> 5.46 us  [the longest x1 4.6 us: local(): lax.ppermute(outs[2], 'graph', odd_pairs)]
    ppermute x6 -> x7, starting transfers between devices: 11.6 us -> 9.5 us  [far_send(): return lax.ppermute(array, 'graph', xor_pairs(devices, 1 << bit))]
    ppermute x7 -> x8, waiting for transfers between devices: 23.7 us -> 22.1 us  [near_send(): return lax.ppermute(array, 'graph', xor_pairs(devices, near_mask(near, k)))]
    pallas_call x8, Pallas kernels: 14.5 us -> 13.1 us  [the longest x2 4.37 us: local(): pl.pallas_call(functools.partial(mlp_kernel, border, start, blocks), out_...]
    unnamed x24 -> x19, local copies, waits for them, and re-layouts: 5.64 us -> 4.54 us
    ppermute x7 -> x8, starting transfers between devices: 11.4 us -> 12 us  [near_send(): return lax.ppermute(array, 'graph', xor_pairs(devices, near_mask(near, k)))]
    ppermute x11 -> x8, waiting for transfers between devices: 2.58 us -> 2.03 us  [swap(): return lax.ppermute(array, 'mp', [(0, 1), (1, 0)])]
  transfers between devices with their start and end apart: 28 -> 25, of which waited for: 11 -> 12; matrix products, arithmetic and copies ran while one was open for 0% -> 0% of each run, Pallas kernels for 14% -> 13%
where the time goes in v3:
time: 95.8 us; the launch traced here: 95.7 us
  waiting for transfers between devices  44.6 us (47%)
  starting transfers between devices  28.7 us (30%)
  Pallas kernels  16.7 us (17%)
  local copies, waits for them, and re-layouts  4.62 us (5%)
    ppermute x8, waiting for transfers between devices, near_send(): return lax.ppermute(array, 'graph', xor_pairs(devices, near_mask(near, k)))  22.1 us
    ppermute x7, waiting for transfers between devices, far_send(): return lax.ppermute(array, 'graph', xor_pairs(devices, 1 << bit))  19.5 us
    ppermute x8, starting transfers between devices, near_send(): return lax.ppermute(array, 'graph', xor_pairs(devices, near_mask(near, k)))  12 us
    ppermute x7, starting transfers between devices, far_send(): return lax.ppermute(array, 'graph', xor_pairs(devices, 1 << bit))  9.5 us
    ppermute x1, starting transfers between devices, local(): lax.ppermute(outs[2], 'graph', odd_pairs)  4.6 us
    unnamed x19, local copies, waits for them, and re-layouts  4.54 us
    pallas_call x2, Pallas kernels, local(): pl.pallas_call(functools.partial(mlp_kernel, border, start, blocks), out_...  4.37 us
    pallas_call x2, Pallas kernels, local(): pl.pallas_call(functools.partial(last_kernel, room, blocks, rows, chunk),...  3.89 us
  transfers between devices with their start and end apart: 25, of which 12 were waited for; matrix products, arithmetic and copies ran while one was open for 0% of the time, Pallas kernels for 13%

profile of v3, /device:TPU:0, one launch (start us, length us, event | category | flops | bytes accessed | tf_op | source)
XLA Modules:
  0.0 95.7 jit_solution(14419800788341760515)
XLA Ops:
  1.0 2.5 %collective-permute-start.3 = (bf16[1024,256]{1,0:T(8,128)(2,1)}, bf16[1024,256]{1,0:T(8,128)(2,1)S(1)}, u32[]{:S(2)}, u32[]{:S(2)}) collective-permute-start(bf16[1024,256]{1,0:T(8,128)(2,1)} %refs_0_.4), channel_id=1, source_target_pairs={{0,2},{2,0},{4,6},{6,4},{8,10},{10,8},{12,14},{14,12},{16,18},{18,... | collective-permute-start | bytes 1572872 | tf_op jit(solution)/shard_map/ppermute | solution.py:278
  3.5 1.6 %collective-permute-start.4 = (bf16[1024,256]{1,0:T(8,128)(2,1)}, bf16[1024,256]{1,0:T(8,128)(2,1)S(1)}, u32[]{:S(2)}, u32[]{:S(2)}) collective-permute-start(bf16[1024,256]{1,0:T(8,128)(2,1)} %refs_0_.4), channel_id=1, source_target_pairs={{0,8},{2,10},{4,12},{6,14},{8,0},{10,2},{12,4},{14,6},{16,24},{18,... | collective-permute-start | bytes 1572872 | tf_op jit(solution)/shard_map/ppermute | solution.py:278
  5.1 1.9 %copy-done.1 = bf16[96,128,128]{2,1,0:T(8,128)(2,1)S(1)} copy-done((bf16[96,128,128]{2,1,0:T(8,128)(2,1)S(1)}, bf16[96,128,128]{2,1,0:T(8,128)(2,1)}, u32[]{:S(2)}) %copy-start.1) | copy-done | bytes 3145752
  9.6 3.6 %pack.1 = (bf16[29,64,128]{2,1,0:T(8,128)(2,1)S(1)}, bf16[29,64,128]{2,1,0:T(8,128)(2,1)S(1)}, bf16[29,64,128]{2,1,0:T(8,128)(2,1)S(1)}, bf16[29,32,128]{2,1,0:T(8,128)(2,1)S(1)}, bf16[28,32,128]{2,1,0:T(8,128)(2,1)S(1)}) custom-call(s32[96]{0:T(128)S(1)} %bitcast.1, s32[96]{0:T(128)S(1)} %copy-done.6, s32[96]{0:T(128)S(1)} %copy-done.7, s32[96]{0:T(128)S(1)} %copy-done.8, ...), custom_call_target="tpu_custom_call" | custom-call | bytes 22140000 | tf_op jit(solution)/shard_map/pack/pallas_call | solution.py:295
  13.2 3.0 %collective-permute-done.3.refs_4_ = bf16[1024,256]{1,0:T(8,128)(2,1)S(1)} collective-permute-done((bf16[1024,256]{1,0:T(8,128)(2,1)}, bf16[1024,256]{1,0:T(8,128)(2,1)S(1)}, u32[]{:S(2)}, u32[]{:S(2)}) %collective-permute-start.3) | collective-permute-done | bytes 524320 | tf_op jit(solution)/shard_map/ppermute | solution.py:278
  16.3 1.9 %collective-permute-start.8 = (bf16[512,256]{1,0:T(8,128)(2,1)S(1)}, bf16[512,256]{1,0:T(8,128)(2,1)S(1)}, u32[]{:S(2)}, u32[]{:S(2)}) collective-permute-start(bf16[512,256]{1,0:T(8,128)(2,1)S(1)} %slice.12), channel_id=1, source_target_pairs={{0,8},{2,10},{4,12},{6,14},{8,0},{10,2},{12,4},{14,6},{16,24},{18,... | collective-permute-start | bytes 786440 | tf_op jit(solution)/shard_map/ppermute | solution.py:278
  18.2 1.5 %collective-permute-start.5 = (bf16[29,64,128]{2,1,0:T(8,128)(2,1)S(1)}, bf16[29,64,128]{2,1,0:T(8,128)(2,1)S(1)}, u32[]{:S(2)}, u32[]{:S(2)}) collective-permute-start(bf16[29,64,128]{2,1,0:T(8,128)(2,1)S(1)} %get-tuple-element.41), channel_id=1, source_target_pairs={{0,2},{2,0},{4,6},{6,4},{8,10},{10,8},{12,14},{14,12},{16,18},{18,... | collective-permute-start | bytes 1425416 | tf_op jit(solution)/shard_map/ppermute | solution.py:278
  20.1 1.3 %collective-permute-start.9 = (bf16[512,256]{1,0:T(8,128)(2,1)S(1)}, bf16[512,256]{1,0:T(8,128)(2,1)S(1)}, u32[]{:S(2)}, u32[]{:S(2)}) collective-permute-start(bf16[512,256]{1,0:T(8,128)(2,1)S(1)} %slice.13), channel_id=1, source_target_pairs={{0,2},{2,0},{4,6},{6,4},{8,10},{10,8},{12,14},{14,12},{16,18},{18,... | collective-permute-start | bytes 786440 | tf_op jit(solution)/shard_map/ppermute | solution.py:278
  21.4 4.1 %collective-permute-done.8 = bf16[512,256]{1,0:T(8,128)(2,1)S(1)} collective-permute-done((bf16[512,256]{1,0:T(8,128)(2,1)S(1)}, bf16[512,256]{1,0:T(8,128)(2,1)S(1)}, u32[]{:S(2)}, u32[]{:S(2)}) %collective-permute-start.8) | collective-permute-done | bytes 262176 | tf_op jit(solution)/shard_map/ppermute | solution.py:278
  25.6 10.4 %collective-permute-done.9 = bf16[512,256]{1,0:T(8,128)(2,1)S(1)} collective-permute-done((bf16[512,256]{1,0:T(8,128)(2,1)S(1)}, bf16[512,256]{1,0:T(8,128)(2,1)S(1)}, u32[]{:S(2)}, u32[]{:S(2)}) %collective-permute-start.9) | collective-permute-done | bytes 262176 | tf_op jit(solution)/shard_map/ppermute | solution.py:278
  36.7 1.4 %collective-permute-start.7 = (bf16[29,32,128]{2,1,0:T(8,128)(2,1)S(1)}, bf16[29,32,128]{2,1,0:T(8,128)(2,1)S(1)}, u32[]{:S(2)}, u32[]{:S(2)}) collective-permute-start(bf16[29,32,128]{2,1,0:T(8,128)(2,1)S(1)} %get-tuple-element.44), channel_id=1, source_target_pairs={{0,10},{2,8},{4,14},{6,12},{8,2},{10,0},{12,6},{14,4},{16,26},{18,... | collective-permute-start | bytes 712712 | tf_op jit(solution)/shard_map/ppermute | solution.py:278
  38.7 3.8 %first_products.1.before = f32[32,64,512]{2,1,0:T(8,128)S(1)} custom-call(bf16[29,64,128]{2,1,0:T(8,128)(2,1)S(1)} %get-tuple-element.45.refs_0_, bf16[29,64,128]{2,1,0:T(8,128)(2,1)S(1)} %collective-permute-done.5.refs_1_, bf16[29,64,128]{2,1,0:T(8,128)(2,1)S(1)} %collective-permute-done.6.refs_2_, bf16[1024,256]{1,0:T(8,128)(2,1)S(1)} %copy-done, ...), custom_call_target="tpu_custom_call" | custom-call | bytes 14760000 | tf_op jit(solution)/shard_map/first_products/pallas_call | solution.py:322
  42.5 3.2 %collective-permute-done.7.labels.basis = bf16[29,32,128]{2,1,0:T(8,128)(2,1)S(1)} collective-permute-done((bf16[29,32,128]{2,1,0:T(8,128)(2,1)S(1)}, bf16[29,32,128]{2,1,0:T(8,128)(2,1)S(1)}, u32[]{:S(2)}, u32[]{:S(2)}) %collective-permute-start.7) | collective-permute-done | bytes 237600 | tf_op jit(solution)/shard_map/ppermute | solution.py:278
  45.7 2.0 %last_products.2 = (bf16[1,8,32,512]{3,2,1,0:T(8,128)(2,1)S(1)}, bf16[1,8,32,512]{3,2,1,0:T(8,128)(2,1)S(1)}, bf16[1,8,32,512]{3,2,1,0:T(8,128)(2,1)S(1)}, bf16[1,8,32,512]{3,2,1,0:T(8,128)(2,1)S(1)}) custom-call(bf16[29,32,128]{2,1,0:T(8,128)(2,1)S(1)} %collective-permute-done.7.labels.basis, bf16[29,32,128]{2,1,0:T(8,128)(2,1)S(1)} %collective-permute-done.7.labels.basis, ...), custom_call_target="tpu_custom_call" | custom-call | bytes 7380000 | tf_op jit(solution)/shard_map/last_products/pallas_call | solution.py:346
  47.6 1.6 %collective-permute-start.13 = (bf16[1,8,32,512]{3,2,1,0:T(8,128)(2,1)S(1)}, bf16[1,8,32,512]{3,2,1,0:T(8,128)(2,1)S(1)}, u32[]{:S(2)}, u32[]{:S(2)}) collective-permute-start(bf16[1,8,32,512]{3,2,1,0:T(8,128)(2,1)S(1)} %get-tuple-element.53), channel_id=1, source_target_pairs={{0,4},{2,6},{4,0},{6,2},{8,12},{10,14},{12,8},{14,10},{16,20},{18,... | collective-permute-start | bytes 786440 | tf_op jit(solution)/shard_map/ppermute | solution.py:281
  49.2 1.4 %collective-permute-start.16 = (bf16[28,32,128]{2,1,0:T(8,128)(2,1)S(1)}, bf16[28,32,128]{2,1,0:T(8,128)(2,1)S(1)}, u32[]{:S(2)}, u32[]{:S(2)}) collective-permute-start(bf16[28,32,128]{2,1,0:T(8,128)(2,1)S(1)} %get-tuple-element.57), channel_id=1, source_target_pairs={{0,10},{2,8},{4,14},{6,12},{8,2},{10,0},{12,6},{14,4},{16,26},{18,... | collective-permute-start | bytes 688136 | tf_op jit(solution)/shard_map/ppermute | solution.py:278
  50.6 5.0 %collective-permute-done.13 = bf16[1,8,32,512]{3,2,1,0:T(8,128)(2,1)S(1)} collective-permute-done((bf16[1,8,32,512]{3,2,1,0:T(8,128)(2,1)S(1)}, bf16[1,8,32,512]{3,2,1,0:T(8,128)(2,1)S(1)}, u32[]{:S(2)}, u32[]{:S(2)}) %collective-permute-start.13) | collective-permute-done | bytes 262176 | tf_op jit(solution)/shard_map/ppermute | solution.py:281
  55.6 1.4 %collective-permute-done.16.basis = bf16[28,32,128]{2,1,0:T(8,128)(2,1)S(1)} collective-permute-done((bf16[28,32,128]{2,1,0:T(8,128)(2,1)S(1)}, bf16[28,32,128]{2,1,0:T(8,128)(2,1)S(1)}, u32[]{:S(2)}, u32[]{:S(2)}) %collective-permute-start.16) | collective-permute-done | bytes 229408 | tf_op jit(solution)/shard_map/ppermute | solution.py:278
  57.0 1.9 %last_products.3 = (bf16[1,8,32,512]{3,2,1,0:T(8,128)(2,1)S(1)}, bf16[1,8,32,512]{3,2,1,0:T(8,128)(2,1)S(1)}, bf16[1,8,32,512]{3,2,1,0:T(8,128)(2,1)S(1)}, bf16[1,8,32,512]{3,2,1,0:T(8,128)(2,1)S(1)}) custom-call(bf16[29,32,128]{2,1,0:T(8,128)(2,1)S(1)} %collective-permute-done.7.labels.basis, bf16[28,32,128]{2,1,0:T(8,128)(2,1)S(1)} %collective-permute-done.16.basis, ...), custom_call_target="tpu_custom_call" | custom-call | bytes 7380000 | tf_op jit(solution)/shard_map/last_products/pallas_call | solution.py:346
  59.6 2.6 %collective-permute-start.15 = (bf16[1,8,32,512]{3,2,1,0:T(8,128)(2,1)S(1)}, bf16[1,8,32,512]{3,2,1,0:T(8,128)(2,1)S(1)}, u32[]{:S(2)}, u32[]{:S(2)}) collective-permute-start(bf16[1,8,32,512]{3,2,1,0:T(8,128)(2,1)S(1)} %add_convert_fusion.1), channel_id=1, source_target_pairs={{0,16},{2,18},{4,20},{6,22},{8,24},{10,26},{12,28},{14,30},{16,0},... | collective-permute-start | bytes 786440 | tf_op jit(solution)/shard_map/ppermute | solution.py:281
  62.2 1.5 %collective-permute-start.14 = (bf16[1,8,32,512]{3,2,1,0:T(8,128)(2,1)S(1)}, bf16[1,8,32,512]{3,2,1,0:T(8,128)(2,1)S(1)}, u32[]{:S(2)}, u32[]{:S(2)}) collective-permute-start(bf16[1,8,32,512]{3,2,1,0:T(8,128)(2,1)S(1)} %get-tuple-element.54), channel_id=1, source_target_pairs={{0,4},{2,6},{4,0},{6,2},{8,12},{10,14},{12,8},{14,10},{16,20},{18,... | collective-permute-start | bytes 786440 | tf_op jit(solution)/shard_map/ppermute | solution.py:281
  63.7 4.6 %collective-permute-done.17 = bf16[1,8,32,512]{3,2,1,0:T(8,128)(2,1)S(1)} collective-permute-done((bf16[1,8,32,512]{3,2,1,0:T(8,128)(2,1)S(1)}, bf16[1,8,32,512]{3,2,1,0:T(8,128)(2,1)S(1)}, u32[]{:S(2)}, u32[]{:S(2)}) %collective-permute-start.17) | collective-permute-done | bytes 262176 | tf_op jit(solution)/shard_map/ppermute | solution.py:281
  68.4 3.2 %collective-permute-start.19 = (bf16[1,4,32,512]{3,2,1,0:T(8,128)(2,1)S(1)}, bf16[1,4,32,512]{3,2,1,0:T(8,128)(2,1)S(1)}, u32[]{:S(2)}, u32[]{:S(2)}) collective-permute-start(bf16[1,4,32,512]{3,2,1,0:T(8,128)(2,1)S(1)} %get-tuple-element.72), channel_id=1, source_target_pairs={{0,16},{2,18},{4,20},{6,22},{8,24},{10,26},{12,28},{14,30},{16,0},... | collective-permute-start | bytes 393224 | tf_op jit(solution)/shard_map/ppermute | solution.py:281
  71.7 7.1 %collective-permute-done.15.refs_4_ = bf16[1,8,32,512]{3,2,1,0:T(8,128)(2,1)S(1)} collective-permute-done((bf16[1,8,32,512]{3,2,1,0:T(8,128)(2,1)S(1)}, bf16[1,8,32,512]{3,2,1,0:T(8,128)(2,1)S(1)}, u32[]{:S(2)}, u32[]{:S(2)}) %collective-permute-start.15) | collective-permute-done | bytes 262176 | tf_op jit(solution)/shard_map/ppermute | solution.py:281
  78.8 2.8 %collective-permute-done.19.refs_7_ = bf16[1,4,32,512]{3,2,1,0:T(8,128)(2,1)S(1)} collective-permute-done((bf16[1,4,32,512]{3,2,1,0:T(8,128)(2,1)S(1)}, bf16[1,4,32,512]{3,2,1,0:T(8,128)(2,1)S(1)}, u32[]{:S(2)}, u32[]{:S(2)}) %collective-permute-start.19) | collective-permute-done | bytes 131104 | tf_op jit(solution)/shard_map/ppermute | solution.py:281
  81.7 0.9 collective-permute-start.20
  82.6 4.6 %collective-permute-start.21 = (bf16[2,64,512]{2,1,0:T(8,128)(2,1)S(1)}, bf16[2,64,512]{2,1,0:T(8,128)(2,1)S(1)}, u32[]{:S(2)}, u32[]{:S(2)}) collective-permute-start(bf16[2,64,512]{2,1,0:T(8,128)(2,1)S(1)} %get-tuple-element.66), channel_id=1, source_target_pairs={{0,30},{2,4},{4,2},{6,8},{8,6},{10,12},{12,10},{14,16},{16,14},{18... | collective-permute-start | bytes 393224 | tf_op jit(solution)/shard_map/ppermute | solution.py:408
  88.0 2.2 %mlp.3 = (bf16[4,64,256]{2,1,0:T(8,128)(2,1)S(1)}, bf16[4,64,256]{2,1,0:T(8,128)(2,1)S(1)}) custom-call(s32[8]{0:T(128)S(1)} %copy-done.4, s32[1]{0:T(128)S(6)} %copy.12.valid, bf16[4,64,512]{2,1,0:T(8,128)(2,1)S(1)} %combine.3.combined, bf16[3,512,256]{2,1,0:T(8,128)(2,1)S(1)} %copy-done.2, bf16[3,512,256]{2,1,0:T(8,128)(2,1)S(1)} %collective-permute-done.1.refs_3_.refs_1_, ...), custom_call_target="tpu_custom_call" | custom-call | bytes 7380000 | tf_op jit(solution)/shard_map/mlp/pallas_call | solution.py:412
  90.3 0.9 collective-permute-done.21.refs_1_
  91.2 2.2 %mlp.2 = (bf16[4,64,256]{2,1,0:T(8,128)(2,1)S(1)}, bf16[4,64,256]{2,1,0:T(8,128)(2,1)S(1)}) custom-call(s32[8]{0:T(128)S(1)} %copy-done.4, s32[1]{0:T(128)S(6)} %copy.12.valid, bf16[4,64,512]{2,1,0:T(8,128)(2,1)S(1)} %get-tuple-element.64.combined, bf16[2,64,512]{2,1,0:T(8,128)(2,1)S(1)} %collective-permute-done.20.refs_0_, ...), custom_call_target="tpu_custom_call" | custom-call | bytes 7380000 | tf_op jit(solution)/shard_map/mlp/pallas_call | solution.py:412
  93.5 1.3 %collective-permute-done.23.refs_2_ = bf16[4,64,256]{2,1,0:T(8,128)(2,1)S(1)} collective-permute-done((bf16[4,64,256]{2,1,0:T(8,128)(2,1)S(1)}, bf16[4,64,256]{2,1,0:T(8,128)(2,1)S(1)}, u32[]{:S(2)}, u32[]{:S(2)}) %collective-permute-start.23) | collective-permute-done | bytes 131104 | tf_op jit(solution)/shard_map/ppermute | solution.py:284
  94.8 0.8 join.1
  (52 shorter events, 6.7 us)
Async XLA Ops:
  0.0 38.7 %copy-start = (bf16[1024,256]{1,0:T(8,128)(2,1)S(1)}, bf16[1024,256]{1,0:T(8,128)(2,1)}, u32[]{:S(2)}) copy-start(bf16[1024,256]{1,0:T(8,128)(2,1)} %refs_0_.4) | copy-start | bytes 1572868
  0.0 5.1 %collective-permute-start.1 = (bf16[3,512,256]{2,1,0:T(8,128)(2,1)}, bf16[3,512,256]{2,1,0:T(8,128)(2,1)S(1)}, u32[]{:S(2)}, u32[]{:S(2)}) collective-permute-start(bf16[3,512,256]{2,1,0:T(8,128)(2,1)} %refs_0_.5), channel_id=1, source_target_pairs={{0,1},{1,0},{2,3},{3,2},{4,5},{5,4},{6,7},{7,6},{8,9},{9,8},{10,11... | collective-permute-start | bytes 2359304 | tf_op jit(solution)/shard_map/ppermute | solution.py:284
  0.5 4.6 %collective-permute-start.2 = (bf16[3,256,512]{2,1,0:T(8,128)(2,1)}, bf16[3,256,512]{2,1,0:T(8,128)(2,1)S(1)}, u32[]{:S(2)}, u32[]{:S(2)}) collective-permute-start(bf16[3,256,512]{2,1,0:T(8,128)(2,1)} %refs_2_.3), channel_id=1, source_target_pairs={{0,1},{1,0},{2,3},{3,2},{4,5},{5,4},{6,7},{7,6},{8,9},{9,8},{10,11... | collective-permute-start | bytes 2359304 | tf_op jit(solution)/shard_map/ppermute | solution.py:284
  0.5 4.6 %collective-permute-start = (bf16[1024,256]{1,0:T(8,128)(2,1)}, bf16[1024,256]{1,0:T(8,128)(2,1)S(1)}, u32[]{:S(2)}, u32[]{:S(2)}) collective-permute-start(bf16[1024,256]{1,0:T(8,128)(2,1)} %refs_0_.4), channel_id=1, source_target_pairs={{0,1},{1,0},{2,3},{3,2},{4,5},{5,4},{6,7},{7,6},{8,9},{9,8},{10,11... | collective-permute-start | bytes 1572872 | tf_op jit(solution)/shard_map/ppermute | solution.py:284
  1.0 15.3 %collective-permute-start.3 = (bf16[1024,256]{1,0:T(8,128)(2,1)}, bf16[1024,256]{1,0:T(8,128)(2,1)S(1)}, u32[]{:S(2)}, u32[]{:S(2)}) collective-permute-start(bf16[1024,256]{1,0:T(8,128)(2,1)} %refs_0_.4), channel_id=1, source_target_pairs={{0,2},{2,0},{4,6},{6,4},{8,10},{10,8},{12,14},{14,12},{16,18},{18,... | collective-permute-start | bytes 1572872 | tf_op jit(solution)/shard_map/ppermute | solution.py:278
  3.5 14.7 %collective-permute-start.4 = (bf16[1024,256]{1,0:T(8,128)(2,1)}, bf16[1024,256]{1,0:T(8,128)(2,1)S(1)}, u32[]{:S(2)}, u32[]{:S(2)}) collective-permute-start(bf16[1024,256]{1,0:T(8,128)(2,1)} %refs_0_.4), channel_id=1, source_target_pairs={{0,8},{2,10},{4,12},{6,14},{8,0},{10,2},{12,4},{14,6},{16,24},{18,... | collective-permute-start | bytes 1572872 | tf_op jit(solution)/shard_map/ppermute | solution.py:278
  5.1 1.9 %copy-start.1 = (bf16[96,128,128]{2,1,0:T(8,128)(2,1)S(1)}, bf16[96,128,128]{2,1,0:T(8,128)(2,1)}, u32[]{:S(2)}) copy-start(bf16[96,128,128]{2,1,0:T(8,128)(2,1)} %basis) | copy-start | bytes 9437188
  7.0 0.7 copy-start.5
  9.0 0.7 copy-start.8
  16.3 9.3 %collective-permute-start.8 = (bf16[512,256]{1,0:T(8,128)(2,1)S(1)}, bf16[512,256]{1,0:T(8,128)(2,1)S(1)}, u32[]{:S(2)}, u32[]{:S(2)}) collective-permute-start(bf16[512,256]{1,0:T(8,128)(2,1)S(1)} %slice.12), channel_id=1, source_target_pairs={{0,8},{2,10},{4,12},{6,14},{8,0},{10,2},{12,4},{14,6},{16,24},{18,... | collective-permute-start | bytes 786440 | tf_op jit(solution)/shard_map/ppermute | solution.py:278
  18.2 17.8 %collective-permute-start.5 = (bf16[29,64,128]{2,1,0:T(8,128)(2,1)S(1)}, bf16[29,64,128]{2,1,0:T(8,128)(2,1)S(1)}, u32[]{:S(2)}, u32[]{:S(2)}) collective-permute-start(bf16[29,64,128]{2,1,0:T(8,128)(2,1)S(1)} %get-tuple-element.41), channel_id=1, source_target_pairs={{0,2},{2,0},{4,6},{6,4},{8,10},{10,8},{12,14},{14,12},{16,18},{18,... | collective-permute-start | bytes 1425416 | tf_op jit(solution)/shard_map/ppermute | solution.py:278
  19.7 16.3 %collective-permute-start.6 = (bf16[29,64,128]{2,1,0:T(8,128)(2,1)S(1)}, bf16[29,64,128]{2,1,0:T(8,128)(2,1)S(1)}, u32[]{:S(2)}, u32[]{:S(2)}) collective-permute-start(bf16[29,64,128]{2,1,0:T(8,128)(2,1)S(1)} %get-tuple-element.43), channel_id=1, source_target_pairs={{0,8},{2,10},{4,12},{6,14},{8,0},{10,2},{12,4},{14,6},{16,24},{18,... | collective-permute-start | bytes 1425416 | tf_op jit(solution)/shard_map/ppermute | solution.py:278
  20.1 15.8 %collective-permute-start.9 = (bf16[512,256]{1,0:T(8,128)(2,1)S(1)}, bf16[512,256]{1,0:T(8,128)(2,1)S(1)}, u32[]{:S(2)}, u32[]{:S(2)}) collective-permute-start(bf16[512,256]{1,0:T(8,128)(2,1)S(1)} %slice.13), channel_id=1, source_target_pairs={{0,2},{2,0},{4,6},{6,4},{8,10},{10,8},{12,14},{14,12},{16,18},{18,... | collective-permute-start | bytes 786440 | tf_op jit(solution)/shard_map/ppermute | solution.py:278
  36.0 2.0 %collective-permute-start.12 = (bf16[1024,256]{1,0:T(8,128)(2,1)S(1)}, bf16[1024,256]{1,0:T(8,128)(2,1)S(1)}, u32[]{:S(2)}, u32[]{:S(2)}) collective-permute-start(bf16[1024,256]{1,0:T(8,128)(2,1)S(1)} %collective-permute-done.4.refs_5_), channel_id=1, source_target_pairs={{0,1},{1,0},{2,3},{3,2},{4,5},{5,4},{6,7},{7,6},{8,9},{9,8},{10,11... | collective-permute-start | bytes 1572872 | tf_op jit(solution)/shard_map/ppermute | solution.py:284
  36.1 2.6 %collective-permute-start.11 = (bf16[1024,256]{1,0:T(8,128)(2,1)S(1)}, bf16[1024,256]{1,0:T(8,128)(2,1)S(1)}, u32[]{:S(2)}, u32[]{:S(2)}) collective-permute-start(bf16[1024,256]{1,0:T(8,128)(2,1)S(1)} %collective-permute-done.3.refs_4_), channel_id=1, source_target_pairs={{0,1},{1,0},{2,3},{3,2},{4,5},{5,4},{6,7},{7,6},{8,9},{9,8},{10,11... | collective-permute-start | bytes 1572872 | tf_op jit(solution)/shard_map/ppermute | solution.py:284
  36.6 9.1 %collective-permute-start.10 = (bf16[1024,256]{1,0:T(8,128)(2,1)S(1)}, bf16[1024,256]{1,0:T(8,128)(2,1)S(1)}, u32[]{:S(2)}, u32[]{:S(2)}) collective-permute-start(bf16[1024,256]{1,0:T(8,128)(2,1)S(1)} %constant_dynamic-update-slice_fusion.mine), channel_id=1, source_target_pairs={{0,1},{1,0},{2,3},{3,2},{4,5},{5,4},{6,7},{7,6},{8,9},{9,8},{10,11... | collective-permute-start | bytes 1572872 | tf_op jit(solution)/shard_map/ppermute | solution.py:284
  36.7 9.0 %collective-permute-start.7 = (bf16[29,32,128]{2,1,0:T(8,128)(2,1)S(1)}, bf16[29,32,128]{2,1,0:T(8,128)(2,1)S(1)}, u32[]{:S(2)}, u32[]{:S(2)}) collective-permute-start(bf16[29,32,128]{2,1,0:T(8,128)(2,1)S(1)} %get-tuple-element.44), channel_id=1, source_target_pairs={{0,10},{2,8},{4,14},{6,12},{8,2},{10,0},{12,6},{14,4},{16,26},{18,... | collective-permute-start | bytes 712712 | tf_op jit(solution)/shard_map/ppermute | solution.py:278
  47.6 7.9 %collective-permute-start.13 = (bf16[1,8,32,512]{3,2,1,0:T(8,128)(2,1)S(1)}, bf16[1,8,32,512]{3,2,1,0:T(8,128)(2,1)S(1)}, u32[]{:S(2)}, u32[]{:S(2)}) collective-permute-start(bf16[1,8,32,512]{3,2,1,0:T(8,128)(2,1)S(1)} %get-tuple-element.53), channel_id=1, source_target_pairs={{0,4},{2,6},{4,0},{6,2},{8,12},{10,14},{12,8},{14,10},{16,20},{18,... | collective-permute-start | bytes 786440 | tf_op jit(solution)/shard_map/ppermute | solution.py:281
  49.2 7.8 %collective-permute-start.16 = (bf16[28,32,128]{2,1,0:T(8,128)(2,1)S(1)}, bf16[28,32,128]{2,1,0:T(8,128)(2,1)S(1)}, u32[]{:S(2)}, u32[]{:S(2)}) collective-permute-start(bf16[28,32,128]{2,1,0:T(8,128)(2,1)S(1)} %get-tuple-element.57), channel_id=1, source_target_pairs={{0,10},{2,8},{4,14},{6,12},{8,2},{10,0},{12,6},{14,4},{16,26},{18,... | collective-permute-start | bytes 688136 | tf_op jit(solution)/shard_map/ppermute | solution.py:278
  59.0 29.0 %copy-start.2 = (bf16[3,512,256]{2,1,0:T(8,128)(2,1)S(1)}, bf16[3,512,256]{2,1,0:T(8,128)(2,1)}, u32[]{:S(2)}) copy-start(bf16[3,512,256]{2,1,0:T(8,128)(2,1)} %refs_0_.5) | copy-start | bytes 2359300
  59.0 29.0 %copy-start.3 = (bf16[3,256,512]{2,1,0:T(8,128)(2,1)S(1)}, bf16[3,256,512]{2,1,0:T(8,128)(2,1)}, u32[]{:S(2)}) copy-start(bf16[3,256,512]{2,1,0:T(8,128)(2,1)} %refs_2_.3) | copy-start | bytes 2359300
  59.0 29.0 %copy-start.4 = (s32[8]{0:T(128)S(1)}, s32[8]{0:T(128)}, u32[]{:S(2)}) copy-start(s32[8]{0:T(128)} %reverse.3) | copy-start | bytes 100
  59.0 9.3 %collective-permute-start.17 = (bf16[1,8,32,512]{3,2,1,0:T(8,128)(2,1)S(1)}, bf16[1,8,32,512]{3,2,1,0:T(8,128)(2,1)S(1)}, u32[]{:S(2)}, u32[]{:S(2)}) collective-permute-start(bf16[1,8,32,512]{3,2,1,0:T(8,128)(2,1)S(1)} %get-tuple-element.61), channel_id=1, source_target_pairs={{0,4},{2,6},{4,0},{6,2},{8,12},{10,14},{12,8},{14,10},{16,20},{18,... | collective-permute-start | bytes 786440 | tf_op jit(solution)/shard_map/ppermute | solution.py:281
  59.6 19.2 %collective-permute-start.15 = (bf16[1,8,32,512]{3,2,1,0:T(8,128)(2,1)S(1)}, bf16[1,8,32,512]{3,2,1,0:T(8,128)(2,1)S(1)}, u32[]{:S(2)}, u32[]{:S(2)}) collective-permute-start(bf16[1,8,32,512]{3,2,1,0:T(8,128)(2,1)S(1)} %add_convert_fusion.1), channel_id=1, source_target_pairs={{0,16},{2,18},{4,20},{6,22},{8,24},{10,26},{12,28},{14,30},{16,0},... | collective-permute-start | bytes 786440 | tf_op jit(solution)/shard_map/ppermute | solution.py:281
  62.2 16.6 %collective-permute-start.14 = (bf16[1,8,32,512]{3,2,1,0:T(8,128)(2,1)S(1)}, bf16[1,8,32,512]{3,2,1,0:T(8,128)(2,1)S(1)}, u32[]{:S(2)}, u32[]{:S(2)}) collective-permute-start(bf16[1,8,32,512]{3,2,1,0:T(8,128)(2,1)S(1)} %get-tuple-element.54), channel_id=1, source_target_pairs={{0,4},{2,6},{4,0},{6,2},{8,12},{10,14},{12,8},{14,10},{16,20},{18,... | collective-permute-start | bytes 786440 | tf_op jit(solution)/shard_map/ppermute | solution.py:281
  68.3 13.3 %collective-permute-start.18 = (bf16[1,8,32,512]{3,2,1,0:T(8,128)(2,1)S(1)}, bf16[1,8,32,512]{3,2,1,0:T(8,128)(2,1)S(1)}, u32[]{:S(2)}, u32[]{:S(2)}) collective-permute-start(bf16[1,8,32,512]{3,2,1,0:T(8,128)(2,1)S(1)} %get-tuple-element.62), channel_id=1, source_target_pairs={{0,4},{2,6},{4,0},{6,2},{8,12},{10,14},{12,8},{14,10},{16,20},{18,... | collective-permute-start | bytes 786440 | tf_op jit(solution)/shard_map/ppermute | solution.py:281
  68.4 13.1 %collective-permute-start.19 = (bf16[1,4,32,512]{3,2,1,0:T(8,128)(2,1)S(1)}, bf16[1,4,32,512]{3,2,1,0:T(8,128)(2,1)S(1)}, u32[]{:S(2)}, u32[]{:S(2)}) collective-permute-start(bf16[1,4,32,512]{3,2,1,0:T(8,128)(2,1)S(1)} %get-tuple-element.72), channel_id=1, source_target_pairs={{0,16},{2,18},{4,20},{6,22},{8,24},{10,26},{12,28},{14,30},{16,0},... | collective-permute-start | bytes 393224 | tf_op jit(solution)/shard_map/ppermute | solution.py:281
  71.6 16.3 %collective-permute-start.22 = (bf16[1,4,32,512]{3,2,1,0:T(8,128)(2,1)S(1)}, bf16[1,4,32,512]{3,2,1,0:T(8,128)(2,1)S(1)}, u32[]{:S(2)}, u32[]{:S(2)}) collective-permute-start(bf16[1,4,32,512]{3,2,1,0:T(8,128)(2,1)S(1)} %get-tuple-element.71), channel_id=1, source_target_pairs={{0,16},{2,18},{4,20},{6,22},{8,24},{10,26},{12,28},{14,30},{16,0},... | collective-permute-start | bytes 393224 | tf_op jit(solution)/shard_map/ppermute | solution.py:281
  81.7 8.6 %collective-permute-start.20 = (bf16[2,64,512]{2,1,0:T(8,128)(2,1)S(1)}, bf16[2,64,512]{2,1,0:T(8,128)(2,1)S(1)}, u32[]{:S(2)}, u32[]{:S(2)}) collective-permute-start(bf16[2,64,512]{2,1,0:T(8,128)(2,1)S(1)} %get-tuple-element.65), channel_id=1, source_target_pairs={{0,2},{2,0},{4,6},{6,4},{8,10},{10,8},{12,14},{14,12},{16,18},{18,... | collective-permute-start | bytes 393224 | tf_op jit(solution)/shard_map/ppermute | solution.py:409
  82.6 8.6 %collective-permute-start.21 = (bf16[2,64,512]{2,1,0:T(8,128)(2,1)S(1)}, bf16[2,64,512]{2,1,0:T(8,128)(2,1)S(1)}, u32[]{:S(2)}, u32[]{:S(2)}) collective-permute-start(bf16[2,64,512]{2,1,0:T(8,128)(2,1)S(1)} %get-tuple-element.66), channel_id=1, source_target_pairs={{0,30},{2,4},{4,2},{6,8},{8,6},{10,12},{12,10},{14,16},{16,14},{18... | collective-permute-start | bytes 393224 | tf_op jit(solution)/shard_map/ppermute | solution.py:408
  90.2 3.3 %collective-permute-start.24 = (bf16[4,64,256]{2,1,0:T(8,128)(2,1)S(1)}, bf16[4,64,256]{2,1,0:T(8,128)(2,1)S(1)}, u32[]{:S(2)}, u32[]{:S(2)}) collective-permute-start(bf16[4,64,256]{2,1,0:T(8,128)(2,1)S(1)} %get-tuple-element.70), channel_id=1, source_target_pairs={{0,1},{1,0},{2,3},{3,2},{4,5},{5,4},{6,7},{7,6},{8,9},{9,8},{10,11... | collective-permute-start | bytes 393224 | tf_op jit(solution)/shard_map/ppermute | solution.py:284
  93.4 1.4 %collective-permute-start.23 = (bf16[4,64,256]{2,1,0:T(8,128)(2,1)S(1)}, bf16[4,64,256]{2,1,0:T(8,128)(2,1)S(1)}, u32[]{:S(2)}, u32[]{:S(2)}) collective-permute-start(bf16[4,64,256]{2,1,0:T(8,128)(2,1)S(1)} %get-tuple-element.69), channel_id=1, source_target_pairs={{0,1},{1,0},{2,3},{3,2},{4,5},{5,4},{6,7},{7,6},{8,9},{9,8},{10,11... | collective-permute-start | bytes 393224 | tf_op jit(solution)/shard_map/ppermute | solution.py:284
  (2 other events, 1.3 us)

commit v4 on v3

--- a/solution.py
+++ b/solution.py
@@ -290,7 +290,7 @@
     share = rows * CHUNKS
     whole_shape = jax.ShapeDtypeStruct((room + 1, share, BLK), bf16)
     cut_shapes = [
-        jax.ShapeDtypeStruct((room + (j == 0), rows, BLK), bf16) for j in range(CHUNKS)
+        jax.ShapeDtypeStruct((room + (1 if j == 0 else 6), rows, BLK), bf16) for j in range(CHUNKS)
     ]
     packed = pl.pallas_call(
         functools.partial(pack_kernel, near, far, room, rows, blocks),
@@ -342,7 +342,7 @@
     sums, lows, highs = [], [], []
     for chunk in range(CHUNKS):
         cut.append(near_send(after_all(packed[last + chunk], *waited), last))
-        waits = [] if came_first is None else [came_first]
+        waits = []
         keep_low, keep_high, send_low, send_high = pl.pallas_call(
             functools.partial(last_kernel, room, blocks, rows, chunk),
             out_shape=[part_owners_shape] * 4,
@@ -358,7 +358,7 @@
             cost_estimate=spent(2),
             name="last_products",
         )(cut[0], after_all(cut[chunk], *waits), mine[last], other[last], partial)
-        waited = [keep_low]
+        waited = [partial]
         came = far_send(send_high, far[0])
         came_first = (keep_high.astype(jnp.float32) + came.astype(jnp.float32)).astype(bf16)
         sums.append(came_first)
@@ -376,6 +376,8 @@
         found = []
         for start, stop in pieces:
             send, addends, bases = sums[chunk][:, start:stop], list(lows[chunk]), [0, 0]
+            if start > 0:
+                send = after_all(send, arrived[0][0][0][-1])
             size = owners // 4
             for index, bit in enumerate(far[1:]):
                 addends.append(far_send(send, bit))

time: 95.8 us -> 91.7 us (0.957)
  waiting for transfers between devices: 44.6 us -> 35.5 us
  starting transfers between devices: 28.7 us -> 33.7 us
    ppermute x7, waiting for transfers between devices: 19.5 us -> 11.6 us  [far_send(): return lax.ppermute(array, 'graph', xor_pairs(devices, 1 << bit))]
    ppermute x7, starting transfers between devices: 9.5 us -> 10.9 us  [far_send(): return lax.ppermute(array, 'graph', xor_pairs(devices, 1 << bit))]
    ppermute x1, starting transfers between devices: 4.6 us -> 5.9 us  [local(): lax.ppermute(outs[2], 'graph', odd_pairs)]
    ppermute x1, starting transfers between devices: 0.86 us -> 2.14 us  [local(): lax.ppermute(outs[1], 'graph', even_pairs)]
    ppermute x8, waiting for transfers between devices: 2.03 us -> 1.04 us  [swap(): return lax.ppermute(array, 'mp', [(0, 1), (1, 0)])]
  transfers between devices with their start and end apart: 25 -> 25, of which waited for: 12 -> 10; matrix products, arithmetic and copies ran while one was open for 0% -> 0% of each run, Pallas kernels for 13% -> 17%
where the time goes in v4:
time: 91.7 us; the launch traced here: 91.5 us
  waiting for transfers between devices  35.5 us (39%)
  starting transfers between devices  33.7 us (37%)
  Pallas kernels  16.7 us (18%)
  local copies, waits for them, and re-layouts  4.62 us (5%)
    ppermute x8, waiting for transfers between devices, near_send(): return lax.ppermute(array, 'graph', xor_pairs(devices, near_mask(near, k)))  22.7 us
    ppermute x8, starting transfers between devices, near_send(): return lax.ppermute(array, 'graph', xor_pairs(devices, near_mask(near, k)))  12.7 us
    ppermute x7, waiting for transfers between devices, far_send(): return lax.ppermute(array, 'graph', xor_pairs(devices, 1 << bit))  11.6 us
    ppermute x7, starting transfers between devices, far_send(): return lax.ppermute(array, 'graph', xor_pairs(devices, 1 << bit))  10.9 us
    ppermute x1, starting transfers between devices, local(): lax.ppermute(outs[2], 'graph', odd_pairs)  5.9 us
    unnamed x19, local copies, waits for them, and re-layouts  4.54 us
    pallas_call x2, Pallas kernels, local(): pl.pallas_call(functools.partial(mlp_kernel, border, start, blocks), out_...  4.37 us
    pallas_call x2, Pallas kernels, local(): pl.pallas_call(functools.partial(last_kernel, room, blocks, rows, chunk),...  3.89 us
  transfers between devices with their start and end apart: 25, of which 10 were waited for; matrix products, arithmetic and copies ran while one was open for 0% of the time, Pallas kernels for 17%

profile of v4, /device:TPU:0, one launch (start us, length us, event | category | flops | bytes accessed | tf_op | source)
XLA Modules:
  0.0 91.5 jit_solution(1434588848002925744)
XLA Ops:
  1.0 2.5 %collective-permute-start.3 = (bf16[1024,256]{1,0:T(8,128)(2,1)}, bf16[1024,256]{1,0:T(8,128)(2,1)S(1)}, u32[]{:S(2)}, u32[]{:S(2)}) collective-permute-start(bf16[1024,256]{1,0:T(8,128)(2,1)} %refs_0_.4), channel_id=1, source_target_pairs={{0,2},{2,0},{4,6},{6,4},{8,10},{10,8},{12,14},{14,12},{16,18},{18,... | collective-permute-start | bytes 1572872 | tf_op jit(solution)/shard_map/ppermute | solution.py:278
  3.5 1.6 %collective-permute-start.4 = (bf16[1024,256]{1,0:T(8,128)(2,1)}, bf16[1024,256]{1,0:T(8,128)(2,1)S(1)}, u32[]{:S(2)}, u32[]{:S(2)}) collective-permute-start(bf16[1024,256]{1,0:T(8,128)(2,1)} %refs_0_.4), channel_id=1, source_target_pairs={{0,8},{2,10},{4,12},{6,14},{8,0},{10,2},{12,4},{14,6},{16,24},{18,... | collective-permute-start | bytes 1572872 | tf_op jit(solution)/shard_map/ppermute | solution.py:278
  5.1 1.9 %copy-done.1 = bf16[96,128,128]{2,1,0:T(8,128)(2,1)S(1)} copy-done((bf16[96,128,128]{2,1,0:T(8,128)(2,1)S(1)}, bf16[96,128,128]{2,1,0:T(8,128)(2,1)}, u32[]{:S(2)}) %copy-start.1) | copy-done | bytes 3145752
  7.0 0.7 copy-done.5
  9.6 3.6 %pack.1 = (bf16[29,64,128]{2,1,0:T(8,128)(2,1)S(1)}, bf16[29,64,128]{2,1,0:T(8,128)(2,1)S(1)}, bf16[29,64,128]{2,1,0:T(8,128)(2,1)S(1)}, bf16[29,32,128]{2,1,0:T(8,128)(2,1)S(1)}, bf16[34,32,128]{2,1,0:T(8,128)(2,1)S(1)}) custom-call(s32[96]{0:T(128)S(1)} %bitcast.1, s32[96]{0:T(128)S(1)} %copy-done.6, s32[96]{0:T(128)S(1)} %copy-done.7, s32[96]{0:T(128)S(1)} %copy-done.8, ...), custom_call_target="tpu_custom_call" | custom-call | bytes 22140000 | tf_op jit(solution)/shard_map/pack/pallas_call | solution.py:295
  13.2 3.0 %collective-permute-done.3.refs_4_ = bf16[1024,256]{1,0:T(8,128)(2,1)S(1)} collective-permute-done((bf16[1024,256]{1,0:T(8,128)(2,1)}, bf16[1024,256]{1,0:T(8,128)(2,1)S(1)}, u32[]{:S(2)}, u32[]{:S(2)}) %collective-permute-start.3) | collective-permute-done | bytes 524320 | tf_op jit(solution)/shard_map/ppermute | solution.py:278
  16.3 1.5 %collective-permute-done.4.refs_5_ = bf16[1024,256]{1,0:T(8,128)(2,1)S(1)} collective-permute-done((bf16[1024,256]{1,0:T(8,128)(2,1)}, bf16[1024,256]{1,0:T(8,128)(2,1)S(1)}, u32[]{:S(2)}, u32[]{:S(2)}) %collective-permute-start.4) | collective-permute-done | bytes 524320 | tf_op jit(solution)/shard_map/ppermute | solution.py:278
  18.1 1.7 %collective-permute-start.6 = (bf16[29,64,128]{2,1,0:T(8,128)(2,1)S(1)}, bf16[29,64,128]{2,1,0:T(8,128)(2,1)S(1)}, u32[]{:S(2)}, u32[]{:S(2)}) collective-permute-start(bf16[29,64,128]{2,1,0:T(8,128)(2,1)S(1)} %get-tuple-element.43), channel_id=1, source_target_pairs={{0,8},{2,10},{4,12},{6,14},{8,0},{10,2},{12,4},{14,6},{16,24},{18,... | collective-permute-start | bytes 1425416 | tf_op jit(solution)/shard_map/ppermute | solution.py:278
  20.3 1.7 %collective-permute-start.9 = (bf16[512,256]{1,0:T(8,128)(2,1)S(1)}, bf16[512,256]{1,0:T(8,128)(2,1)S(1)}, u32[]{:S(2)}, u32[]{:S(2)}) collective-permute-start(bf16[512,256]{1,0:T(8,128)(2,1)S(1)} %slice.13), channel_id=1, source_target_pairs={{0,2},{2,0},{4,6},{6,4},{8,10},{10,8},{12,14},{14,12},{16,18},{18,... | collective-permute-start | bytes 786440 | tf_op jit(solution)/shard_map/ppermute | solution.py:278
  21.9 13.9 %collective-permute-done.8 = bf16[512,256]{1,0:T(8,128)(2,1)S(1)} collective-permute-done((bf16[512,256]{1,0:T(8,128)(2,1)S(1)}, bf16[512,256]{1,0:T(8,128)(2,1)S(1)}, u32[]{:S(2)}, u32[]{:S(2)}) %collective-permute-start.8) | collective-permute-done | bytes 262176 | tf_op jit(solution)/shard_map/ppermute | solution.py:278
  36.7 2.3 %collective-permute-start.7 = (bf16[29,32,128]{2,1,0:T(8,128)(2,1)S(1)}, bf16[29,32,128]{2,1,0:T(8,128)(2,1)S(1)}, u32[]{:S(2)}, u32[]{:S(2)}) collective-permute-start(bf16[29,32,128]{2,1,0:T(8,128)(2,1)S(1)} %get-tuple-element.44), channel_id=1, source_target_pairs={{0,10},{2,8},{4,14},{6,12},{8,2},{10,0},{12,6},{14,4},{16,26},{18,... | collective-permute-start | bytes 712712 | tf_op jit(solution)/shard_map/ppermute | solution.py:278
  39.0 3.8 %first_products.1.before = f32[32,64,512]{2,1,0:T(8,128)S(1)} custom-call(bf16[29,64,128]{2,1,0:T(8,128)(2,1)S(1)} %get-tuple-element.45.refs_0_, bf16[29,64,128]{2,1,0:T(8,128)(2,1)S(1)} %collective-permute-done.5.refs_1_, bf16[29,64,128]{2,1,0:T(8,128)(2,1)S(1)} %collective-permute-done.6.refs_2_, bf16[1024,256]{1,0:T(8,128)(2,1)S(1)} %copy-done, ...), custom_call_target="tpu_custom_call" | custom-call | bytes 14760000 | tf_op jit(solution)/shard_map/first_products/pallas_call | solution.py:322
  42.8 2.0 %collective-permute-start.16 = (bf16[34,32,128]{2,1,0:T(8,128)(2,1)S(1)}, bf16[34,32,128]{2,1,0:T(8,128)(2,1)S(1)}, u32[]{:S(2)}, u32[]{:S(2)}) collective-permute-start(bf16[34,32,128]{2,1,0:T(8,128)(2,1)S(1)} %get-tuple-element.57), channel_id=1, source_target_pairs={{0,10},{2,8},{4,14},{6,12},{8,2},{10,0},{12,6},{14,4},{16,26},{18,... | collective-permute-start | bytes 835592 | tf_op jit(solution)/shard_map/ppermute | solution.py:278
  44.8 0.9 collective-permute-done.7.labels.basis
  45.7 2.0 %last_products.2 = (bf16[1,8,32,512]{3,2,1,0:T(8,128)(2,1)S(1)}, bf16[1,8,32,512]{3,2,1,0:T(8,128)(2,1)S(1)}, bf16[1,8,32,512]{3,2,1,0:T(8,128)(2,1)S(1)}, bf16[1,8,32,512]{3,2,1,0:T(8,128)(2,1)S(1)}) custom-call(bf16[29,32,128]{2,1,0:T(8,128)(2,1)S(1)} %collective-permute-done.7.labels.basis, bf16[29,32,128]{2,1,0:T(8,128)(2,1)S(1)} %collective-permute-done.7.labels.basis, ...), custom_call_target="tpu_custom_call" | custom-call | bytes 7380000 | tf_op jit(solution)/shard_map/last_products/pallas_call | solution.py:346
  47.7 1.5 %collective-permute-start.13 = (bf16[1,8,32,512]{3,2,1,0:T(8,128)(2,1)S(1)}, bf16[1,8,32,512]{3,2,1,0:T(8,128)(2,1)S(1)}, u32[]{:S(2)}, u32[]{:S(2)}) collective-permute-start(bf16[1,8,32,512]{3,2,1,0:T(8,128)(2,1)S(1)} %get-tuple-element.53), channel_id=1, source_target_pairs={{0,4},{2,6},{4,0},{6,2},{8,12},{10,14},{12,8},{14,10},{16,20},{18,... | collective-permute-start | bytes 786440 | tf_op jit(solution)/shard_map/ppermute | solution.py:281
  49.1 3.3 %collective-permute-done.16.basis = bf16[34,32,128]{2,1,0:T(8,128)(2,1)S(1)} collective-permute-done((bf16[34,32,128]{2,1,0:T(8,128)(2,1)S(1)}, bf16[34,32,128]{2,1,0:T(8,128)(2,1)S(1)}, u32[]{:S(2)}, u32[]{:S(2)}) %collective-permute-start.16) | collective-permute-done | bytes 278560 | tf_op jit(solution)/shard_map/ppermute | solution.py:278
  52.5 1.9 %last_products.3 = (bf16[1,8,32,512]{3,2,1,0:T(8,128)(2,1)S(1)}, bf16[1,8,32,512]{3,2,1,0:T(8,128)(2,1)S(1)}, bf16[1,8,32,512]{3,2,1,0:T(8,128)(2,1)S(1)}, bf16[1,8,32,512]{3,2,1,0:T(8,128)(2,1)S(1)}) custom-call(bf16[29,32,128]{2,1,0:T(8,128)(2,1)S(1)} %collective-permute-done.7.labels.basis, bf16[34,32,128]{2,1,0:T(8,128)(2,1)S(1)} %collective-permute-done.16.basis, ...), custom_call_target="tpu_custom_call" | custom-call | bytes 7380000 | tf_op jit(solution)/shard_map/last_products/pallas_call | solution.py:346
  54.4 1.6 %collective-permute-start.17 = (bf16[1,8,32,512]{3,2,1,0:T(8,128)(2,1)S(1)}, bf16[1,8,32,512]{3,2,1,0:T(8,128)(2,1)S(1)}, u32[]{:S(2)}, u32[]{:S(2)}) collective-permute-start(bf16[1,8,32,512]{3,2,1,0:T(8,128)(2,1)S(1)} %get-tuple-element.60), channel_id=1, source_target_pairs={{0,4},{2,6},{4,0},{6,2},{8,12},{10,14},{12,8},{14,10},{16,20},{18,... | collective-permute-start | bytes 786440 | tf_op jit(solution)/shard_map/ppermute | solution.py:281
  56.1 2.7 %collective-permute-start.15 = (bf16[1,8,32,512]{3,2,1,0:T(8,128)(2,1)S(1)}, bf16[1,8,32,512]{3,2,1,0:T(8,128)(2,1)S(1)}, u32[]{:S(2)}, u32[]{:S(2)}) collective-permute-start(bf16[1,8,32,512]{3,2,1,0:T(8,128)(2,1)S(1)} %add_convert_fusion.1), channel_id=1, source_target_pairs={{0,16},{2,18},{4,20},{6,22},{8,24},{10,26},{12,28},{14,30},{16,0},... | collective-permute-start | bytes 786440 | tf_op jit(solution)/shard_map/ppermute | solution.py:281
  58.8 1.0 %collective-permute-start.14 = (bf16[1,8,32,512]{3,2,1,0:T(8,128)(2,1)S(1)}, bf16[1,8,32,512]{3,2,1,0:T(8,128)(2,1)S(1)}, u32[]{:S(2)}, u32[]{:S(2)}) collective-permute-start(bf16[1,8,32,512]{3,2,1,0:T(8,128)(2,1)S(1)} %get-tuple-element.54), channel_id=1, source_target_pairs={{0,4},{2,6},{4,0},{6,2},{8,12},{10,14},{12,8},{14,10},{16,20},{18,... | collective-permute-start | bytes 786440 | tf_op jit(solution)/shard_map/ppermute | solution.py:281
  59.7 4.0 %collective-permute-done.17 = bf16[1,8,32,512]{3,2,1,0:T(8,128)(2,1)S(1)} collective-permute-done((bf16[1,8,32,512]{3,2,1,0:T(8,128)(2,1)S(1)}, bf16[1,8,32,512]{3,2,1,0:T(8,128)(2,1)S(1)}, u32[]{:S(2)}, u32[]{:S(2)}) %collective-permute-start.17) | collective-permute-done | bytes 262176 | tf_op jit(solution)/shard_map/ppermute | solution.py:281
  63.8 1.5 %collective-permute-start.18 = (bf16[1,8,32,512]{3,2,1,0:T(8,128)(2,1)S(1)}, bf16[1,8,32,512]{3,2,1,0:T(8,128)(2,1)S(1)}, u32[]{:S(2)}, u32[]{:S(2)}) collective-permute-start(bf16[1,8,32,512]{3,2,1,0:T(8,128)(2,1)S(1)} %get-tuple-element.61), channel_id=1, source_target_pairs={{0,4},{2,6},{4,0},{6,2},{8,12},{10,14},{12,8},{14,10},{16,20},{18,... | collective-permute-start | bytes 786440 | tf_op jit(solution)/shard_map/ppermute | solution.py:281
  65.4 2.7 %collective-permute-start.19 = (bf16[1,4,32,512]{3,2,1,0:T(8,128)(2,1)S(1)}, bf16[1,4,32,512]{3,2,1,0:T(8,128)(2,1)S(1)}, u32[]{:S(2)}, u32[]{:S(2)}) collective-permute-start(bf16[1,4,32,512]{3,2,1,0:T(8,128)(2,1)S(1)} %get-tuple-element.72), channel_id=1, source_target_pairs={{0,16},{2,18},{4,20},{6,22},{8,24},{10,26},{12,28},{14,30},{16,0},... | collective-permute-start | bytes 393224 | tf_op jit(solution)/shard_map/ppermute | solution.py:281
  68.0 5.4 %collective-permute-done.15.refs_4_ = bf16[1,8,32,512]{3,2,1,0:T(8,128)(2,1)S(1)} collective-permute-done((bf16[1,8,32,512]{3,2,1,0:T(8,128)(2,1)S(1)}, bf16[1,8,32,512]{3,2,1,0:T(8,128)(2,1)S(1)}, u32[]{:S(2)}, u32[]{:S(2)}) %collective-permute-start.15) | collective-permute-done | bytes 262176 | tf_op jit(solution)/shard_map/ppermute | solution.py:281
  73.4 2.1 %collective-permute-done.19.refs_7_ = bf16[1,4,32,512]{3,2,1,0:T(8,128)(2,1)S(1)} collective-permute-done((bf16[1,4,32,512]{3,2,1,0:T(8,128)(2,1)S(1)}, bf16[1,4,32,512]{3,2,1,0:T(8,128)(2,1)S(1)}, u32[]{:S(2)}, u32[]{:S(2)}) %collective-permute-start.19) | collective-permute-done | bytes 131104 | tf_op jit(solution)/shard_map/ppermute | solution.py:281
  75.7 2.1 %collective-permute-start.20 = (bf16[2,64,512]{2,1,0:T(8,128)(2,1)S(1)}, bf16[2,64,512]{2,1,0:T(8,128)(2,1)S(1)}, u32[]{:S(2)}, u32[]{:S(2)}) collective-permute-start(bf16[2,64,512]{2,1,0:T(8,128)(2,1)S(1)} %get-tuple-element.64), channel_id=1, source_target_pairs={{0,2},{2,0},{4,6},{6,4},{8,10},{10,8},{12,14},{14,12},{16,18},{18,... | collective-permute-start | bytes 393224 | tf_op jit(solution)/shard_map/ppermute | solution.py:411
  77.9 5.9 %collective-permute-start.21 = (bf16[2,64,512]{2,1,0:T(8,128)(2,1)S(1)}, bf16[2,64,512]{2,1,0:T(8,128)(2,1)S(1)}, u32[]{:S(2)}, u32[]{:S(2)}) collective-permute-start(bf16[2,64,512]{2,1,0:T(8,128)(2,1)S(1)} %get-tuple-element.65), channel_id=1, source_target_pairs={{0,30},{2,4},{4,2},{6,8},{8,6},{10,12},{12,10},{14,16},{16,14},{18... | collective-permute-start | bytes 393224 | tf_op jit(solution)/shard_map/ppermute | solution.py:410
  84.6 2.2 %mlp.3 = (bf16[4,64,256]{2,1,0:T(8,128)(2,1)S(1)}, bf16[4,64,256]{2,1,0:T(8,128)(2,1)S(1)}) custom-call(s32[8]{0:T(128)S(1)} %copy-done.4, s32[1]{0:T(128)S(6)} %copy.12.valid, bf16[4,64,512]{2,1,0:T(8,128)(2,1)S(1)} %combine.3.combined, bf16[3,512,256]{2,1,0:T(8,128)(2,1)S(1)} %copy-done.2, bf16[3,512,256]{2,1,0:T(8,128)(2,1)S(1)} %collective-permute-done.1.refs_3_.refs_1_, ...), custom_call_target="tpu_custom_call" | custom-call | bytes 7380000 | tf_op jit(solution)/shard_map/mlp/pallas_call | solution.py:414
  87.1 2.2 %mlp.2 = (bf16[4,64,256]{2,1,0:T(8,128)(2,1)S(1)}, bf16[4,64,256]{2,1,0:T(8,128)(2,1)S(1)}) custom-call(s32[8]{0:T(128)S(1)} %copy-done.4, s32[1]{0:T(128)S(6)} %copy.12.valid, bf16[4,64,512]{2,1,0:T(8,128)(2,1)S(1)} %get-tuple-element.63.combined, bf16[2,64,512]{2,1,0:T(8,128)(2,1)S(1)} %collective-permute-done.20.refs_0_, ...), custom_call_target="tpu_custom_call" | custom-call | bytes 7380000 | tf_op jit(solution)/shard_map/mlp/pallas_call | solution.py:414
  89.6 1.0 %collective-permute-done.23.refs_2_ = bf16[4,64,256]{2,1,0:T(8,128)(2,1)S(1)} collective-permute-done((bf16[4,64,256]{2,1,0:T(8,128)(2,1)S(1)}, bf16[4,64,256]{2,1,0:T(8,128)(2,1)S(1)}, u32[]{:S(2)}, u32[]{:S(2)}) %collective-permute-start.23) | collective-permute-done | bytes 131104 | tf_op jit(solution)/shard_map/ppermute | solution.py:284
  90.7 0.8 join.1
  (52 shorter events, 5.6 us)
Async XLA Ops:
  0.0 39.0 %copy-start = (bf16[1024,256]{1,0:T(8,128)(2,1)S(1)}, bf16[1024,256]{1,0:T(8,128)(2,1)}, u32[]{:S(2)}) copy-start(bf16[1024,256]{1,0:T(8,128)(2,1)} %refs_0_.4) | copy-start | bytes 1572868
  0.0 5.1 %collective-permute-start.1 = (bf16[3,512,256]{2,1,0:T(8,128)(2,1)}, bf16[3,512,256]{2,1,0:T(8,128)(2,1)S(1)}, u32[]{:S(2)}, u32[]{:S(2)}) collective-permute-start(bf16[3,512,256]{2,1,0:T(8,128)(2,1)} %refs_0_.5), channel_id=1, source_target_pairs={{0,1},{1,0},{2,3},{3,2},{4,5},{5,4},{6,7},{7,6},{8,9},{9,8},{10,11... | collective-permute-start | bytes 2359304 | tf_op jit(solution)/shard_map/ppermute | solution.py:284
  0.5 4.6 %collective-permute-start.2 = (bf16[3,256,512]{2,1,0:T(8,128)(2,1)}, bf16[3,256,512]{2,1,0:T(8,128)(2,1)S(1)}, u32[]{:S(2)}, u32[]{:S(2)}) collective-permute-start(bf16[3,256,512]{2,1,0:T(8,128)(2,1)} %refs_2_.3), channel_id=1, source_target_pairs={{0,1},{1,0},{2,3},{3,2},{4,5},{5,4},{6,7},{7,6},{8,9},{9,8},{10,11... | collective-permute-start | bytes 2359304 | tf_op jit(solution)/shard_map/ppermute | solution.py:284
  0.5 4.6 %collective-permute-start = (bf16[1024,256]{1,0:T(8,128)(2,1)}, bf16[1024,256]{1,0:T(8,128)(2,1)S(1)}, u32[]{:S(2)}, u32[]{:S(2)}) collective-permute-start(bf16[1024,256]{1,0:T(8,128)(2,1)} %refs_0_.4), channel_id=1, source_target_pairs={{0,1},{1,0},{2,3},{3,2},{4,5},{5,4},{6,7},{7,6},{8,9},{9,8},{10,11... | collective-permute-start | bytes 1572872 | tf_op jit(solution)/shard_map/ppermute | solution.py:284
  1.0 15.3 %collective-permute-start.3 = (bf16[1024,256]{1,0:T(8,128)(2,1)}, bf16[1024,256]{1,0:T(8,128)(2,1)S(1)}, u32[]{:S(2)}, u32[]{:S(2)}) collective-permute-start(bf16[1024,256]{1,0:T(8,128)(2,1)} %refs_0_.4), channel_id=1, source_target_pairs={{0,2},{2,0},{4,6},{6,4},{8,10},{10,8},{12,14},{14,12},{16,18},{18,... | collective-permute-start | bytes 1572872 | tf_op jit(solution)/shard_map/ppermute | solution.py:278
  3.5 14.2 %collective-permute-start.4 = (bf16[1024,256]{1,0:T(8,128)(2,1)}, bf16[1024,256]{1,0:T(8,128)(2,1)S(1)}, u32[]{:S(2)}, u32[]{:S(2)}) collective-permute-start(bf16[1024,256]{1,0:T(8,128)(2,1)} %refs_0_.4), channel_id=1, source_target_pairs={{0,8},{2,10},{4,12},{6,14},{8,0},{10,2},{12,4},{14,6},{16,24},{18,... | collective-permute-start | bytes 1572872 | tf_op jit(solution)/shard_map/ppermute | solution.py:278
  5.1 1.9 %copy-start.1 = (bf16[96,128,128]{2,1,0:T(8,128)(2,1)S(1)}, bf16[96,128,128]{2,1,0:T(8,128)(2,1)}, u32[]{:S(2)}) copy-start(bf16[96,128,128]{2,1,0:T(8,128)(2,1)} %basis) | copy-start | bytes 9437188
  7.0 0.7 copy-start.5
  7.7 0.7 copy-start.6
  17.7 18.2 %collective-permute-start.5 = (bf16[29,64,128]{2,1,0:T(8,128)(2,1)S(1)}, bf16[29,64,128]{2,1,0:T(8,128)(2,1)S(1)}, u32[]{:S(2)}, u32[]{:S(2)}) collective-permute-start(bf16[29,64,128]{2,1,0:T(8,128)(2,1)S(1)} %get-tuple-element.41), channel_id=1, source_target_pairs={{0,2},{2,0},{4,6},{6,4},{8,10},{10,8},{12,14},{14,12},{16,18},{18,... | collective-permute-start | bytes 1425416 | tf_op jit(solution)/shard_map/ppermute | solution.py:278
  18.1 17.8 %collective-permute-start.6 = (bf16[29,64,128]{2,1,0:T(8,128)(2,1)S(1)}, bf16[29,64,128]{2,1,0:T(8,128)(2,1)S(1)}, u32[]{:S(2)}, u32[]{:S(2)}) collective-permute-start(bf16[29,64,128]{2,1,0:T(8,128)(2,1)S(1)} %get-tuple-element.43), channel_id=1, source_target_pairs={{0,8},{2,10},{4,12},{6,14},{8,0},{10,2},{12,4},{14,6},{16,24},{18,... | collective-permute-start | bytes 1425416 | tf_op jit(solution)/shard_map/ppermute | solution.py:278
  19.9 16.0 %collective-permute-start.8 = (bf16[512,256]{1,0:T(8,128)(2,1)S(1)}, bf16[512,256]{1,0:T(8,128)(2,1)S(1)}, u32[]{:S(2)}, u32[]{:S(2)}) collective-permute-start(bf16[512,256]{1,0:T(8,128)(2,1)S(1)} %slice.12), channel_id=1, source_target_pairs={{0,8},{2,10},{4,12},{6,14},{8,0},{10,2},{12,4},{14,6},{16,24},{18,... | collective-permute-start | bytes 786440 | tf_op jit(solution)/shard_map/ppermute | solution.py:278
  20.3 16.3 %collective-permute-start.9 = (bf16[512,256]{1,0:T(8,128)(2,1)S(1)}, bf16[512,256]{1,0:T(8,128)(2,1)S(1)}, u32[]{:S(2)}, u32[]{:S(2)}) collective-permute-start(bf16[512,256]{1,0:T(8,128)(2,1)S(1)} %slice.13), channel_id=1, source_target_pairs={{0,2},{2,0},{4,6},{6,4},{8,10},{10,8},{12,14},{14,12},{16,18},{18,... | collective-permute-start | bytes 786440 | tf_op jit(solution)/shard_map/ppermute | solution.py:278
  35.9 3.1 %collective-permute-start.12 = (bf16[1024,256]{1,0:T(8,128)(2,1)S(1)}, bf16[1024,256]{1,0:T(8,128)(2,1)S(1)}, u32[]{:S(2)}, u32[]{:S(2)}) collective-permute-start(bf16[1024,256]{1,0:T(8,128)(2,1)S(1)} %collective-permute-done.4.refs_5_), channel_id=1, source_target_pairs={{0,1},{1,0},{2,3},{3,2},{4,5},{5,4},{6,7},{7,6},{8,9},{9,8},{10,11... | collective-permute-start | bytes 1572872 | tf_op jit(solution)/shard_map/ppermute | solution.py:284
  36.0 3.0 %collective-permute-start.11 = (bf16[1024,256]{1,0:T(8,128)(2,1)S(1)}, bf16[1024,256]{1,0:T(8,128)(2,1)S(1)}, u32[]{:S(2)}, u32[]{:S(2)}) collective-permute-start(bf16[1024,256]{1,0:T(8,128)(2,1)S(1)} %collective-permute-done.3.refs_4_), channel_id=1, source_target_pairs={{0,1},{1,0},{2,3},{3,2},{4,5},{5,4},{6,7},{7,6},{8,9},{9,8},{10,11... | collective-permute-start | bytes 1572872 | tf_op jit(solution)/shard_map/ppermute | solution.py:284
  36.5 9.2 %collective-permute-start.10 = (bf16[1024,256]{1,0:T(8,128)(2,1)S(1)}, bf16[1024,256]{1,0:T(8,128)(2,1)S(1)}, u32[]{:S(2)}, u32[]{:S(2)}) collective-permute-start(bf16[1024,256]{1,0:T(8,128)(2,1)S(1)} %constant_dynamic-update-slice_fusion.mine), channel_id=1, source_target_pairs={{0,1},{1,0},{2,3},{3,2},{4,5},{5,4},{6,7},{7,6},{8,9},{9,8},{10,11... | collective-permute-start | bytes 1572872 | tf_op jit(solution)/shard_map/ppermute | solution.py:284
  36.7 9.0 %collective-permute-start.7 = (bf16[29,32,128]{2,1,0:T(8,128)(2,1)S(1)}, bf16[29,32,128]{2,1,0:T(8,128)(2,1)S(1)}, u32[]{:S(2)}, u32[]{:S(2)}) collective-permute-start(bf16[29,32,128]{2,1,0:T(8,128)(2,1)S(1)} %get-tuple-element.44), channel_id=1, source_target_pairs={{0,10},{2,8},{4,14},{6,12},{8,2},{10,0},{12,6},{14,4},{16,26},{18,... | collective-permute-start | bytes 712712 | tf_op jit(solution)/shard_map/ppermute | solution.py:278
  42.8 9.7 %collective-permute-start.16 = (bf16[34,32,128]{2,1,0:T(8,128)(2,1)S(1)}, bf16[34,32,128]{2,1,0:T(8,128)(2,1)S(1)}, u32[]{:S(2)}, u32[]{:S(2)}) collective-permute-start(bf16[34,32,128]{2,1,0:T(8,128)(2,1)S(1)} %get-tuple-element.57), channel_id=1, source_target_pairs={{0,10},{2,8},{4,14},{6,12},{8,2},{10,0},{12,6},{14,4},{16,26},{18,... | collective-permute-start | bytes 835592 | tf_op jit(solution)/shard_map/ppermute | solution.py:278
  47.7 8.4 %collective-permute-start.13 = (bf16[1,8,32,512]{3,2,1,0:T(8,128)(2,1)S(1)}, bf16[1,8,32,512]{3,2,1,0:T(8,128)(2,1)S(1)}, u32[]{:S(2)}, u32[]{:S(2)}) collective-permute-start(bf16[1,8,32,512]{3,2,1,0:T(8,128)(2,1)S(1)} %get-tuple-element.53), channel_id=1, source_target_pairs={{0,4},{2,6},{4,0},{6,2},{8,12},{10,14},{12,8},{14,10},{16,20},{18,... | collective-permute-start | bytes 786440 | tf_op jit(solution)/shard_map/ppermute | solution.py:281
  54.4 30.2 %copy-start.2 = (bf16[3,512,256]{2,1,0:T(8,128)(2,1)S(1)}, bf16[3,512,256]{2,1,0:T(8,128)(2,1)}, u32[]{:S(2)}) copy-start(bf16[3,512,256]{2,1,0:T(8,128)(2,1)} %refs_0_.5) | copy-start | bytes 2359300
  54.4 30.2 %copy-start.3 = (bf16[3,256,512]{2,1,0:T(8,128)(2,1)S(1)}, bf16[3,256,512]{2,1,0:T(8,128)(2,1)}, u32[]{:S(2)}) copy-start(bf16[3,256,512]{2,1,0:T(8,128)(2,1)} %refs_2_.3) | copy-start | bytes 2359300
  54.4 30.2 %copy-start.4 = (s32[8]{0:T(128)S(1)}, s32[8]{0:T(128)}, u32[]{:S(2)}) copy-start(s32[8]{0:T(128)} %reverse.3) | copy-start | bytes 100
  54.4 9.3 %collective-permute-start.17 = (bf16[1,8,32,512]{3,2,1,0:T(8,128)(2,1)S(1)}, bf16[1,8,32,512]{3,2,1,0:T(8,128)(2,1)S(1)}, u32[]{:S(2)}, u32[]{:S(2)}) collective-permute-start(bf16[1,8,32,512]{3,2,1,0:T(8,128)(2,1)S(1)} %get-tuple-element.60), channel_id=1, source_target_pairs={{0,4},{2,6},{4,0},{6,2},{8,12},{10,14},{12,8},{14,10},{16,20},{18,... | collective-permute-start | bytes 786440 | tf_op jit(solution)/shard_map/ppermute | solution.py:281
  56.1 17.3 %collective-permute-start.15 = (bf16[1,8,32,512]{3,2,1,0:T(8,128)(2,1)S(1)}, bf16[1,8,32,512]{3,2,1,0:T(8,128)(2,1)S(1)}, u32[]{:S(2)}, u32[]{:S(2)}) collective-permute-start(bf16[1,8,32,512]{3,2,1,0:T(8,128)(2,1)S(1)} %add_convert_fusion.1), channel_id=1, source_target_pairs={{0,16},{2,18},{4,20},{6,22},{8,24},{10,26},{12,28},{14,30},{16,0},... | collective-permute-start | bytes 786440 | tf_op jit(solution)/shard_map/ppermute | solution.py:281
  58.8 14.7 %collective-permute-start.14 = (bf16[1,8,32,512]{3,2,1,0:T(8,128)(2,1)S(1)}, bf16[1,8,32,512]{3,2,1,0:T(8,128)(2,1)S(1)}, u32[]{:S(2)}, u32[]{:S(2)}) collective-permute-start(bf16[1,8,32,512]{3,2,1,0:T(8,128)(2,1)S(1)} %get-tuple-element.54), channel_id=1, source_target_pairs={{0,4},{2,6},{4,0},{6,2},{8,12},{10,14},{12,8},{14,10},{16,20},{18,... | collective-permute-start | bytes 786440 | tf_op jit(solution)/shard_map/ppermute | solution.py:281
  63.8 11.8 %collective-permute-start.18 = (bf16[1,8,32,512]{3,2,1,0:T(8,128)(2,1)S(1)}, bf16[1,8,32,512]{3,2,1,0:T(8,128)(2,1)S(1)}, u32[]{:S(2)}, u32[]{:S(2)}) collective-permute-start(bf16[1,8,32,512]{3,2,1,0:T(8,128)(2,1)S(1)} %get-tuple-element.61), channel_id=1, source_target_pairs={{0,4},{2,6},{4,0},{6,2},{8,12},{10,14},{12,8},{14,10},{16,20},{18,... | collective-permute-start | bytes 786440 | tf_op jit(solution)/shard_map/ppermute | solution.py:281
  65.4 10.2 %collective-permute-start.19 = (bf16[1,4,32,512]{3,2,1,0:T(8,128)(2,1)S(1)}, bf16[1,4,32,512]{3,2,1,0:T(8,128)(2,1)S(1)}, u32[]{:S(2)}, u32[]{:S(2)}) collective-permute-start(bf16[1,4,32,512]{3,2,1,0:T(8,128)(2,1)S(1)} %get-tuple-element.72), channel_id=1, source_target_pairs={{0,16},{2,18},{4,20},{6,22},{8,24},{10,26},{12,28},{14,30},{16,0},... | collective-permute-start | bytes 393224 | tf_op jit(solution)/shard_map/ppermute | solution.py:281
  73.4 11.0 %collective-permute-start.22 = (bf16[1,4,32,512]{3,2,1,0:T(8,128)(2,1)S(1)}, bf16[1,4,32,512]{3,2,1,0:T(8,128)(2,1)S(1)}, u32[]{:S(2)}, u32[]{:S(2)}) collective-permute-start(bf16[1,4,32,512]{3,2,1,0:T(8,128)(2,1)S(1)} %get-tuple-element.67), channel_id=1, source_target_pairs={{0,16},{2,18},{4,20},{6,22},{8,24},{10,26},{12,28},{14,30},{16,0},... | collective-permute-start | bytes 393224 | tf_op jit(solution)/shard_map/ppermute | solution.py:281
  75.7 11.2 %collective-permute-start.20 = (bf16[2,64,512]{2,1,0:T(8,128)(2,1)S(1)}, bf16[2,64,512]{2,1,0:T(8,128)(2,1)S(1)}, u32[]{:S(2)}, u32[]{:S(2)}) collective-permute-start(bf16[2,64,512]{2,1,0:T(8,128)(2,1)S(1)} %get-tuple-element.64), channel_id=1, source_target_pairs={{0,2},{2,0},{4,6},{6,4},{8,10},{10,8},{12,14},{14,12},{16,18},{18,... | collective-permute-start | bytes 393224 | tf_op jit(solution)/shard_map/ppermute | solution.py:411
  77.9 9.2 %collective-permute-start.21 = (bf16[2,64,512]{2,1,0:T(8,128)(2,1)S(1)}, bf16[2,64,512]{2,1,0:T(8,128)(2,1)S(1)}, u32[]{:S(2)}, u32[]{:S(2)}) collective-permute-start(bf16[2,64,512]{2,1,0:T(8,128)(2,1)S(1)} %get-tuple-element.65), channel_id=1, source_target_pairs={{0,30},{2,4},{4,2},{6,8},{8,6},{10,12},{12,10},{14,16},{16,14},{18... | collective-permute-start | bytes 393224 | tf_op jit(solution)/shard_map/ppermute | solution.py:410
  86.8 2.8 %collective-permute-start.24 = (bf16[4,64,256]{2,1,0:T(8,128)(2,1)S(1)}, bf16[4,64,256]{2,1,0:T(8,128)(2,1)S(1)}, u32[]{:S(2)}, u32[]{:S(2)}) collective-permute-start(bf16[4,64,256]{2,1,0:T(8,128)(2,1)S(1)} %get-tuple-element.70), channel_id=1, source_target_pairs={{0,1},{1,0},{2,3},{3,2},{4,5},{5,4},{6,7},{7,6},{8,9},{9,8},{10,11... | collective-permute-start | bytes 393224 | tf_op jit(solution)/shard_map/ppermute | solution.py:284
  89.3 1.4 %collective-permute-start.23 = (bf16[4,64,256]{2,1,0:T(8,128)(2,1)S(1)}, bf16[4,64,256]{2,1,0:T(8,128)(2,1)S(1)}, u32[]{:S(2)}, u32[]{:S(2)}) collective-permute-start(bf16[4,64,256]{2,1,0:T(8,128)(2,1)S(1)} %get-tuple-element.69), channel_id=1, source_target_pairs={{0,1},{1,0},{2,3},{3,2},{4,5},{5,4},{6,7},{7,6},{8,9},{9,8},{10,11... | collective-permute-start | bytes 393224 | tf_op jit(solution)/shard_map/ppermute | solution.py:284
  (2 other events, 1.3 us)

commit v5 on v4

--- a/solution.py
+++ b/solution.py
@@ -284,7 +284,6 @@
         return lax.ppermute(array, "mp", [(0, 1), (1, 0)])
 
     mine = [messages, near_send(messages, 1), near_send(messages, 2)]
-    other = [swap(messages)]
     in_other, out_other = swap(weight_in), swap(weight_out)
 
     share = rows * CHUNKS
@@ -306,13 +305,14 @@
         source_block,
         target_block,
         row_counts,
-        after_all(basis_blocks, other[0], in_other, out_other),
+        after_all(basis_blocks, in_other, out_other),
     )
     last = groups - 1
     middle = edge_rows // 2
+    other = [swap(after_all(messages, packed[0]))]
     basis = [packed[0]]
     for k in range(1, last):
-        basis.append(near_send(after_all(packed[k], *mine[1:]), k))
+        basis.append(near_send(packed[k], k))
     ready = [after_all(array, packed[0]) for array in mine[1:]]
     onward = [near_send(ready[0][:middle], 2), near_send(ready[1][middle:], 1)]
     mine.append(jnp.concatenate(onward, axis=0))
@@ -365,7 +365,7 @@
         highs.append(came)
         lows.append((keep_low, send_low))
     lows = [
-        (keep_low, far_send(after_all(send_low, came), far[0]))
+        (keep_low, far_send(after_all(send_low, highs[-1]), far[0]))
         for (keep_low, send_low), came in zip(lows, highs)
     ]
     starts = [0, 2 * border]

time: 91.7 us -> 89 us (0.971)
  waiting for transfers between devices: 35.5 us -> 32.2 us
    ppermute x8, waiting for transfers between devices: 22.7 us -> 18.3 us  [near_send(): return lax.ppermute(array, 'graph', xor_pairs(devices, near_mask(near, k)))]
    ppermute x1, starting transfers between devices: 5.9 us -> 7.37 us  [local(): lax.ppermute(outs[2], 'graph', odd_pairs)]
    ppermute x1, starting transfers between devices: 2.14 us -> 0.88 us  [local(): lax.ppermute(outs[1], 'graph', even_pairs)]
    ppermute x8, starting transfers between devices: 12.7 us -> 13.8 us  [near_send(): return lax.ppermute(array, 'graph', xor_pairs(devices, near_mask(near, k)))]
  transfers between devices with their start and end apart: 25 -> 25, of which waited for: 10 -> 9; matrix products, arithmetic and copies ran while one was open for 0% -> 0% of each run, Pallas kernels for 17% -> 18%
where the time goes in v5:
time: 89 us; the launch traced here: 88.8 us
  starting transfers between devices  34.2 us (38%)
  waiting for transfers between devices  32.2 us (36%)
  Pallas kernels  16.7 us (19%)
  local copies, waits for them, and re-layouts  4.62 us (5%)
    ppermute x8, waiting for transfers between devices, near_send(): return lax.ppermute(array, 'graph', xor_pairs(devices, near_mask(near, k)))  18.3 us
    ppermute x8, starting transfers between devices, near_send(): return lax.ppermute(array, 'graph', xor_pairs(devices, near_mask(near, k)))  13.8 us
    ppermute x7, waiting for transfers between devices, far_send(): return lax.ppermute(array, 'graph', xor_pairs(devices, 1 << bit))  12.3 us
    ppermute x7, starting transfers between devices, far_send(): return lax.ppermute(array, 'graph', xor_pairs(devices, 1 << bit))  10.5 us
    ppermute x1, starting transfers between devices, local(): lax.ppermute(outs[2], 'graph', odd_pairs)  7.37 us
    unnamed x19, local copies, waits for them, and re-layouts  4.55 us
    pallas_call x2, Pallas kernels, local(): pl.pallas_call(functools.partial(mlp_kernel, border, start, blocks), out_...  4.37 us
    pallas_call x2, Pallas kernels, local(): pl.pallas_call(functools.partial(last_kernel, room, blocks, rows, chunk),...  3.89 us
  transfers between devices with their start and end apart: 25, of which 9 were waited for; matrix products, arithmetic and copies ran while one was open for 0% of the time, Pallas kernels for 18%

profile of v5, /device:TPU:0, one launch (start us, length us, event | category | flops | bytes accessed | tf_op | source)
XLA Modules:
  0.0 88.8 jit_solution(3275248133268483942)
XLA Ops:
  0.5 2.9 %collective-permute-start.6 = (bf16[1024,256]{1,0:T(8,128)(2,1)}, bf16[1024,256]{1,0:T(8,128)(2,1)S(1)}, u32[]{:S(2)}, u32[]{:S(2)}) collective-permute-start(bf16[1024,256]{1,0:T(8,128)(2,1)} %refs_0_.4), channel_id=1, source_target_pairs={{0,2},{2,0},{4,6},{6,4},{8,10},{10,8},{12,14},{14,12},{16,18},{18,... | collective-permute-start | bytes 1572872 | tf_op jit(solution)/shard_map/ppermute | solution.py:278
  3.5 1.6 %collective-permute-start.8 = (bf16[1024,256]{1,0:T(8,128)(2,1)}, bf16[1024,256]{1,0:T(8,128)(2,1)S(1)}, u32[]{:S(2)}, u32[]{:S(2)}) collective-permute-start(bf16[1024,256]{1,0:T(8,128)(2,1)} %refs_0_.4), channel_id=1, source_target_pairs={{0,8},{2,10},{4,12},{6,14},{8,0},{10,2},{12,4},{14,6},{16,24},{18,... | collective-permute-start | bytes 1572872 | tf_op jit(solution)/shard_map/ppermute | solution.py:278
  5.0 1.9 %copy-done.1 = bf16[96,128,128]{2,1,0:T(8,128)(2,1)S(1)} copy-done((bf16[96,128,128]{2,1,0:T(8,128)(2,1)S(1)}, bf16[96,128,128]{2,1,0:T(8,128)(2,1)}, u32[]{:S(2)}) %copy-start.1) | copy-done | bytes 3145752
  6.9 0.7 copy-done.5
  7.6 0.7 copy-done.6
  9.6 3.6 %pack.1 = (bf16[29,64,128]{2,1,0:T(8,128)(2,1)S(1)}, bf16[29,64,128]{2,1,0:T(8,128)(2,1)S(1)}, bf16[29,64,128]{2,1,0:T(8,128)(2,1)S(1)}, bf16[29,32,128]{2,1,0:T(8,128)(2,1)S(1)}, bf16[34,32,128]{2,1,0:T(8,128)(2,1)S(1)}) custom-call(s32[96]{0:T(128)S(1)} %bitcast.1, s32[96]{0:T(128)S(1)} %copy-done.6, s32[96]{0:T(128)S(1)} %copy-done.7, s32[96]{0:T(128)S(1)} %copy-done.8, ...), custom_call_target="tpu_custom_call" | custom-call | bytes 22140000 | tf_op jit(solution)/shard_map/pack/pallas_call | solution.py:294
  13.2 1.6 %collective-permute-start.3 = (bf16[29,64,128]{2,1,0:T(8,128)(2,1)S(1)}, bf16[29,64,128]{2,1,0:T(8,128)(2,1)S(1)}, u32[]{:S(2)}, u32[]{:S(2)}) collective-permute-start(bf16[29,64,128]{2,1,0:T(8,128)(2,1)S(1)} %get-tuple-element.41), channel_id=1, source_target_pairs={{0,2},{2,0},{4,6},{6,4},{8,10},{10,8},{12,14},{14,12},{16,18},{18,... | collective-permute-start | bytes 1425416 | tf_op jit(solution)/shard_map/ppermute | solution.py:278
  14.7 1.6 %collective-permute-start.4 = (bf16[29,64,128]{2,1,0:T(8,128)(2,1)S(1)}, bf16[29,64,128]{2,1,0:T(8,128)(2,1)S(1)}, u32[]{:S(2)}, u32[]{:S(2)}) collective-permute-start(bf16[29,64,128]{2,1,0:T(8,128)(2,1)S(1)} %get-tuple-element.42), channel_id=1, source_target_pairs={{0,8},{2,10},{4,12},{6,14},{8,0},{10,2},{12,4},{14,6},{16,24},{18,... | collective-permute-start | bytes 1425416 | tf_op jit(solution)/shard_map/ppermute | solution.py:278
  16.3 1.4 %collective-permute-start.7 = (bf16[512,256]{1,0:T(8,128)(2,1)S(1)}, bf16[512,256]{1,0:T(8,128)(2,1)S(1)}, u32[]{:S(2)}, u32[]{:S(2)}) collective-permute-start(bf16[512,256]{1,0:T(8,128)(2,1)S(1)} %slice.12), channel_id=1, source_target_pairs={{0,8},{2,10},{4,12},{6,14},{8,0},{10,2},{12,4},{14,6},{16,24},{18,... | collective-permute-start | bytes 786440 | tf_op jit(solution)/shard_map/ppermute | solution.py:278
  17.8 1.6 %collective-permute-start.9 = (bf16[512,256]{1,0:T(8,128)(2,1)S(1)}, bf16[512,256]{1,0:T(8,128)(2,1)S(1)}, u32[]{:S(2)}, u32[]{:S(2)}) collective-permute-start(bf16[512,256]{1,0:T(8,128)(2,1)S(1)} %slice.13), channel_id=1, source_target_pairs={{0,2},{2,0},{4,6},{6,4},{8,10},{10,8},{12,14},{14,12},{16,18},{18,... | collective-permute-start | bytes 786440 | tf_op jit(solution)/shard_map/ppermute | solution.py:278
  19.3 13.7 %collective-permute-done.7 = bf16[512,256]{1,0:T(8,128)(2,1)S(1)} collective-permute-done((bf16[512,256]{1,0:T(8,128)(2,1)S(1)}, bf16[512,256]{1,0:T(8,128)(2,1)S(1)}, u32[]{:S(2)}, u32[]{:S(2)}) %collective-permute-start.7) | collective-permute-done | bytes 262176 | tf_op jit(solution)/shard_map/ppermute | solution.py:278
  33.9 1.5 %collective-permute-start.5 = (bf16[29,32,128]{2,1,0:T(8,128)(2,1)S(1)}, bf16[29,32,128]{2,1,0:T(8,128)(2,1)S(1)}, u32[]{:S(2)}, u32[]{:S(2)}) collective-permute-start(bf16[29,32,128]{2,1,0:T(8,128)(2,1)S(1)} %get-tuple-element.43), channel_id=1, source_target_pairs={{0,10},{2,8},{4,14},{6,12},{8,2},{10,0},{12,6},{14,4},{16,26},{18,... | collective-permute-start | bytes 712712 | tf_op jit(solution)/shard_map/ppermute | solution.py:278
  35.8 3.7 %first_products.1.before = f32[32,64,512]{2,1,0:T(8,128)S(1)} custom-call(bf16[29,64,128]{2,1,0:T(8,128)(2,1)S(1)} %get-tuple-element.38.refs_0_, bf16[29,64,128]{2,1,0:T(8,128)(2,1)S(1)} %collective-permute-done.3.refs_1_, bf16[29,64,128]{2,1,0:T(8,128)(2,1)S(1)} %collective-permute-done.4.refs_2_, bf16[1024,256]{1,0:T(8,128)(2,1)S(1)} %copy-done, ...), custom_call_target="tpu_custom_call" | custom-call | bytes 14760000 | tf_op jit(solution)/shard_map/first_products/pallas_call | solution.py:322
  39.6 1.6 %collective-permute-start.13 = (bf16[34,32,128]{2,1,0:T(8,128)(2,1)S(1)}, bf16[34,32,128]{2,1,0:T(8,128)(2,1)S(1)}, u32[]{:S(2)}, u32[]{:S(2)}) collective-permute-start(bf16[34,32,128]{2,1,0:T(8,128)(2,1)S(1)} %get-tuple-element.52), channel_id=1, source_target_pairs={{0,10},{2,8},{4,14},{6,12},{8,2},{10,0},{12,6},{14,4},{16,26},{18,... | collective-permute-start | bytes 835592 | tf_op jit(solution)/shard_map/ppermute | solution.py:278
  41.2 1.7 %collective-permute-done.5.labels.basis = bf16[29,32,128]{2,1,0:T(8,128)(2,1)S(1)} collective-permute-done((bf16[29,32,128]{2,1,0:T(8,128)(2,1)S(1)}, bf16[29,32,128]{2,1,0:T(8,128)(2,1)S(1)}, u32[]{:S(2)}, u32[]{:S(2)}) %collective-permute-start.5) | collective-permute-done | bytes 237600 | tf_op jit(solution)/shard_map/ppermute | solution.py:278
  42.9 2.0 %last_products.2 = (bf16[1,8,32,512]{3,2,1,0:T(8,128)(2,1)S(1)}, bf16[1,8,32,512]{3,2,1,0:T(8,128)(2,1)S(1)}, bf16[1,8,32,512]{3,2,1,0:T(8,128)(2,1)S(1)}, bf16[1,8,32,512]{3,2,1,0:T(8,128)(2,1)S(1)}) custom-call(bf16[29,32,128]{2,1,0:T(8,128)(2,1)S(1)} %collective-permute-done.5.labels.basis, bf16[29,32,128]{2,1,0:T(8,128)(2,1)S(1)} %collective-permute-done.5.labels.basis, ...), custom_call_target="tpu_custom_call" | custom-call | bytes 7380000 | tf_op jit(solution)/shard_map/last_products/pallas_call | solution.py:346
  44.9 1.6 %collective-permute-start.16 = (bf16[1,8,32,512]{3,2,1,0:T(8,128)(2,1)S(1)}, bf16[1,8,32,512]{3,2,1,0:T(8,128)(2,1)S(1)}, u32[]{:S(2)}, u32[]{:S(2)}) collective-permute-start(bf16[1,8,32,512]{3,2,1,0:T(8,128)(2,1)S(1)} %get-tuple-element.56), channel_id=1, source_target_pairs={{0,4},{2,6},{4,0},{6,2},{8,12},{10,14},{12,8},{14,10},{16,20},{18,... | collective-permute-start | bytes 786440 | tf_op jit(solution)/shard_map/ppermute | solution.py:281
  46.4 2.8 %collective-permute-done.13.basis = bf16[34,32,128]{2,1,0:T(8,128)(2,1)S(1)} collective-permute-done((bf16[34,32,128]{2,1,0:T(8,128)(2,1)S(1)}, bf16[34,32,128]{2,1,0:T(8,128)(2,1)S(1)}, u32[]{:S(2)}, u32[]{:S(2)}) %collective-permute-start.13) | collective-permute-done | bytes 278560 | tf_op jit(solution)/shard_map/ppermute | solution.py:278
  49.3 1.9 %last_products.3 = (bf16[1,8,32,512]{3,2,1,0:T(8,128)(2,1)S(1)}, bf16[1,8,32,512]{3,2,1,0:T(8,128)(2,1)S(1)}, bf16[1,8,32,512]{3,2,1,0:T(8,128)(2,1)S(1)}, bf16[1,8,32,512]{3,2,1,0:T(8,128)(2,1)S(1)}) custom-call(bf16[29,32,128]{2,1,0:T(8,128)(2,1)S(1)} %collective-permute-done.5.labels.basis, bf16[34,32,128]{2,1,0:T(8,128)(2,1)S(1)} %collective-permute-done.13.basis, ...), custom_call_target="tpu_custom_call" | custom-call | bytes 7380000 | tf_op jit(solution)/shard_map/last_products/pallas_call | solution.py:346
  51.2 1.6 %collective-permute-start.14 = (bf16[1,8,32,512]{3,2,1,0:T(8,128)(2,1)S(1)}, bf16[1,8,32,512]{3,2,1,0:T(8,128)(2,1)S(1)}, u32[]{:S(2)}, u32[]{:S(2)}) collective-permute-start(bf16[1,8,32,512]{3,2,1,0:T(8,128)(2,1)S(1)} %get-tuple-element.53), channel_id=1, source_target_pairs={{0,4},{2,6},{4,0},{6,2},{8,12},{10,14},{12,8},{14,10},{16,20},{18,... | collective-permute-start | bytes 786440 | tf_op jit(solution)/shard_map/ppermute | solution.py:281
  52.9 2.7 %collective-permute-start.17 = (bf16[1,8,32,512]{3,2,1,0:T(8,128)(2,1)S(1)}, bf16[1,8,32,512]{3,2,1,0:T(8,128)(2,1)S(1)}, u32[]{:S(2)}, u32[]{:S(2)}) collective-permute-start(bf16[1,8,32,512]{3,2,1,0:T(8,128)(2,1)S(1)} %add_convert_fusion.1), channel_id=1, source_target_pairs={{0,16},{2,18},{4,20},{6,22},{8,24},{10,26},{12,28},{14,30},{16,0},... | collective-permute-start | bytes 786440 | tf_op jit(solution)/shard_map/ppermute | solution.py:281
  55.6 3.3 %collective-permute-done.14 = bf16[1,8,32,512]{3,2,1,0:T(8,128)(2,1)S(1)} collective-permute-done((bf16[1,8,32,512]{3,2,1,0:T(8,128)(2,1)S(1)}, bf16[1,8,32,512]{3,2,1,0:T(8,128)(2,1)S(1)}, u32[]{:S(2)}, u32[]{:S(2)}) %collective-permute-start.14) | collective-permute-done | bytes 262176 | tf_op jit(solution)/shard_map/ppermute | solution.py:281
  58.8 1.5 %collective-permute-start.18 = (bf16[1,8,32,512]{3,2,1,0:T(8,128)(2,1)S(1)}, bf16[1,8,32,512]{3,2,1,0:T(8,128)(2,1)S(1)}, u32[]{:S(2)}, u32[]{:S(2)}) collective-permute-start(bf16[1,8,32,512]{3,2,1,0:T(8,128)(2,1)S(1)} %get-tuple-element.59), channel_id=1, source_target_pairs={{0,4},{2,6},{4,0},{6,2},{8,12},{10,14},{12,8},{14,10},{16,20},{18,... | collective-permute-start | bytes 786440 | tf_op jit(solution)/shard_map/ppermute | solution.py:281
  61.0 2.6 %collective-permute-start.19 = (bf16[1,4,32,512]{3,2,1,0:T(8,128)(2,1)S(1)}, bf16[1,4,32,512]{3,2,1,0:T(8,128)(2,1)S(1)}, u32[]{:S(2)}, u32[]{:S(2)}) collective-permute-start(bf16[1,4,32,512]{3,2,1,0:T(8,128)(2,1)S(1)} %get-tuple-element.70), channel_id=1, source_target_pairs={{0,16},{2,18},{4,20},{6,22},{8,24},{10,26},{12,28},{14,30},{16,0},... | collective-permute-start | bytes 393224 | tf_op jit(solution)/shard_map/ppermute | solution.py:281
  63.6 7.1 %collective-permute-done.17.refs_4_ = bf16[1,8,32,512]{3,2,1,0:T(8,128)(2,1)S(1)} collective-permute-done((bf16[1,8,32,512]{3,2,1,0:T(8,128)(2,1)S(1)}, bf16[1,8,32,512]{3,2,1,0:T(8,128)(2,1)S(1)}, u32[]{:S(2)}, u32[]{:S(2)}) %collective-permute-start.17) | collective-permute-done | bytes 262176 | tf_op jit(solution)/shard_map/ppermute | solution.py:281
  70.7 1.9 %collective-permute-done.19.refs_7_ = bf16[1,4,32,512]{3,2,1,0:T(8,128)(2,1)S(1)} collective-permute-done((bf16[1,4,32,512]{3,2,1,0:T(8,128)(2,1)S(1)}, bf16[1,4,32,512]{3,2,1,0:T(8,128)(2,1)S(1)}, u32[]{:S(2)}, u32[]{:S(2)}) %collective-permute-start.19) | collective-permute-done | bytes 131104 | tf_op jit(solution)/shard_map/ppermute | solution.py:281
  72.8 0.9 collective-permute-start.20
  73.7 7.4 %collective-permute-start.21 = (bf16[2,64,512]{2,1,0:T(8,128)(2,1)S(1)}, bf16[2,64,512]{2,1,0:T(8,128)(2,1)S(1)}, u32[]{:S(2)}, u32[]{:S(2)}) collective-permute-start(bf16[2,64,512]{2,1,0:T(8,128)(2,1)S(1)} %get-tuple-element.63), channel_id=1, source_target_pairs={{0,30},{2,4},{4,2},{6,8},{8,6},{10,12},{12,10},{14,16},{16,14},{18... | collective-permute-start | bytes 393224 | tf_op jit(solution)/shard_map/ppermute | solution.py:410
  81.9 2.2 %mlp.3 = (bf16[4,64,256]{2,1,0:T(8,128)(2,1)S(1)}, bf16[4,64,256]{2,1,0:T(8,128)(2,1)S(1)}) custom-call(s32[8]{0:T(128)S(1)} %copy-done.4, s32[1]{0:T(128)S(6)} %copy.12.valid, bf16[4,64,512]{2,1,0:T(8,128)(2,1)S(1)} %combine.3.combined, bf16[3,512,256]{2,1,0:T(8,128)(2,1)S(1)} %copy-done.2, bf16[3,512,256]{2,1,0:T(8,128)(2,1)S(1)} %collective-permute-done.refs_3_.refs_1_, ...), custom_call_target="tpu_custom_call" | custom-call | bytes 7380000 | tf_op jit(solution)/shard_map/mlp/pallas_call | solution.py:414
  84.4 2.2 %mlp.2 = (bf16[4,64,256]{2,1,0:T(8,128)(2,1)S(1)}, bf16[4,64,256]{2,1,0:T(8,128)(2,1)S(1)}) custom-call(s32[8]{0:T(128)S(1)} %copy-done.4, s32[1]{0:T(128)S(6)} %copy.12.valid, bf16[4,64,512]{2,1,0:T(8,128)(2,1)S(1)} %get-tuple-element.61.combined, bf16[2,64,512]{2,1,0:T(8,128)(2,1)S(1)} %collective-permute-done.20.refs_0_, ...), custom_call_target="tpu_custom_call" | custom-call | bytes 7380000 | tf_op jit(solution)/shard_map/mlp/pallas_call | solution.py:414
  86.9 1.0 %collective-permute-done.23.refs_2_ = bf16[4,64,256]{2,1,0:T(8,128)(2,1)S(1)} collective-permute-done((bf16[4,64,256]{2,1,0:T(8,128)(2,1)S(1)}, bf16[4,64,256]{2,1,0:T(8,128)(2,1)S(1)}, u32[]{:S(2)}, u32[]{:S(2)}) %collective-permute-start.23) | collective-permute-done | bytes 131104 | tf_op jit(solution)/shard_map/ppermute | solution.py:284
  88.0 0.8 join.1
  (52 shorter events, 4.7 us)
Async XLA Ops:
  0.0 19.3 %copy-start = (bf16[1024,256]{1,0:T(8,128)(2,1)S(1)}, bf16[1024,256]{1,0:T(8,128)(2,1)}, u32[]{:S(2)}) copy-start(bf16[1024,256]{1,0:T(8,128)(2,1)} %refs_0_.4) | copy-start | bytes 1572868
  0.0 5.0 %collective-permute-start = (bf16[3,512,256]{2,1,0:T(8,128)(2,1)}, bf16[3,512,256]{2,1,0:T(8,128)(2,1)S(1)}, u32[]{:S(2)}, u32[]{:S(2)}) collective-permute-start(bf16[3,512,256]{2,1,0:T(8,128)(2,1)} %refs_0_.5), channel_id=1, source_target_pairs={{0,1},{1,0},{2,3},{3,2},{4,5},{5,4},{6,7},{7,6},{8,9},{9,8},{10,11... | collective-permute-start | bytes 2359304 | tf_op jit(solution)/shard_map/ppermute | solution.py:284
  0.5 4.6 %collective-permute-start.1 = (bf16[3,256,512]{2,1,0:T(8,128)(2,1)}, bf16[3,256,512]{2,1,0:T(8,128)(2,1)S(1)}, u32[]{:S(2)}, u32[]{:S(2)}) collective-permute-start(bf16[3,256,512]{2,1,0:T(8,128)(2,1)} %refs_2_.3), channel_id=1, source_target_pairs={{0,1},{1,0},{2,3},{3,2},{4,5},{5,4},{6,7},{7,6},{8,9},{9,8},{10,11... | collective-permute-start | bytes 2359304 | tf_op jit(solution)/shard_map/ppermute | solution.py:284
  0.5 15.8 %collective-permute-start.6 = (bf16[1024,256]{1,0:T(8,128)(2,1)}, bf16[1024,256]{1,0:T(8,128)(2,1)S(1)}, u32[]{:S(2)}, u32[]{:S(2)}) collective-permute-start(bf16[1024,256]{1,0:T(8,128)(2,1)} %refs_0_.4), channel_id=1, source_target_pairs={{0,2},{2,0},{4,6},{6,4},{8,10},{10,8},{12,14},{14,12},{16,18},{18,... | collective-permute-start | bytes 1572872 | tf_op jit(solution)/shard_map/ppermute | solution.py:278
  3.5 14.3 %collective-permute-start.8 = (bf16[1024,256]{1,0:T(8,128)(2,1)}, bf16[1024,256]{1,0:T(8,128)(2,1)S(1)}, u32[]{:S(2)}, u32[]{:S(2)}) collective-permute-start(bf16[1024,256]{1,0:T(8,128)(2,1)} %refs_0_.4), channel_id=1, source_target_pairs={{0,8},{2,10},{4,12},{6,14},{8,0},{10,2},{12,4},{14,6},{16,24},{18,... | collective-permute-start | bytes 1572872 | tf_op jit(solution)/shard_map/ppermute | solution.py:278
  5.0 1.9 %copy-start.1 = (bf16[96,128,128]{2,1,0:T(8,128)(2,1)S(1)}, bf16[96,128,128]{2,1,0:T(8,128)(2,1)}, u32[]{:S(2)}) copy-start(bf16[96,128,128]{2,1,0:T(8,128)(2,1)} %basis) | copy-start | bytes 9437188
  6.9 0.7 copy-start.5
  7.6 0.7 copy-start.6
  13.2 19.9 %collective-permute-start.3 = (bf16[29,64,128]{2,1,0:T(8,128)(2,1)S(1)}, bf16[29,64,128]{2,1,0:T(8,128)(2,1)S(1)}, u32[]{:S(2)}, u32[]{:S(2)}) collective-permute-start(bf16[29,64,128]{2,1,0:T(8,128)(2,1)S(1)} %get-tuple-element.41), channel_id=1, source_target_pairs={{0,2},{2,0},{4,6},{6,4},{8,10},{10,8},{12,14},{14,12},{16,18},{18,... | collective-permute-start | bytes 1425416 | tf_op jit(solution)/shard_map/ppermute | solution.py:278
  14.7 18.4 %collective-permute-start.4 = (bf16[29,64,128]{2,1,0:T(8,128)(2,1)S(1)}, bf16[29,64,128]{2,1,0:T(8,128)(2,1)S(1)}, u32[]{:S(2)}, u32[]{:S(2)}) collective-permute-start(bf16[29,64,128]{2,1,0:T(8,128)(2,1)S(1)} %get-tuple-element.42), channel_id=1, source_target_pairs={{0,8},{2,10},{4,12},{6,14},{8,0},{10,2},{12,4},{14,6},{16,24},{18,... | collective-permute-start | bytes 1425416 | tf_op jit(solution)/shard_map/ppermute | solution.py:278
  16.3 16.7 %collective-permute-start.7 = (bf16[512,256]{1,0:T(8,128)(2,1)S(1)}, bf16[512,256]{1,0:T(8,128)(2,1)S(1)}, u32[]{:S(2)}, u32[]{:S(2)}) collective-permute-start(bf16[512,256]{1,0:T(8,128)(2,1)S(1)} %slice.12), channel_id=1, source_target_pairs={{0,8},{2,10},{4,12},{6,14},{8,0},{10,2},{12,4},{14,6},{16,24},{18,... | collective-permute-start | bytes 786440 | tf_op jit(solution)/shard_map/ppermute | solution.py:278
  17.8 15.9 %collective-permute-start.9 = (bf16[512,256]{1,0:T(8,128)(2,1)S(1)}, bf16[512,256]{1,0:T(8,128)(2,1)S(1)}, u32[]{:S(2)}, u32[]{:S(2)}) collective-permute-start(bf16[512,256]{1,0:T(8,128)(2,1)S(1)} %slice.13), channel_id=1, source_target_pairs={{0,2},{2,0},{4,6},{6,4},{8,10},{10,8},{12,14},{14,12},{16,18},{18,... | collective-permute-start | bytes 786440 | tf_op jit(solution)/shard_map/ppermute | solution.py:278
  19.3 16.1 %collective-permute-start.2 = (bf16[1024,256]{1,0:T(8,128)(2,1)S(1)}, bf16[1024,256]{1,0:T(8,128)(2,1)S(1)}, u32[]{:S(2)}, u32[]{:S(2)}) collective-permute-start(bf16[1024,256]{1,0:T(8,128)(2,1)S(1)} %copy-done), channel_id=1, source_target_pairs={{0,1},{1,0},{2,3},{3,2},{4,5},{5,4},{6,7},{7,6},{8,9},{9,8},{10,11... | collective-permute-start | bytes 1572872 | tf_op jit(solution)/shard_map/ppermute | solution.py:284
  33.1 2.3 %collective-permute-start.11 = (bf16[1024,256]{1,0:T(8,128)(2,1)S(1)}, bf16[1024,256]{1,0:T(8,128)(2,1)S(1)}, u32[]{:S(2)}, u32[]{:S(2)}) collective-permute-start(bf16[1024,256]{1,0:T(8,128)(2,1)S(1)} %collective-permute-done.6.refs_4_), channel_id=1, source_target_pairs={{0,1},{1,0},{2,3},{3,2},{4,5},{5,4},{6,7},{7,6},{8,9},{9,8},{10,11... | collective-permute-start | bytes 1572872 | tf_op jit(solution)/shard_map/ppermute | solution.py:284
  33.2 2.6 %collective-permute-start.12 = (bf16[1024,256]{1,0:T(8,128)(2,1)S(1)}, bf16[1024,256]{1,0:T(8,128)(2,1)S(1)}, u32[]{:S(2)}, u32[]{:S(2)}) collective-permute-start(bf16[1024,256]{1,0:T(8,128)(2,1)S(1)} %collective-permute-done.8.refs_5_), channel_id=1, source_target_pairs={{0,1},{1,0},{2,3},{3,2},{4,5},{5,4},{6,7},{7,6},{8,9},{9,8},{10,11... | collective-permute-start | bytes 1572872 | tf_op jit(solution)/shard_map/ppermute | solution.py:284
  33.7 9.2 %collective-permute-start.10 = (bf16[1024,256]{1,0:T(8,128)(2,1)S(1)}, bf16[1024,256]{1,0:T(8,128)(2,1)S(1)}, u32[]{:S(2)}, u32[]{:S(2)}) collective-permute-start(bf16[1024,256]{1,0:T(8,128)(2,1)S(1)} %constant_dynamic-update-slice_fusion.mine), channel_id=1, source_target_pairs={{0,1},{1,0},{2,3},{3,2},{4,5},{5,4},{6,7},{7,6},{8,9},{9,8},{10,11... | collective-permute-start | bytes 1572872 | tf_op jit(solution)/shard_map/ppermute | solution.py:284
  33.9 9.0 %collective-permute-start.5 = (bf16[29,32,128]{2,1,0:T(8,128)(2,1)S(1)}, bf16[29,32,128]{2,1,0:T(8,128)(2,1)S(1)}, u32[]{:S(2)}, u32[]{:S(2)}) collective-permute-start(bf16[29,32,128]{2,1,0:T(8,128)(2,1)S(1)} %get-tuple-element.43), channel_id=1, source_target_pairs={{0,10},{2,8},{4,14},{6,12},{8,2},{10,0},{12,6},{14,4},{16,26},{18,... | collective-permute-start | bytes 712712 | tf_op jit(solution)/shard_map/ppermute | solution.py:278
  39.6 9.7 %collective-permute-start.13 = (bf16[34,32,128]{2,1,0:T(8,128)(2,1)S(1)}, bf16[34,32,128]{2,1,0:T(8,128)(2,1)S(1)}, u32[]{:S(2)}, u32[]{:S(2)}) collective-permute-start(bf16[34,32,128]{2,1,0:T(8,128)(2,1)S(1)} %get-tuple-element.52), channel_id=1, source_target_pairs={{0,10},{2,8},{4,14},{6,12},{8,2},{10,0},{12,6},{14,4},{16,26},{18,... | collective-permute-start | bytes 835592 | tf_op jit(solution)/shard_map/ppermute | solution.py:278
  44.9 8.0 %collective-permute-start.16 = (bf16[1,8,32,512]{3,2,1,0:T(8,128)(2,1)S(1)}, bf16[1,8,32,512]{3,2,1,0:T(8,128)(2,1)S(1)}, u32[]{:S(2)}, u32[]{:S(2)}) collective-permute-start(bf16[1,8,32,512]{3,2,1,0:T(8,128)(2,1)S(1)} %get-tuple-element.56), channel_id=1, source_target_pairs={{0,4},{2,6},{4,0},{6,2},{8,12},{10,14},{12,8},{14,10},{16,20},{18,... | collective-permute-start | bytes 786440 | tf_op jit(solution)/shard_map/ppermute | solution.py:281
  51.2 30.7 %copy-start.2 = (bf16[3,512,256]{2,1,0:T(8,128)(2,1)S(1)}, bf16[3,512,256]{2,1,0:T(8,128)(2,1)}, u32[]{:S(2)}) copy-start(bf16[3,512,256]{2,1,0:T(8,128)(2,1)} %refs_0_.5) | copy-start | bytes 2359300
  51.2 30.7 %copy-start.3 = (bf16[3,256,512]{2,1,0:T(8,128)(2,1)S(1)}, bf16[3,256,512]{2,1,0:T(8,128)(2,1)}, u32[]{:S(2)}) copy-start(bf16[3,256,512]{2,1,0:T(8,128)(2,1)} %refs_2_.3) | copy-start | bytes 2359300
  51.2 30.7 %copy-start.4 = (s32[8]{0:T(128)S(1)}, s32[8]{0:T(128)}, u32[]{:S(2)}) copy-start(s32[8]{0:T(128)} %reverse.3) | copy-start | bytes 100
  51.2 7.6 %collective-permute-start.14 = (bf16[1,8,32,512]{3,2,1,0:T(8,128)(2,1)S(1)}, bf16[1,8,32,512]{3,2,1,0:T(8,128)(2,1)S(1)}, u32[]{:S(2)}, u32[]{:S(2)}) collective-permute-start(bf16[1,8,32,512]{3,2,1,0:T(8,128)(2,1)S(1)} %get-tuple-element.53), channel_id=1, source_target_pairs={{0,4},{2,6},{4,0},{6,2},{8,12},{10,14},{12,8},{14,10},{16,20},{18,... | collective-permute-start | bytes 786440 | tf_op jit(solution)/shard_map/ppermute | solution.py:281
  52.9 17.8 %collective-permute-start.17 = (bf16[1,8,32,512]{3,2,1,0:T(8,128)(2,1)S(1)}, bf16[1,8,32,512]{3,2,1,0:T(8,128)(2,1)S(1)}, u32[]{:S(2)}, u32[]{:S(2)}) collective-permute-start(bf16[1,8,32,512]{3,2,1,0:T(8,128)(2,1)S(1)} %add_convert_fusion.1), channel_id=1, source_target_pairs={{0,16},{2,18},{4,20},{6,22},{8,24},{10,26},{12,28},{14,30},{16,0},... | collective-permute-start | bytes 786440 | tf_op jit(solution)/shard_map/ppermute | solution.py:281
  58.8 13.8 %collective-permute-start.18 = (bf16[1,8,32,512]{3,2,1,0:T(8,128)(2,1)S(1)}, bf16[1,8,32,512]{3,2,1,0:T(8,128)(2,1)S(1)}, u32[]{:S(2)}, u32[]{:S(2)}) collective-permute-start(bf16[1,8,32,512]{3,2,1,0:T(8,128)(2,1)S(1)} %get-tuple-element.59), channel_id=1, source_target_pairs={{0,4},{2,6},{4,0},{6,2},{8,12},{10,14},{12,8},{14,10},{16,20},{18,... | collective-permute-start | bytes 786440 | tf_op jit(solution)/shard_map/ppermute | solution.py:281
  60.3 12.3 %collective-permute-start.15 = (bf16[1,8,32,512]{3,2,1,0:T(8,128)(2,1)S(1)}, bf16[1,8,32,512]{3,2,1,0:T(8,128)(2,1)S(1)}, u32[]{:S(2)}, u32[]{:S(2)}) collective-permute-start(bf16[1,8,32,512]{3,2,1,0:T(8,128)(2,1)S(1)} %get-tuple-element.54), channel_id=1, source_target_pairs={{0,4},{2,6},{4,0},{6,2},{8,12},{10,14},{12,8},{14,10},{16,20},{18,... | collective-permute-start | bytes 786440 | tf_op jit(solution)/shard_map/ppermute | solution.py:281
  61.0 11.7 %collective-permute-start.19 = (bf16[1,4,32,512]{3,2,1,0:T(8,128)(2,1)S(1)}, bf16[1,4,32,512]{3,2,1,0:T(8,128)(2,1)S(1)}, u32[]{:S(2)}, u32[]{:S(2)}) collective-permute-start(bf16[1,4,32,512]{3,2,1,0:T(8,128)(2,1)S(1)} %get-tuple-element.70), channel_id=1, source_target_pairs={{0,16},{2,18},{4,20},{6,22},{8,24},{10,26},{12,28},{14,30},{16,0},... | collective-permute-start | bytes 393224 | tf_op jit(solution)/shard_map/ppermute | solution.py:281
  70.7 11.0 %collective-permute-start.22 = (bf16[1,4,32,512]{3,2,1,0:T(8,128)(2,1)S(1)}, bf16[1,4,32,512]{3,2,1,0:T(8,128)(2,1)S(1)}, u32[]{:S(2)}, u32[]{:S(2)}) collective-permute-start(bf16[1,4,32,512]{3,2,1,0:T(8,128)(2,1)S(1)} %get-tuple-element.65), channel_id=1, source_target_pairs={{0,16},{2,18},{4,20},{6,22},{8,24},{10,26},{12,28},{14,30},{16,0},... | collective-permute-start | bytes 393224 | tf_op jit(solution)/shard_map/ppermute | solution.py:281
  72.8 11.4 %collective-permute-start.20 = (bf16[2,64,512]{2,1,0:T(8,128)(2,1)S(1)}, bf16[2,64,512]{2,1,0:T(8,128)(2,1)S(1)}, u32[]{:S(2)}, u32[]{:S(2)}) collective-permute-start(bf16[2,64,512]{2,1,0:T(8,128)(2,1)S(1)} %get-tuple-element.62), channel_id=1, source_target_pairs={{0,2},{2,0},{4,6},{6,4},{8,10},{10,8},{12,14},{14,12},{16,18},{18,... | collective-permute-start | bytes 393224 | tf_op jit(solution)/shard_map/ppermute | solution.py:411
  73.7 10.7 %collective-permute-start.21 = (bf16[2,64,512]{2,1,0:T(8,128)(2,1)S(1)}, bf16[2,64,512]{2,1,0:T(8,128)(2,1)S(1)}, u32[]{:S(2)}, u32[]{:S(2)}) collective-permute-start(bf16[2,64,512]{2,1,0:T(8,128)(2,1)S(1)} %get-tuple-element.63), channel_id=1, source_target_pairs={{0,30},{2,4},{4,2},{6,8},{8,6},{10,12},{12,10},{14,16},{16,14},{18... | collective-permute-start | bytes 393224 | tf_op jit(solution)/shard_map/ppermute | solution.py:410
  84.1 2.8 %collective-permute-start.24 = (bf16[4,64,256]{2,1,0:T(8,128)(2,1)S(1)}, bf16[4,64,256]{2,1,0:T(8,128)(2,1)S(1)}, u32[]{:S(2)}, u32[]{:S(2)}) collective-permute-start(bf16[4,64,256]{2,1,0:T(8,128)(2,1)S(1)} %get-tuple-element.68), channel_id=1, source_target_pairs={{0,1},{1,0},{2,3},{3,2},{4,5},{5,4},{6,7},{7,6},{8,9},{9,8},{10,11... | collective-permute-start | bytes 393224 | tf_op jit(solution)/shard_map/ppermute | solution.py:284
  86.6 1.4 %collective-permute-start.23 = (bf16[4,64,256]{2,1,0:T(8,128)(2,1)S(1)}, bf16[4,64,256]{2,1,0:T(8,128)(2,1)S(1)}, u32[]{:S(2)}, u32[]{:S(2)}) collective-permute-start(bf16[4,64,256]{2,1,0:T(8,128)(2,1)S(1)} %get-tuple-element.67), channel_id=1, source_target_pairs={{0,1},{1,0},{2,3},{3,2},{4,5},{5,4},{6,7},{7,6},{8,9},{9,8},{10,11... | collective-permute-start | bytes 393224 | tf_op jit(solution)/shard_map/ppermute | solution.py:284
  (2 other events, 1.3 us)

commit v6 on v5

--- a/solution.py
+++ b/solution.py
@@ -10,7 +10,9 @@
 MLPS = 3
 BLK = 128
 CHUNKS = 2
-UNROLL = 14
+UNROLL = 28
+LABEL_ROWS = 16
+SPARE = 6
 GRANT = 12 * 1024 * 1024
 
 pair_scale = 0.7071067811865476
@@ -86,8 +88,8 @@
     share = rows * CHUNKS
     first = core * share
     row = lax.broadcasted_iota(jnp.int32, (share, BLK), 0)
-    label_row = lax.broadcasted_iota(jnp.int32, (rows, BLK), 0)
-    lane = lax.broadcasted_iota(jnp.int32, (rows, BLK), 1)
+    label_row = lax.broadcasted_iota(jnp.int32, (LABEL_ROWS, BLK), 0)
+    lane = lax.broadcasted_iota(jnp.int32, (LABEL_ROWS, BLK), 1)
     for k in range(groups):
 
         def one(p, labels):
@@ -105,28 +107,29 @@
             block = basis[s, pl.ds(pl.multiple_of(first, share), share), :]
             block = jnp.where(row + first < count, block, jnp.zeros_like(block))
             if k < groups - 1:
-                whole[k][p] = block
+                whole[k][pl.ds(pl.multiple_of(p * share, share), share), :] = block
             else:
                 for j in range(CHUNKS):
-                    cut[j][p] = block[j * rows : (j + 1) * rows]
+                    at = pl.ds(pl.multiple_of(p * rows, rows), rows)
+                    cut[j][at, :] = block[j * rows : (j + 1) * rows]
             return labels
 
-        labels = lax.fori_loop(0, room, one, jnp.zeros((rows, BLK), jnp.int32), unroll=2)
+        labels = lax.fori_loop(0, room, one, jnp.zeros((LABEL_ROWS, BLK), jnp.int32), unroll=2)
         labels = labels.astype(jnp.float32).astype(jnp.bfloat16)
         if k < groups - 1:
-            whole[k][room, :rows] = labels
+            whole[k][room * share :, :] = labels
         else:
-            cut[0][room] = labels
-
-
-def add_products(room, labels, basis, mine, other, acc, staged, metas, sem):
+            cut[0][room * rows :, :] = labels
+
+
+def add_products(room, height, labels, basis, mine, other, acc, staged, metas, sem):
     sources = len(basis)
     core = lax.axis_index("mp")
     width = mine[0].shape[1]
     own_cols = pl.ds(pl.multiple_of(core * width, width), width)
     other_cols = pl.ds(pl.multiple_of((1 - core) * width, width), width)
     for k in range(sources):
-        staged[k] = labels[k][room, :16, :].astype(jnp.float32).astype(jnp.int32)
+        staged[k] = labels[k][room * height :, :].astype(jnp.float32).astype(jnp.int32)[:8]
     copy = pltpu.make_async_copy(staged, metas, sem)
     copy.start()
     acc[...] = jnp.zeros_like(acc)
@@ -139,7 +142,7 @@
                 p = step * UNROLL + u
                 s = metas[k, 1, p]
                 at = pl.ds(pl.multiple_of(s * BLK, BLK), BLK)
-                left = basis[k][p]
+                left = basis[k][pl.ds(pl.multiple_of(p * height, height), height), :]
                 a = jnp.dot(left, mine[k][at, :], preferred_element_type=jnp.float32)
                 b = jnp.dot(left, other[k][at, :], preferred_element_type=jnp.float32)
                 sums.append((metas[k, 0, p], a, b))
@@ -154,13 +157,14 @@
 def first_kernel(sources, room, *refs):
     basis, mine, other = (refs[i * sources : (i + 1) * sources] for i in range(3))
     acc, staged, metas, sem = refs[3 * sources :]
-    add_products(room, basis, basis, mine, other, acc, staged, metas, sem)
+    height = (basis[0].shape[0] - LABEL_ROWS) // room
+    add_products(room, height, basis, basis, mine, other, acc, staged, metas, sem)
 
 
 def last_kernel(room, blocks, rows, chunk, labels, basis, mine, other, before, *refs):
     keep_low, keep_high, send_low, send_high, acc, staged, metas, sem = refs
     held = slice(chunk * rows, (chunk + 1) * rows)
-    add_products(room, [labels], [basis], [mine], [other], acc, staged, metas, sem)
+    add_products(room, rows, [labels], [basis], [mine], [other], acc, staged, metas, sem)
     part = keep_low.shape[0]
     for i, out in enumerate((keep_low, keep_high, send_low, send_high)):
         for o in range(part):
@@ -207,7 +211,7 @@
         b = start + i
         within = reverse[b] % blocks
         if came is None:
-            pair = combined[within - start]
+            pair = combined[jnp.clip(within - start, 0, count - 1)]
         else:
             w = jnp.clip(within - (border if b < border else 0), 0, border - 1)
             pair = jnp.where(odd == (b < border), came[0][w], came[1][w])
@@ -219,7 +223,7 @@
         total = state[...]
         for w_in, w_out in ((in_own, out_own), (in_other, out_other)):
             value = jnp.dot(layer_input, w_in[layer], preferred_element_type=jnp.float32)
-            hidden = (value / (1.0 + jnp.exp(-value))).astype(jnp.bfloat16)
+            hidden = (0.5 * value * (1.0 + jnp.tanh(0.5 * value))).astype(jnp.bfloat16)
             total = total + jnp.dot(hidden, w_out[layer], preferred_element_type=jnp.float32)
         state[...] = total
     half = width // 2
@@ -287,9 +291,10 @@
     in_other, out_other = swap(weight_in), swap(weight_out)
 
     share = rows * CHUNKS
-    whole_shape = jax.ShapeDtypeStruct((room + 1, share, BLK), bf16)
+    whole_shape = jax.ShapeDtypeStruct((room * share + LABEL_ROWS, BLK), bf16)
     cut_shapes = [
-        jax.ShapeDtypeStruct((room + (1 if j == 0 else 6), rows, BLK), bf16) for j in range(CHUNKS)
+        jax.ShapeDtypeStruct((room * rows + (LABEL_ROWS if j == 0 else SPARE * rows), BLK), bf16)
+        for j in range(CHUNKS)
     ]
     packed = pl.pallas_call(
         functools.partial(pack_kernel, near, far, room, rows, blocks),
@@ -325,8 +330,8 @@
         in_specs=[full(None)] * (3 * last),
         out_specs=full(None),
         scratch_shapes=[
-            pltpu.VMEM((last, 16, BLK), jnp.int32),
-            pltpu.SMEM((last, 16, BLK), jnp.int32),
+            pltpu.VMEM((last, 8, BLK), jnp.int32),
+            pltpu.SMEM((last, 8, BLK), jnp.int32),
             pltpu.SemaphoreType.DMA,
         ],
         compiler_params=grant(CHUNKS * acc_bytes),
@@ -338,11 +343,10 @@
     border_shape = jax.ShapeDtypeStruct((border, share, width), bf16)
     even_pairs = [(i, i ^ 1) for i in range(devices)]
     odd_pairs = [(i, (i + 1 if i % 2 else i - 1) % devices) for i in range(devices)]
-    cut, waited, came_first = [], basis[1:], None
+    cut, waited = [], basis[1:]
     sums, lows, highs = [], [], []
     for chunk in range(CHUNKS):
         cut.append(near_send(after_all(packed[last + chunk], *waited), last))
-        waits = []
         keep_low, keep_high, send_low, send_high = pl.pallas_call(
             functools.partial(last_kernel, room, blocks, rows, chunk),
             out_shape=[part_owners_shape] * 4,
@@ -350,23 +354,22 @@
             out_specs=[full(None)] * 4,
             scratch_shapes=[
                 pltpu.VMEM(acc_shape, jnp.float32),
-                pltpu.VMEM((1, 16, BLK), jnp.int32),
-                pltpu.SMEM((1, 16, BLK), jnp.int32),
+                pltpu.VMEM((1, 8, BLK), jnp.int32),
+                pltpu.SMEM((1, 8, BLK), jnp.int32),
                 pltpu.SemaphoreType.DMA,
             ],
             compiler_params=grant(4 * acc_bytes),
             cost_estimate=spent(2),
             name="last_products",
-        )(cut[0], after_all(cut[chunk], *waits), mine[last], other[last], partial)
+        )(cut[0], cut[chunk], mine[last], other[last], partial)
         waited = [partial]
         came = far_send(send_high, far[0])
-        came_first = (keep_high.astype(jnp.float32) + came.astype(jnp.float32)).astype(bf16)
-        sums.append(came_first)
+        sums.append((keep_high.astype(jnp.float32) + came.astype(jnp.float32)).astype(bf16))
         highs.append(came)
         lows.append((keep_low, send_low))
     lows = [
         (keep_low, far_send(after_all(send_low, highs[-1]), far[0]))
-        for (keep_low, send_low), came in zip(lows, highs)
+        for keep_low, send_low in lows
     ]
     starts = [0, 2 * border]
     stops = [2 * border, blocks]

time: 89 us -> 88.1 us (0.990)
  Pallas kernels: 16.7 us -> 15.3 us
  transfers between devices with their start and end apart: 25 -> 25, of which waited for: 9 -> 10; matrix products, arithmetic and copies ran while one was open for 0% -> 0% of each run, Pallas kernels for 18% -> 16%
where the time goes in v6:
time: 88.1 us; the launch traced here: 87.9 us
  starting transfers between devices  34.1 us (39%)
  waiting for transfers between devices  32.9 us (37%)
  Pallas kernels  15.3 us (17%)
  local copies, waits for them, and re-layouts  4.62 us (5%)
    ppermute x8, waiting for transfers between devices, near_send(): return lax.ppermute(array, 'graph', xor_pairs(devices, near_mask(near, k)))  18.6 us
    ppermute x8, starting transfers between devices, near_send(): return lax.ppermute(array, 'graph', xor_pairs(devices, near_mask(near, k)))  13.7 us
    ppermute x7, waiting for transfers between devices, far_send(): return lax.ppermute(array, 'graph', xor_pairs(devices, 1 << bit))  12.6 us
    ppermute x7, starting transfers between devices, far_send(): return lax.ppermute(array, 'graph', xor_pairs(devices, 1 << bit))  10.5 us
    ppermute x1, starting transfers between devices, local(): lax.ppermute(outs[2], 'graph', odd_pairs)  7.59 us
    unnamed x19, local copies, waits for them, and re-layouts  4.55 us
    pallas_call x2, Pallas kernels, local(): pl.pallas_call(functools.partial(mlp_kernel, border, start, blocks), out_...  4.31 us
    pallas_call x1, Pallas kernels, local(): pl.pallas_call(functools.partial(pack_kernel, near, far, room, rows, bloc...  3.64 us
  transfers between devices with their start and end apart: 25, of which 10 were waited for; matrix products, arithmetic and copies ran while one was open for 0% of the time, Pallas kernels for 16%

profile of v6, /device:TPU:0, one launch (start us, length us, event | category | flops | bytes accessed | tf_op | source)
XLA Modules:
  0.0 87.9 jit_solution(14927967001229518468)
XLA Ops:
  0.5 2.9 %collective-permute-start.6 = (bf16[1024,256]{1,0:T(8,128)(2,1)}, bf16[1024,256]{1,0:T(8,128)(2,1)S(1)}, u32[]{:S(2)}, u32[]{:S(2)}) collective-permute-start(bf16[1024,256]{1,0:T(8,128)(2,1)} %refs_0_.4), channel_id=1, source_target_pairs={{0,2},{2,0},{4,6},{6,4},{8,10},{10,8},{12,14},{14,12},{16,18},{18,... | collective-permute-start | bytes 1572872 | tf_op jit(solution)/shard_map/ppermute | solution.py:282
  3.5 1.6 %collective-permute-start.8 = (bf16[1024,256]{1,0:T(8,128)(2,1)}, bf16[1024,256]{1,0:T(8,128)(2,1)S(1)}, u32[]{:S(2)}, u32[]{:S(2)}) collective-permute-start(bf16[1024,256]{1,0:T(8,128)(2,1)} %refs_0_.4), channel_id=1, source_target_pairs={{0,8},{2,10},{4,12},{6,14},{8,0},{10,2},{12,4},{14,6},{16,24},{18,... | collective-permute-start | bytes 1572872 | tf_op jit(solution)/shard_map/ppermute | solution.py:282
  5.0 1.9 %copy-done.1 = bf16[96,128,128]{2,1,0:T(8,128)(2,1)S(1)} copy-done((bf16[96,128,128]{2,1,0:T(8,128)(2,1)S(1)}, bf16[96,128,128]{2,1,0:T(8,128)(2,1)}, u32[]{:S(2)}) %copy-start.1) | copy-done | bytes 3145752
  6.9 0.7 copy-done.5
  7.6 0.7 copy-done.6
  8.9 0.7 copy-done.8
  9.6 3.6 %pack.1 = (bf16[1808,128]{1,0:T(8,128)(2,1)S(1)}, bf16[1808,128]{1,0:T(8,128)(2,1)S(1)}, bf16[1808,128]{1,0:T(8,128)(2,1)S(1)}, bf16[912,128]{1,0:T(8,128)(2,1)S(1)}, bf16[1088,128]{1,0:T(8,128)(2,1)S(1)}) custom-call(s32[96]{0:T(128)S(1)} %bitcast.1, s32[96]{0:T(128)S(1)} %copy-done.6, s32[96]{0:T(128)S(1)} %copy-done.7, s32[96]{0:T(128)S(1)} %copy-done.8, ...), custom_call_target="tpu_custom_call" | custom-call | bytes 22140000 | tf_op jit(solution)/shard_map/pack/pallas_call | solution.py:299
  13.2 1.6 %collective-permute-start.3 = (bf16[1808,128]{1,0:T(8,128)(2,1)S(1)}, bf16[1808,128]{1,0:T(8,128)(2,1)S(1)}, u32[]{:S(2)}, u32[]{:S(2)}) collective-permute-start(bf16[1808,128]{1,0:T(8,128)(2,1)S(1)} %get-tuple-element.41), channel_id=1, source_target_pairs={{0,2},{2,0},{4,6},{6,4},{8,10},{10,8},{12,14},{14,12},{16,18},{18,... | collective-permute-start | bytes 1388552 | tf_op jit(solution)/shard_map/ppermute | solution.py:282
  14.8 1.6 %collective-permute-start.4 = (bf16[1808,128]{1,0:T(8,128)(2,1)S(1)}, bf16[1808,128]{1,0:T(8,128)(2,1)S(1)}, u32[]{:S(2)}, u32[]{:S(2)}) collective-permute-start(bf16[1808,128]{1,0:T(8,128)(2,1)S(1)} %get-tuple-element.42), channel_id=1, source_target_pairs={{0,8},{2,10},{4,12},{6,14},{8,0},{10,2},{12,4},{14,6},{16,24},{18,... | collective-permute-start | bytes 1388552 | tf_op jit(solution)/shard_map/ppermute | solution.py:282
  16.4 1.3 %collective-permute-start.7 = (bf16[512,256]{1,0:T(8,128)(2,1)S(1)}, bf16[512,256]{1,0:T(8,128)(2,1)S(1)}, u32[]{:S(2)}, u32[]{:S(2)}) collective-permute-start(bf16[512,256]{1,0:T(8,128)(2,1)S(1)} %slice.12), channel_id=1, source_target_pairs={{0,8},{2,10},{4,12},{6,14},{8,0},{10,2},{12,4},{14,6},{16,24},{18,... | collective-permute-start | bytes 786440 | tf_op jit(solution)/shard_map/ppermute | solution.py:282
  17.8 1.6 %collective-permute-start.9 = (bf16[512,256]{1,0:T(8,128)(2,1)S(1)}, bf16[512,256]{1,0:T(8,128)(2,1)S(1)}, u32[]{:S(2)}, u32[]{:S(2)}) collective-permute-start(bf16[512,256]{1,0:T(8,128)(2,1)S(1)} %slice.13), channel_id=1, source_target_pairs={{0,2},{2,0},{4,6},{6,4},{8,10},{10,8},{12,14},{14,12},{16,18},{18,... | collective-permute-start | bytes 786440 | tf_op jit(solution)/shard_map/ppermute | solution.py:282
  19.3 13.5 %collective-permute-done.7 = bf16[512,256]{1,0:T(8,128)(2,1)S(1)} collective-permute-done((bf16[512,256]{1,0:T(8,128)(2,1)S(1)}, bf16[512,256]{1,0:T(8,128)(2,1)S(1)}, u32[]{:S(2)}, u32[]{:S(2)}) %collective-permute-start.7) | collective-permute-done | bytes 262176 | tf_op jit(solution)/shard_map/ppermute | solution.py:282
  33.6 1.5 %collective-permute-start.5 = (bf16[912,128]{1,0:T(8,128)(2,1)S(1)}, bf16[912,128]{1,0:T(8,128)(2,1)S(1)}, u32[]{:S(2)}, u32[]{:S(2)}) collective-permute-start(bf16[912,128]{1,0:T(8,128)(2,1)S(1)} %get-tuple-element.43), channel_id=1, source_target_pairs={{0,10},{2,8},{4,14},{6,12},{8,2},{10,0},{12,6},{14,4},{16,26},{18,... | collective-permute-start | bytes 700424 | tf_op jit(solution)/shard_map/ppermute | solution.py:282
  35.6 3.0 %first_products.1.before = f32[32,64,512]{2,1,0:T(8,128)S(1)} custom-call(bf16[1808,128]{1,0:T(8,128)(2,1)S(1)} %get-tuple-element.38.refs_0_, bf16[1808,128]{1,0:T(8,128)(2,1)S(1)} %collective-permute-done.3.refs_1_, bf16[1808,128]{1,0:T(8,128)(2,1)S(1)} %collective-permute-done.4.refs_2_, bf16[1024,256]{1,0:T(8,128)(2,1)S(1)} %copy-done, ...), custom_call_target="tpu_custom_call" | custom-call | bytes 14760000 | tf_op jit(solution)/shard_map/first_products/pallas_call | solution.py:327
  38.6 1.6 %collective-permute-start.13 = (bf16[1088,128]{1,0:T(8,128)(2,1)S(1)}, bf16[1088,128]{1,0:T(8,128)(2,1)S(1)}, u32[]{:S(2)}, u32[]{:S(2)}) collective-permute-start(bf16[1088,128]{1,0:T(8,128)(2,1)S(1)} %get-tuple-element.52), channel_id=1, source_target_pairs={{0,10},{2,8},{4,14},{6,12},{8,2},{10,0},{12,6},{14,4},{16,26},{18,... | collective-permute-start | bytes 835592 | tf_op jit(solution)/shard_map/ppermute | solution.py:282
  40.2 2.5 %collective-permute-done.5.labels.basis = bf16[912,128]{1,0:T(8,128)(2,1)S(1)} collective-permute-done((bf16[912,128]{1,0:T(8,128)(2,1)S(1)}, bf16[912,128]{1,0:T(8,128)(2,1)S(1)}, u32[]{:S(2)}, u32[]{:S(2)}) %collective-permute-start.5) | collective-permute-done | bytes 233504 | tf_op jit(solution)/shard_map/ppermute | solution.py:282
  42.7 1.6 %last_products.2 = (bf16[1,8,32,512]{3,2,1,0:T(8,128)(2,1)S(1)}, bf16[1,8,32,512]{3,2,1,0:T(8,128)(2,1)S(1)}, bf16[1,8,32,512]{3,2,1,0:T(8,128)(2,1)S(1)}, bf16[1,8,32,512]{3,2,1,0:T(8,128)(2,1)S(1)}) custom-call(bf16[912,128]{1,0:T(8,128)(2,1)S(1)} %collective-permute-done.5.labels.basis, bf16[912,128]{1,0:T(8,128)(2,1)S(1)} %collective-permute-done.5.labels.basis, ...), custom_call_target="tpu_custom_call" | custom-call | bytes 7380000 | tf_op jit(solution)/shard_map/last_products/pallas_call | solution.py:350
  44.4 1.6 %collective-permute-start.16 = (bf16[1,8,32,512]{3,2,1,0:T(8,128)(2,1)S(1)}, bf16[1,8,32,512]{3,2,1,0:T(8,128)(2,1)S(1)}, u32[]{:S(2)}, u32[]{:S(2)}) collective-permute-start(bf16[1,8,32,512]{3,2,1,0:T(8,128)(2,1)S(1)} %get-tuple-element.56), channel_id=1, source_target_pairs={{0,4},{2,6},{4,0},{6,2},{8,12},{10,14},{12,8},{14,10},{16,20},{18,... | collective-permute-start | bytes 786440 | tf_op jit(solution)/shard_map/ppermute | solution.py:285
  46.0 2.5 %collective-permute-done.13.basis = bf16[1088,128]{1,0:T(8,128)(2,1)S(1)} collective-permute-done((bf16[1088,128]{1,0:T(8,128)(2,1)S(1)}, bf16[1088,128]{1,0:T(8,128)(2,1)S(1)}, u32[]{:S(2)}, u32[]{:S(2)}) %collective-permute-start.13) | collective-permute-done | bytes 278560 | tf_op jit(solution)/shard_map/ppermute | solution.py:282
  48.5 1.6 %last_products.3 = (bf16[1,8,32,512]{3,2,1,0:T(8,128)(2,1)S(1)}, bf16[1,8,32,512]{3,2,1,0:T(8,128)(2,1)S(1)}, bf16[1,8,32,512]{3,2,1,0:T(8,128)(2,1)S(1)}, bf16[1,8,32,512]{3,2,1,0:T(8,128)(2,1)S(1)}) custom-call(bf16[912,128]{1,0:T(8,128)(2,1)S(1)} %collective-permute-done.5.labels.basis, bf16[1088,128]{1,0:T(8,128)(2,1)S(1)} %collective-permute-done.13.basis, ...), custom_call_target="tpu_custom_call" | custom-call | bytes 7380000 | tf_op jit(solution)/shard_map/last_products/pallas_call | solution.py:350
  50.2 1.6 %collective-permute-start.14 = (bf16[1,8,32,512]{3,2,1,0:T(8,128)(2,1)S(1)}, bf16[1,8,32,512]{3,2,1,0:T(8,128)(2,1)S(1)}, u32[]{:S(2)}, u32[]{:S(2)}) collective-permute-start(bf16[1,8,32,512]{3,2,1,0:T(8,128)(2,1)S(1)} %get-tuple-element.53), channel_id=1, source_target_pairs={{0,4},{2,6},{4,0},{6,2},{8,12},{10,14},{12,8},{14,10},{16,20},{18,... | collective-permute-start | bytes 786440 | tf_op jit(solution)/shard_map/ppermute | solution.py:285
  52.2 2.7 %collective-permute-start.17 = (bf16[1,8,32,512]{3,2,1,0:T(8,128)(2,1)S(1)}, bf16[1,8,32,512]{3,2,1,0:T(8,128)(2,1)S(1)}, u32[]{:S(2)}, u32[]{:S(2)}) collective-permute-start(bf16[1,8,32,512]{3,2,1,0:T(8,128)(2,1)S(1)} %add_convert_fusion.1), channel_id=1, source_target_pairs={{0,16},{2,18},{4,20},{6,22},{8,24},{10,26},{12,28},{14,30},{16,0},... | collective-permute-start | bytes 786440 | tf_op jit(solution)/shard_map/ppermute | solution.py:285
  54.8 3.1 %collective-permute-done.14 = bf16[1,8,32,512]{3,2,1,0:T(8,128)(2,1)S(1)} collective-permute-done((bf16[1,8,32,512]{3,2,1,0:T(8,128)(2,1)S(1)}, bf16[1,8,32,512]{3,2,1,0:T(8,128)(2,1)S(1)}, u32[]{:S(2)}, u32[]{:S(2)}) %collective-permute-start.14) | collective-permute-done | bytes 262176 | tf_op jit(solution)/shard_map/ppermute | solution.py:285
  58.0 1.5 %collective-permute-start.18 = (bf16[1,8,32,512]{3,2,1,0:T(8,128)(2,1)S(1)}, bf16[1,8,32,512]{3,2,1,0:T(8,128)(2,1)S(1)}, u32[]{:S(2)}, u32[]{:S(2)}) collective-permute-start(bf16[1,8,32,512]{3,2,1,0:T(8,128)(2,1)S(1)} %get-tuple-element.59), channel_id=1, source_target_pairs={{0,4},{2,6},{4,0},{6,2},{8,12},{10,14},{12,8},{14,10},{16,20},{18,... | collective-permute-start | bytes 786440 | tf_op jit(solution)/shard_map/ppermute | solution.py:285
  60.1 2.7 %collective-permute-start.19 = (bf16[1,4,32,512]{3,2,1,0:T(8,128)(2,1)S(1)}, bf16[1,4,32,512]{3,2,1,0:T(8,128)(2,1)S(1)}, u32[]{:S(2)}, u32[]{:S(2)}) collective-permute-start(bf16[1,4,32,512]{3,2,1,0:T(8,128)(2,1)S(1)} %get-tuple-element.70), channel_id=1, source_target_pairs={{0,16},{2,18},{4,20},{6,22},{8,24},{10,26},{12,28},{14,30},{16,0},... | collective-permute-start | bytes 393224 | tf_op jit(solution)/shard_map/ppermute | solution.py:285
  62.8 7.1 %collective-permute-done.17.refs_4_ = bf16[1,8,32,512]{3,2,1,0:T(8,128)(2,1)S(1)} collective-permute-done((bf16[1,8,32,512]{3,2,1,0:T(8,128)(2,1)S(1)}, bf16[1,8,32,512]{3,2,1,0:T(8,128)(2,1)S(1)}, u32[]{:S(2)}, u32[]{:S(2)}) %collective-permute-start.17) | collective-permute-done | bytes 262176 | tf_op jit(solution)/shard_map/ppermute | solution.py:285
  69.9 1.9 %collective-permute-done.19.refs_7_ = bf16[1,4,32,512]{3,2,1,0:T(8,128)(2,1)S(1)} collective-permute-done((bf16[1,4,32,512]{3,2,1,0:T(8,128)(2,1)S(1)}, bf16[1,4,32,512]{3,2,1,0:T(8,128)(2,1)S(1)}, u32[]{:S(2)}, u32[]{:S(2)}) %collective-permute-start.19) | collective-permute-done | bytes 131104 | tf_op jit(solution)/shard_map/ppermute | solution.py:285
  72.6 7.6 %collective-permute-start.21 = (bf16[2,64,512]{2,1,0:T(8,128)(2,1)S(1)}, bf16[2,64,512]{2,1,0:T(8,128)(2,1)S(1)}, u32[]{:S(2)}, u32[]{:S(2)}) collective-permute-start(bf16[2,64,512]{2,1,0:T(8,128)(2,1)S(1)} %get-tuple-element.63), channel_id=1, source_target_pairs={{0,30},{2,4},{4,2},{6,8},{8,6},{10,12},{12,10},{14,16},{16,14},{18... | collective-permute-start | bytes 393224 | tf_op jit(solution)/shard_map/ppermute | solution.py:413
  81.0 2.2 %mlp.3 = (bf16[4,64,256]{2,1,0:T(8,128)(2,1)S(1)}, bf16[4,64,256]{2,1,0:T(8,128)(2,1)S(1)}) custom-call(s32[8]{0:T(128)S(1)} %copy-done.4, s32[1]{0:T(128)S(6)} %copy.12.valid, bf16[4,64,512]{2,1,0:T(8,128)(2,1)S(1)} %combine.3.combined, bf16[3,512,256]{2,1,0:T(8,128)(2,1)S(1)} %copy-done.2, bf16[3,512,256]{2,1,0:T(8,128)(2,1)S(1)} %collective-permute-done.refs_3_.refs_1_, ...), custom_call_target="tpu_custom_call" | custom-call | bytes 7380000 | tf_op jit(solution)/shard_map/mlp/pallas_call | solution.py:417
  83.5 2.2 %mlp.2 = (bf16[4,64,256]{2,1,0:T(8,128)(2,1)S(1)}, bf16[4,64,256]{2,1,0:T(8,128)(2,1)S(1)}) custom-call(s32[8]{0:T(128)S(1)} %copy-done.4, s32[1]{0:T(128)S(6)} %copy.12.valid, bf16[4,64,512]{2,1,0:T(8,128)(2,1)S(1)} %get-tuple-element.61.combined, bf16[2,64,512]{2,1,0:T(8,128)(2,1)S(1)} %collective-permute-done.20.refs_0_, ...), custom_call_target="tpu_custom_call" | custom-call | bytes 7380000 | tf_op jit(solution)/shard_map/mlp/pallas_call | solution.py:417
  86.0 1.0 %collective-permute-done.23.refs_2_ = bf16[4,64,256]{2,1,0:T(8,128)(2,1)S(1)} collective-permute-done((bf16[4,64,256]{2,1,0:T(8,128)(2,1)S(1)}, bf16[4,64,256]{2,1,0:T(8,128)(2,1)S(1)}, u32[]{:S(2)}, u32[]{:S(2)}) %collective-permute-start.23) | collective-permute-done | bytes 131104 | tf_op jit(solution)/shard_map/ppermute | solution.py:288
  87.0 0.8 join.1
  (52 shorter events, 5.0 us)
Async XLA Ops:
  0.0 19.3 %copy-start = (bf16[1024,256]{1,0:T(8,128)(2,1)S(1)}, bf16[1024,256]{1,0:T(8,128)(2,1)}, u32[]{:S(2)}) copy-start(bf16[1024,256]{1,0:T(8,128)(2,1)} %refs_0_.4) | copy-start | bytes 1572868
  0.0 5.0 %collective-permute-start = (bf16[3,512,256]{2,1,0:T(8,128)(2,1)}, bf16[3,512,256]{2,1,0:T(8,128)(2,1)S(1)}, u32[]{:S(2)}, u32[]{:S(2)}) collective-permute-start(bf16[3,512,256]{2,1,0:T(8,128)(2,1)} %refs_0_.5), channel_id=1, source_target_pairs={{0,1},{1,0},{2,3},{3,2},{4,5},{5,4},{6,7},{7,6},{8,9},{9,8},{10,11... | collective-permute-start | bytes 2359304 | tf_op jit(solution)/shard_map/ppermute | solution.py:288
  0.5 4.6 %collective-permute-start.1 = (bf16[3,256,512]{2,1,0:T(8,128)(2,1)}, bf16[3,256,512]{2,1,0:T(8,128)(2,1)S(1)}, u32[]{:S(2)}, u32[]{:S(2)}) collective-permute-start(bf16[3,256,512]{2,1,0:T(8,128)(2,1)} %refs_2_.3), channel_id=1, source_target_pairs={{0,1},{1,0},{2,3},{3,2},{4,5},{5,4},{6,7},{7,6},{8,9},{9,8},{10,11... | collective-permute-start | bytes 2359304 | tf_op jit(solution)/shard_map/ppermute | solution.py:288
  0.5 15.8 %collective-permute-start.6 = (bf16[1024,256]{1,0:T(8,128)(2,1)}, bf16[1024,256]{1,0:T(8,128)(2,1)S(1)}, u32[]{:S(2)}, u32[]{:S(2)}) collective-permute-start(bf16[1024,256]{1,0:T(8,128)(2,1)} %refs_0_.4), channel_id=1, source_target_pairs={{0,2},{2,0},{4,6},{6,4},{8,10},{10,8},{12,14},{14,12},{16,18},{18,... | collective-permute-start | bytes 1572872 | tf_op jit(solution)/shard_map/ppermute | solution.py:282
  3.5 14.3 %collective-permute-start.8 = (bf16[1024,256]{1,0:T(8,128)(2,1)}, bf16[1024,256]{1,0:T(8,128)(2,1)S(1)}, u32[]{:S(2)}, u32[]{:S(2)}) collective-permute-start(bf16[1024,256]{1,0:T(8,128)(2,1)} %refs_0_.4), channel_id=1, source_target_pairs={{0,8},{2,10},{4,12},{6,14},{8,0},{10,2},{12,4},{14,6},{16,24},{18,... | collective-permute-start | bytes 1572872 | tf_op jit(solution)/shard_map/ppermute | solution.py:282
  5.0 1.9 %copy-start.1 = (bf16[96,128,128]{2,1,0:T(8,128)(2,1)S(1)}, bf16[96,128,128]{2,1,0:T(8,128)(2,1)}, u32[]{:S(2)}) copy-start(bf16[96,128,128]{2,1,0:T(8,128)(2,1)} %basis) | copy-start | bytes 9437188
  6.9 0.7 copy-start.5
  7.6 0.7 copy-start.6
  13.2 19.6 %collective-permute-start.3 = (bf16[1808,128]{1,0:T(8,128)(2,1)S(1)}, bf16[1808,128]{1,0:T(8,128)(2,1)S(1)}, u32[]{:S(2)}, u32[]{:S(2)}) collective-permute-start(bf16[1808,128]{1,0:T(8,128)(2,1)S(1)} %get-tuple-element.41), channel_id=1, source_target_pairs={{0,2},{2,0},{4,6},{6,4},{8,10},{10,8},{12,14},{14,12},{16,18},{18,... | collective-permute-start | bytes 1388552 | tf_op jit(solution)/shard_map/ppermute | solution.py:282
  14.8 18.1 %collective-permute-start.4 = (bf16[1808,128]{1,0:T(8,128)(2,1)S(1)}, bf16[1808,128]{1,0:T(8,128)(2,1)S(1)}, u32[]{:S(2)}, u32[]{:S(2)}) collective-permute-start(bf16[1808,128]{1,0:T(8,128)(2,1)S(1)} %get-tuple-element.42), channel_id=1, source_target_pairs={{0,8},{2,10},{4,12},{6,14},{8,0},{10,2},{12,4},{14,6},{16,24},{18,... | collective-permute-start | bytes 1388552 | tf_op jit(solution)/shard_map/ppermute | solution.py:282
  16.4 16.4 %collective-permute-start.7 = (bf16[512,256]{1,0:T(8,128)(2,1)S(1)}, bf16[512,256]{1,0:T(8,128)(2,1)S(1)}, u32[]{:S(2)}, u32[]{:S(2)}) collective-permute-start(bf16[512,256]{1,0:T(8,128)(2,1)S(1)} %slice.12), channel_id=1, source_target_pairs={{0,8},{2,10},{4,12},{6,14},{8,0},{10,2},{12,4},{14,6},{16,24},{18,... | collective-permute-start | bytes 786440 | tf_op jit(solution)/shard_map/ppermute | solution.py:282
  17.8 15.7 %collective-permute-start.9 = (bf16[512,256]{1,0:T(8,128)(2,1)S(1)}, bf16[512,256]{1,0:T(8,128)(2,1)S(1)}, u32[]{:S(2)}, u32[]{:S(2)}) collective-permute-start(bf16[512,256]{1,0:T(8,128)(2,1)S(1)} %slice.13), channel_id=1, source_target_pairs={{0,2},{2,0},{4,6},{6,4},{8,10},{10,8},{12,14},{14,12},{16,18},{18,... | collective-permute-start | bytes 786440 | tf_op jit(solution)/shard_map/ppermute | solution.py:282
  19.3 15.8 %collective-permute-start.2 = (bf16[1024,256]{1,0:T(8,128)(2,1)S(1)}, bf16[1024,256]{1,0:T(8,128)(2,1)S(1)}, u32[]{:S(2)}, u32[]{:S(2)}) collective-permute-start(bf16[1024,256]{1,0:T(8,128)(2,1)S(1)} %copy-done), channel_id=1, source_target_pairs={{0,1},{1,0},{2,3},{3,2},{4,5},{5,4},{6,7},{7,6},{8,9},{9,8},{10,11... | collective-permute-start | bytes 1572872 | tf_op jit(solution)/shard_map/ppermute | solution.py:288
  32.9 2.3 %collective-permute-start.11 = (bf16[1024,256]{1,0:T(8,128)(2,1)S(1)}, bf16[1024,256]{1,0:T(8,128)(2,1)S(1)}, u32[]{:S(2)}, u32[]{:S(2)}) collective-permute-start(bf16[1024,256]{1,0:T(8,128)(2,1)S(1)} %collective-permute-done.6.refs_4_), channel_id=1, source_target_pairs={{0,1},{1,0},{2,3},{3,2},{4,5},{5,4},{6,7},{7,6},{8,9},{9,8},{10,11... | collective-permute-start | bytes 1572872 | tf_op jit(solution)/shard_map/ppermute | solution.py:288
  32.9 2.6 %collective-permute-start.12 = (bf16[1024,256]{1,0:T(8,128)(2,1)S(1)}, bf16[1024,256]{1,0:T(8,128)(2,1)S(1)}, u32[]{:S(2)}, u32[]{:S(2)}) collective-permute-start(bf16[1024,256]{1,0:T(8,128)(2,1)S(1)} %collective-permute-done.8.refs_5_), channel_id=1, source_target_pairs={{0,1},{1,0},{2,3},{3,2},{4,5},{5,4},{6,7},{7,6},{8,9},{9,8},{10,11... | collective-permute-start | bytes 1572872 | tf_op jit(solution)/shard_map/ppermute | solution.py:288
  33.5 9.3 %collective-permute-start.10 = (bf16[1024,256]{1,0:T(8,128)(2,1)S(1)}, bf16[1024,256]{1,0:T(8,128)(2,1)S(1)}, u32[]{:S(2)}, u32[]{:S(2)}) collective-permute-start(bf16[1024,256]{1,0:T(8,128)(2,1)S(1)} %constant_dynamic-update-slice_fusion.mine), channel_id=1, source_target_pairs={{0,1},{1,0},{2,3},{3,2},{4,5},{5,4},{6,7},{7,6},{8,9},{9,8},{10,11... | collective-permute-start | bytes 1572872 | tf_op jit(solution)/shard_map/ppermute | solution.py:288
  33.6 9.1 %collective-permute-start.5 = (bf16[912,128]{1,0:T(8,128)(2,1)S(1)}, bf16[912,128]{1,0:T(8,128)(2,1)S(1)}, u32[]{:S(2)}, u32[]{:S(2)}) collective-permute-start(bf16[912,128]{1,0:T(8,128)(2,1)S(1)} %get-tuple-element.43), channel_id=1, source_target_pairs={{0,10},{2,8},{4,14},{6,12},{8,2},{10,0},{12,6},{14,4},{16,26},{18,... | collective-permute-start | bytes 700424 | tf_op jit(solution)/shard_map/ppermute | solution.py:282
  38.6 9.9 %collective-permute-start.13 = (bf16[1088,128]{1,0:T(8,128)(2,1)S(1)}, bf16[1088,128]{1,0:T(8,128)(2,1)S(1)}, u32[]{:S(2)}, u32[]{:S(2)}) collective-permute-start(bf16[1088,128]{1,0:T(8,128)(2,1)S(1)} %get-tuple-element.52), channel_id=1, source_target_pairs={{0,10},{2,8},{4,14},{6,12},{8,2},{10,0},{12,6},{14,4},{16,26},{18,... | collective-permute-start | bytes 835592 | tf_op jit(solution)/shard_map/ppermute | solution.py:282
  44.4 7.7 %collective-permute-start.16 = (bf16[1,8,32,512]{3,2,1,0:T(8,128)(2,1)S(1)}, bf16[1,8,32,512]{3,2,1,0:T(8,128)(2,1)S(1)}, u32[]{:S(2)}, u32[]{:S(2)}) collective-permute-start(bf16[1,8,32,512]{3,2,1,0:T(8,128)(2,1)S(1)} %get-tuple-element.56), channel_id=1, source_target_pairs={{0,4},{2,6},{4,0},{6,2},{8,12},{10,14},{12,8},{14,10},{16,20},{18,... | collective-permute-start | bytes 786440 | tf_op jit(solution)/shard_map/ppermute | solution.py:285
  50.1 30.8 %copy-start.2 = (bf16[3,512,256]{2,1,0:T(8,128)(2,1)S(1)}, bf16[3,512,256]{2,1,0:T(8,128)(2,1)}, u32[]{:S(2)}) copy-start(bf16[3,512,256]{2,1,0:T(8,128)(2,1)} %refs_0_.5) | copy-start | bytes 2359300
  50.1 30.8 %copy-start.3 = (bf16[3,256,512]{2,1,0:T(8,128)(2,1)S(1)}, bf16[3,256,512]{2,1,0:T(8,128)(2,1)}, u32[]{:S(2)}) copy-start(bf16[3,256,512]{2,1,0:T(8,128)(2,1)} %refs_2_.3) | copy-start | bytes 2359300
  50.2 30.8 %copy-start.4 = (s32[8]{0:T(128)S(1)}, s32[8]{0:T(128)}, u32[]{:S(2)}) copy-start(s32[8]{0:T(128)} %reverse.3) | copy-start | bytes 100
  50.2 7.8 %collective-permute-start.14 = (bf16[1,8,32,512]{3,2,1,0:T(8,128)(2,1)S(1)}, bf16[1,8,32,512]{3,2,1,0:T(8,128)(2,1)S(1)}, u32[]{:S(2)}, u32[]{:S(2)}) collective-permute-start(bf16[1,8,32,512]{3,2,1,0:T(8,128)(2,1)S(1)} %get-tuple-element.53), channel_id=1, source_target_pairs={{0,4},{2,6},{4,0},{6,2},{8,12},{10,14},{12,8},{14,10},{16,20},{18,... | collective-permute-start | bytes 786440 | tf_op jit(solution)/shard_map/ppermute | solution.py:285
  52.2 17.7 %collective-permute-start.17 = (bf16[1,8,32,512]{3,2,1,0:T(8,128)(2,1)S(1)}, bf16[1,8,32,512]{3,2,1,0:T(8,128)(2,1)S(1)}, u32[]{:S(2)}, u32[]{:S(2)}) collective-permute-start(bf16[1,8,32,512]{3,2,1,0:T(8,128)(2,1)S(1)} %add_convert_fusion.1), channel_id=1, source_target_pairs={{0,16},{2,18},{4,20},{6,22},{8,24},{10,26},{12,28},{14,30},{16,0},... | collective-permute-start | bytes 786440 | tf_op jit(solution)/shard_map/ppermute | solution.py:285
  58.0 13.8 %collective-permute-start.18 = (bf16[1,8,32,512]{3,2,1,0:T(8,128)(2,1)S(1)}, bf16[1,8,32,512]{3,2,1,0:T(8,128)(2,1)S(1)}, u32[]{:S(2)}, u32[]{:S(2)}) collective-permute-start(bf16[1,8,32,512]{3,2,1,0:T(8,128)(2,1)S(1)} %get-tuple-element.59), channel_id=1, source_target_pairs={{0,4},{2,6},{4,0},{6,2},{8,12},{10,14},{12,8},{14,10},{16,20},{18,... | collective-permute-start | bytes 786440 | tf_op jit(solution)/shard_map/ppermute | solution.py:285
  59.5 12.3 %collective-permute-start.15 = (bf16[1,8,32,512]{3,2,1,0:T(8,128)(2,1)S(1)}, bf16[1,8,32,512]{3,2,1,0:T(8,128)(2,1)S(1)}, u32[]{:S(2)}, u32[]{:S(2)}) collective-permute-start(bf16[1,8,32,512]{3,2,1,0:T(8,128)(2,1)S(1)} %get-tuple-element.54), channel_id=1, source_target_pairs={{0,4},{2,6},{4,0},{6,2},{8,12},{10,14},{12,8},{14,10},{16,20},{18,... | collective-permute-start | bytes 786440 | tf_op jit(solution)/shard_map/ppermute | solution.py:285
  60.1 11.7 %collective-permute-start.19 = (bf16[1,4,32,512]{3,2,1,0:T(8,128)(2,1)S(1)}, bf16[1,4,32,512]{3,2,1,0:T(8,128)(2,1)S(1)}, u32[]{:S(2)}, u32[]{:S(2)}) collective-permute-start(bf16[1,4,32,512]{3,2,1,0:T(8,128)(2,1)S(1)} %get-tuple-element.70), channel_id=1, source_target_pairs={{0,16},{2,18},{4,20},{6,22},{8,24},{10,26},{12,28},{14,30},{16,0},... | collective-permute-start | bytes 393224 | tf_op jit(solution)/shard_map/ppermute | solution.py:285
  69.9 10.9 %collective-permute-start.22 = (bf16[1,4,32,512]{3,2,1,0:T(8,128)(2,1)S(1)}, bf16[1,4,32,512]{3,2,1,0:T(8,128)(2,1)S(1)}, u32[]{:S(2)}, u32[]{:S(2)}) collective-permute-start(bf16[1,4,32,512]{3,2,1,0:T(8,128)(2,1)S(1)} %get-tuple-element.65), channel_id=1, source_target_pairs={{0,16},{2,18},{4,20},{6,22},{8,24},{10,26},{12,28},{14,30},{16,0},... | collective-permute-start | bytes 393224 | tf_op jit(solution)/shard_map/ppermute | solution.py:285
  72.0 11.3 %collective-permute-start.20 = (bf16[2,64,512]{2,1,0:T(8,128)(2,1)S(1)}, bf16[2,64,512]{2,1,0:T(8,128)(2,1)S(1)}, u32[]{:S(2)}, u32[]{:S(2)}) collective-permute-start(bf16[2,64,512]{2,1,0:T(8,128)(2,1)S(1)} %get-tuple-element.62), channel_id=1, source_target_pairs={{0,2},{2,0},{4,6},{6,4},{8,10},{10,8},{12,14},{14,12},{16,18},{18,... | collective-permute-start | bytes 393224 | tf_op jit(solution)/shard_map/ppermute | solution.py:414
  72.6 10.9 %collective-permute-start.21 = (bf16[2,64,512]{2,1,0:T(8,128)(2,1)S(1)}, bf16[2,64,512]{2,1,0:T(8,128)(2,1)S(1)}, u32[]{:S(2)}, u32[]{:S(2)}) collective-permute-start(bf16[2,64,512]{2,1,0:T(8,128)(2,1)S(1)} %get-tuple-element.63), channel_id=1, source_target_pairs={{0,30},{2,4},{4,2},{6,8},{8,6},{10,12},{12,10},{14,16},{16,14},{18... | collective-permute-start | bytes 393224 | tf_op jit(solution)/shard_map/ppermute | solution.py:413
  83.2 2.8 %collective-permute-start.24 = (bf16[4,64,256]{2,1,0:T(8,128)(2,1)S(1)}, bf16[4,64,256]{2,1,0:T(8,128)(2,1)S(1)}, u32[]{:S(2)}, u32[]{:S(2)}) collective-permute-start(bf16[4,64,256]{2,1,0:T(8,128)(2,1)S(1)} %get-tuple-element.68), channel_id=1, source_target_pairs={{0,1},{1,0},{2,3},{3,2},{4,5},{5,4},{6,7},{7,6},{8,9},{9,8},{10,11... | collective-permute-start | bytes 393224 | tf_op jit(solution)/shard_map/ppermute | solution.py:288
  85.6 1.4 %collective-permute-start.23 = (bf16[4,64,256]{2,1,0:T(8,128)(2,1)S(1)}, bf16[4,64,256]{2,1,0:T(8,128)(2,1)S(1)}, u32[]{:S(2)}, u32[]{:S(2)}) collective-permute-start(bf16[4,64,256]{2,1,0:T(8,128)(2,1)S(1)} %get-tuple-element.67), channel_id=1, source_target_pairs={{0,1},{1,0},{2,3},{3,2},{4,5},{5,4},{6,7},{7,6},{8,9},{9,8},{10,11... | collective-permute-start | bytes 393224 | tf_op jit(solution)/shard_map/ppermute | solution.py:288
  (2 other events, 1.3 us)

commit v7 on v6

--- a/solution.py
+++ b/solution.py
@@ -221,10 +221,13 @@
     for layer in range(MLPS):
         layer_input = state[...].astype(jnp.bfloat16)
         total = state[...]
-        for w_in, w_out in ((in_own, out_own), (in_other, out_other)):
-            value = jnp.dot(layer_input, w_in[layer], preferred_element_type=jnp.float32)
-            hidden = (0.5 * value * (1.0 + jnp.tanh(0.5 * value))).astype(jnp.bfloat16)
-            total = total + jnp.dot(hidden, w_out[layer], preferred_element_type=jnp.float32)
+        values = [
+            jnp.dot(layer_input, w_in[layer], preferred_element_type=jnp.float32)
+            for w_in in (in_own, in_other)
+        ]
+        hidden = [(0.5 * v * (1.0 + jnp.tanh(0.5 * v))).astype(jnp.bfloat16) for v in values]
+        for part, w_out in zip(hidden, (out_own, out_other)):
+            total = total + jnp.dot(part, w_out[layer], preferred_element_type=jnp.float32)
         state[...] = total
     half = width // 2
     own_cols = pl.ds(pl.multiple_of(core * half, half), half)

time: 88.1 us -> 88 us (level)
  no operation moved by 1% of the time
where the time goes in v7:
time: 88 us; the launch traced here: 87.8 us
  starting transfers between devices  34 us (39%)
  waiting for transfers between devices  33 us (38%)
  Pallas kernels  15.2 us (17%)
  local copies, waits for them, and re-layouts  4.62 us (5%)
    ppermute x8, waiting for transfers between devices, near_send(): return lax.ppermute(array, 'graph', xor_pairs(devices, near_mask(near, k)))  18.6 us
    ppermute x8, starting transfers between devices, near_send(): return lax.ppermute(array, 'graph', xor_pairs(devices, near_mask(near, k)))  13.7 us
    ppermute x7, waiting for transfers between devices, far_send(): return lax.ppermute(array, 'graph', xor_pairs(devices, 1 << bit))  12.6 us
    ppermute x7, starting transfers between devices, far_send(): return lax.ppermute(array, 'graph', xor_pairs(devices, 1 << bit))  10.5 us
    ppermute x1, starting transfers between devices, local(): lax.ppermute(outs[2], 'graph', odd_pairs)  7.59 us
    unnamed x19, local copies, waits for them, and re-layouts  4.55 us
    pallas_call x2, Pallas kernels, local(): pl.pallas_call(functools.partial(mlp_kernel, border, start, blocks), out_...  4.18 us
    pallas_call x1, Pallas kernels, local(): pl.pallas_call(functools.partial(pack_kernel, near, far, room, rows, bloc...  3.64 us
  transfers between devices with their start and end apart: 25, of which 10 were waited for; matrix products, arithmetic and copies ran while one was open for 0% of the time, Pallas kernels for 16%

profile of v7, /device:TPU:0, one launch (start us, length us, event | category | flops | bytes accessed | tf_op | source)
XLA Modules:
  0.0 87.8 jit_solution(18362308954652479049)
XLA Ops:
  0.5 2.9 %collective-permute-start.6 = (bf16[1024,256]{1,0:T(8,128)(2,1)}, bf16[1024,256]{1,0:T(8,128)(2,1)S(1)}, u32[]{:S(2)}, u32[]{:S(2)}) collective-permute-start(bf16[1024,256]{1,0:T(8,128)(2,1)} %refs_0_.4), channel_id=1, source_target_pairs={{0,2},{2,0},{4,6},{6,4},{8,10},{10,8},{12,14},{14,12},{16,18},{18,... | collective-permute-start | bytes 1572872 | tf_op jit(solution)/shard_map/ppermute | solution.py:285
  3.5 1.6 %collective-permute-start.8 = (bf16[1024,256]{1,0:T(8,128)(2,1)}, bf16[1024,256]{1,0:T(8,128)(2,1)S(1)}, u32[]{:S(2)}, u32[]{:S(2)}) collective-permute-start(bf16[1024,256]{1,0:T(8,128)(2,1)} %refs_0_.4), channel_id=1, source_target_pairs={{0,8},{2,10},{4,12},{6,14},{8,0},{10,2},{12,4},{14,6},{16,24},{18,... | collective-permute-start | bytes 1572872 | tf_op jit(solution)/shard_map/ppermute | solution.py:285
  5.0 1.9 %copy-done.1 = bf16[96,128,128]{2,1,0:T(8,128)(2,1)S(1)} copy-done((bf16[96,128,128]{2,1,0:T(8,128)(2,1)S(1)}, bf16[96,128,128]{2,1,0:T(8,128)(2,1)}, u32[]{:S(2)}) %copy-start.1) | copy-done | bytes 3145752
  6.9 0.7 copy-done.5
  7.6 0.7 copy-done.6
  8.2 0.7 copy-done.7
  9.6 3.6 %pack.1 = (bf16[1808,128]{1,0:T(8,128)(2,1)S(1)}, bf16[1808,128]{1,0:T(8,128)(2,1)S(1)}, bf16[1808,128]{1,0:T(8,128)(2,1)S(1)}, bf16[912,128]{1,0:T(8,128)(2,1)S(1)}, bf16[1088,128]{1,0:T(8,128)(2,1)S(1)}) custom-call(s32[96]{0:T(128)S(1)} %bitcast.1, s32[96]{0:T(128)S(1)} %copy-done.6, s32[96]{0:T(128)S(1)} %copy-done.7, s32[96]{0:T(128)S(1)} %copy-done.8, ...), custom_call_target="tpu_custom_call" | custom-call | bytes 22140000 | tf_op jit(solution)/shard_map/pack/pallas_call | solution.py:302
  13.2 1.6 %collective-permute-start.3 = (bf16[1808,128]{1,0:T(8,128)(2,1)S(1)}, bf16[1808,128]{1,0:T(8,128)(2,1)S(1)}, u32[]{:S(2)}, u32[]{:S(2)}) collective-permute-start(bf16[1808,128]{1,0:T(8,128)(2,1)S(1)} %get-tuple-element.41), channel_id=1, source_target_pairs={{0,2},{2,0},{4,6},{6,4},{8,10},{10,8},{12,14},{14,12},{16,18},{18,... | collective-permute-start | bytes 1388552 | tf_op jit(solution)/shard_map/ppermute | solution.py:285
  14.8 1.6 %collective-permute-start.4 = (bf16[1808,128]{1,0:T(8,128)(2,1)S(1)}, bf16[1808,128]{1,0:T(8,128)(2,1)S(1)}, u32[]{:S(2)}, u32[]{:S(2)}) collective-permute-start(bf16[1808,128]{1,0:T(8,128)(2,1)S(1)} %get-tuple-element.42), channel_id=1, source_target_pairs={{0,8},{2,10},{4,12},{6,14},{8,0},{10,2},{12,4},{14,6},{16,24},{18,... | collective-permute-start | bytes 1388552 | tf_op jit(solution)/shard_map/ppermute | solution.py:285
  16.4 1.3 %collective-permute-start.7 = (bf16[512,256]{1,0:T(8,128)(2,1)S(1)}, bf16[512,256]{1,0:T(8,128)(2,1)S(1)}, u32[]{:S(2)}, u32[]{:S(2)}) collective-permute-start(bf16[512,256]{1,0:T(8,128)(2,1)S(1)} %slice.12), channel_id=1, source_target_pairs={{0,8},{2,10},{4,12},{6,14},{8,0},{10,2},{12,4},{14,6},{16,24},{18,... | collective-permute-start | bytes 786440 | tf_op jit(solution)/shard_map/ppermute | solution.py:285
  17.8 1.6 %collective-permute-start.9 = (bf16[512,256]{1,0:T(8,128)(2,1)S(1)}, bf16[512,256]{1,0:T(8,128)(2,1)S(1)}, u32[]{:S(2)}, u32[]{:S(2)}) collective-permute-start(bf16[512,256]{1,0:T(8,128)(2,1)S(1)} %slice.13), channel_id=1, source_target_pairs={{0,2},{2,0},{4,6},{6,4},{8,10},{10,8},{12,14},{14,12},{16,18},{18,... | collective-permute-start | bytes 786440 | tf_op jit(solution)/shard_map/ppermute | solution.py:285
  19.3 13.5 %collective-permute-done.7 = bf16[512,256]{1,0:T(8,128)(2,1)S(1)} collective-permute-done((bf16[512,256]{1,0:T(8,128)(2,1)S(1)}, bf16[512,256]{1,0:T(8,128)(2,1)S(1)}, u32[]{:S(2)}, u32[]{:S(2)}) %collective-permute-start.7) | collective-permute-done | bytes 262176 | tf_op jit(solution)/shard_map/ppermute | solution.py:285
  33.6 1.5 %collective-permute-start.5 = (bf16[912,128]{1,0:T(8,128)(2,1)S(1)}, bf16[912,128]{1,0:T(8,128)(2,1)S(1)}, u32[]{:S(2)}, u32[]{:S(2)}) collective-permute-start(bf16[912,128]{1,0:T(8,128)(2,1)S(1)} %get-tuple-element.43), channel_id=1, source_target_pairs={{0,10},{2,8},{4,14},{6,12},{8,2},{10,0},{12,6},{14,4},{16,26},{18,... | collective-permute-start | bytes 700424 | tf_op jit(solution)/shard_map/ppermute | solution.py:285
  35.6 3.0 %first_products.1.before = f32[32,64,512]{2,1,0:T(8,128)S(1)} custom-call(bf16[1808,128]{1,0:T(8,128)(2,1)S(1)} %get-tuple-element.38.refs_0_, bf16[1808,128]{1,0:T(8,128)(2,1)S(1)} %collective-permute-done.3.refs_1_, bf16[1808,128]{1,0:T(8,128)(2,1)S(1)} %collective-permute-done.4.refs_2_, bf16[1024,256]{1,0:T(8,128)(2,1)S(1)} %copy-done, ...), custom_call_target="tpu_custom_call" | custom-call | bytes 14760000 | tf_op jit(solution)/shard_map/first_products/pallas_call | solution.py:330
  38.6 1.6 %collective-permute-start.13 = (bf16[1088,128]{1,0:T(8,128)(2,1)S(1)}, bf16[1088,128]{1,0:T(8,128)(2,1)S(1)}, u32[]{:S(2)}, u32[]{:S(2)}) collective-permute-start(bf16[1088,128]{1,0:T(8,128)(2,1)S(1)} %get-tuple-element.52), channel_id=1, source_target_pairs={{0,10},{2,8},{4,14},{6,12},{8,2},{10,0},{12,6},{14,4},{16,26},{18,... | collective-permute-start | bytes 835592 | tf_op jit(solution)/shard_map/ppermute | solution.py:285
  40.2 2.5 %collective-permute-done.5.labels.basis = bf16[912,128]{1,0:T(8,128)(2,1)S(1)} collective-permute-done((bf16[912,128]{1,0:T(8,128)(2,1)S(1)}, bf16[912,128]{1,0:T(8,128)(2,1)S(1)}, u32[]{:S(2)}, u32[]{:S(2)}) %collective-permute-start.5) | collective-permute-done | bytes 233504 | tf_op jit(solution)/shard_map/ppermute | solution.py:285
  42.7 1.6 %last_products.2 = (bf16[1,8,32,512]{3,2,1,0:T(8,128)(2,1)S(1)}, bf16[1,8,32,512]{3,2,1,0:T(8,128)(2,1)S(1)}, bf16[1,8,32,512]{3,2,1,0:T(8,128)(2,1)S(1)}, bf16[1,8,32,512]{3,2,1,0:T(8,128)(2,1)S(1)}) custom-call(bf16[912,128]{1,0:T(8,128)(2,1)S(1)} %collective-permute-done.5.labels.basis, bf16[912,128]{1,0:T(8,128)(2,1)S(1)} %collective-permute-done.5.labels.basis, ...), custom_call_target="tpu_custom_call" | custom-call | bytes 7380000 | tf_op jit(solution)/shard_map/last_products/pallas_call | solution.py:353
  44.4 1.6 %collective-permute-start.16 = (bf16[1,8,32,512]{3,2,1,0:T(8,128)(2,1)S(1)}, bf16[1,8,32,512]{3,2,1,0:T(8,128)(2,1)S(1)}, u32[]{:S(2)}, u32[]{:S(2)}) collective-permute-start(bf16[1,8,32,512]{3,2,1,0:T(8,128)(2,1)S(1)} %get-tuple-element.56), channel_id=1, source_target_pairs={{0,4},{2,6},{4,0},{6,2},{8,12},{10,14},{12,8},{14,10},{16,20},{18,... | collective-permute-start | bytes 786440 | tf_op jit(solution)/shard_map/ppermute | solution.py:288
  46.0 2.5 %collective-permute-done.13.basis = bf16[1088,128]{1,0:T(8,128)(2,1)S(1)} collective-permute-done((bf16[1088,128]{1,0:T(8,128)(2,1)S(1)}, bf16[1088,128]{1,0:T(8,128)(2,1)S(1)}, u32[]{:S(2)}, u32[]{:S(2)}) %collective-permute-start.13) | collective-permute-done | bytes 278560 | tf_op jit(solution)/shard_map/ppermute | solution.py:285
  48.5 1.6 %last_products.3 = (bf16[1,8,32,512]{3,2,1,0:T(8,128)(2,1)S(1)}, bf16[1,8,32,512]{3,2,1,0:T(8,128)(2,1)S(1)}, bf16[1,8,32,512]{3,2,1,0:T(8,128)(2,1)S(1)}, bf16[1,8,32,512]{3,2,1,0:T(8,128)(2,1)S(1)}) custom-call(bf16[912,128]{1,0:T(8,128)(2,1)S(1)} %collective-permute-done.5.labels.basis, bf16[1088,128]{1,0:T(8,128)(2,1)S(1)} %collective-permute-done.13.basis, ...), custom_call_target="tpu_custom_call" | custom-call | bytes 7380000 | tf_op jit(solution)/shard_map/last_products/pallas_call | solution.py:353
  50.2 1.6 %collective-permute-start.14 = (bf16[1,8,32,512]{3,2,1,0:T(8,128)(2,1)S(1)}, bf16[1,8,32,512]{3,2,1,0:T(8,128)(2,1)S(1)}, u32[]{:S(2)}, u32[]{:S(2)}) collective-permute-start(bf16[1,8,32,512]{3,2,1,0:T(8,128)(2,1)S(1)} %get-tuple-element.53), channel_id=1, source_target_pairs={{0,4},{2,6},{4,0},{6,2},{8,12},{10,14},{12,8},{14,10},{16,20},{18,... | collective-permute-start | bytes 786440 | tf_op jit(solution)/shard_map/ppermute | solution.py:288
  52.2 2.7 %collective-permute-start.17 = (bf16[1,8,32,512]{3,2,1,0:T(8,128)(2,1)S(1)}, bf16[1,8,32,512]{3,2,1,0:T(8,128)(2,1)S(1)}, u32[]{:S(2)}, u32[]{:S(2)}) collective-permute-start(bf16[1,8,32,512]{3,2,1,0:T(8,128)(2,1)S(1)} %add_convert_fusion.1), channel_id=1, source_target_pairs={{0,16},{2,18},{4,20},{6,22},{8,24},{10,26},{12,28},{14,30},{16,0},... | collective-permute-start | bytes 786440 | tf_op jit(solution)/shard_map/ppermute | solution.py:288
  54.8 3.1 %collective-permute-done.14 = bf16[1,8,32,512]{3,2,1,0:T(8,128)(2,1)S(1)} collective-permute-done((bf16[1,8,32,512]{3,2,1,0:T(8,128)(2,1)S(1)}, bf16[1,8,32,512]{3,2,1,0:T(8,128)(2,1)S(1)}, u32[]{:S(2)}, u32[]{:S(2)}) %collective-permute-start.14) | collective-permute-done | bytes 262176 | tf_op jit(solution)/shard_map/ppermute | solution.py:288
  58.0 1.5 %collective-permute-start.18 = (bf16[1,8,32,512]{3,2,1,0:T(8,128)(2,1)S(1)}, bf16[1,8,32,512]{3,2,1,0:T(8,128)(2,1)S(1)}, u32[]{:S(2)}, u32[]{:S(2)}) collective-permute-start(bf16[1,8,32,512]{3,2,1,0:T(8,128)(2,1)S(1)} %get-tuple-element.59), channel_id=1, source_target_pairs={{0,4},{2,6},{4,0},{6,2},{8,12},{10,14},{12,8},{14,10},{16,20},{18,... | collective-permute-start | bytes 786440 | tf_op jit(solution)/shard_map/ppermute | solution.py:288
  60.1 2.7 %collective-permute-start.19 = (bf16[1,4,32,512]{3,2,1,0:T(8,128)(2,1)S(1)}, bf16[1,4,32,512]{3,2,1,0:T(8,128)(2,1)S(1)}, u32[]{:S(2)}, u32[]{:S(2)}) collective-permute-start(bf16[1,4,32,512]{3,2,1,0:T(8,128)(2,1)S(1)} %get-tuple-element.70), channel_id=1, source_target_pairs={{0,16},{2,18},{4,20},{6,22},{8,24},{10,26},{12,28},{14,30},{16,0},... | collective-permute-start | bytes 393224 | tf_op jit(solution)/shard_map/ppermute | solution.py:288
  62.8 7.1 %collective-permute-done.17.refs_4_ = bf16[1,8,32,512]{3,2,1,0:T(8,128)(2,1)S(1)} collective-permute-done((bf16[1,8,32,512]{3,2,1,0:T(8,128)(2,1)S(1)}, bf16[1,8,32,512]{3,2,1,0:T(8,128)(2,1)S(1)}, u32[]{:S(2)}, u32[]{:S(2)}) %collective-permute-start.17) | collective-permute-done | bytes 262176 | tf_op jit(solution)/shard_map/ppermute | solution.py:288
  69.9 1.9 %collective-permute-done.19.refs_7_ = bf16[1,4,32,512]{3,2,1,0:T(8,128)(2,1)S(1)} collective-permute-done((bf16[1,4,32,512]{3,2,1,0:T(8,128)(2,1)S(1)}, bf16[1,4,32,512]{3,2,1,0:T(8,128)(2,1)S(1)}, u32[]{:S(2)}, u32[]{:S(2)}) %collective-permute-start.19) | collective-permute-done | bytes 131104 | tf_op jit(solution)/shard_map/ppermute | solution.py:288
  72.6 7.6 %collective-permute-start.21 = (bf16[2,64,512]{2,1,0:T(8,128)(2,1)S(1)}, bf16[2,64,512]{2,1,0:T(8,128)(2,1)S(1)}, u32[]{:S(2)}, u32[]{:S(2)}) collective-permute-start(bf16[2,64,512]{2,1,0:T(8,128)(2,1)S(1)} %get-tuple-element.63), channel_id=1, source_target_pairs={{0,30},{2,4},{4,2},{6,8},{8,6},{10,12},{12,10},{14,16},{16,14},{18... | collective-permute-start | bytes 393224 | tf_op jit(solution)/shard_map/ppermute | solution.py:416
  81.0 2.1 %mlp.3 = (bf16[4,64,256]{2,1,0:T(8,128)(2,1)S(1)}, bf16[4,64,256]{2,1,0:T(8,128)(2,1)S(1)}) custom-call(s32[8]{0:T(128)S(1)} %copy-done.4, s32[1]{0:T(128)S(6)} %copy.12.valid, bf16[4,64,512]{2,1,0:T(8,128)(2,1)S(1)} %combine.3.combined, bf16[3,512,256]{2,1,0:T(8,128)(2,1)S(1)} %copy-done.2, bf16[3,512,256]{2,1,0:T(8,128)(2,1)S(1)} %collective-permute-done.refs_3_.refs_1_, ...), custom_call_target="tpu_custom_call" | custom-call | bytes 7380000 | tf_op jit(solution)/shard_map/mlp/pallas_call | solution.py:420
  83.5 2.1 %mlp.2 = (bf16[4,64,256]{2,1,0:T(8,128)(2,1)S(1)}, bf16[4,64,256]{2,1,0:T(8,128)(2,1)S(1)}) custom-call(s32[8]{0:T(128)S(1)} %copy-done.4, s32[1]{0:T(128)S(6)} %copy.12.valid, bf16[4,64,512]{2,1,0:T(8,128)(2,1)S(1)} %get-tuple-element.61.combined, bf16[2,64,512]{2,1,0:T(8,128)(2,1)S(1)} %collective-permute-done.20.refs_0_, ...), custom_call_target="tpu_custom_call" | custom-call | bytes 7380000 | tf_op jit(solution)/shard_map/mlp/pallas_call | solution.py:420
  85.8 1.1 %collective-permute-done.23.refs_2_ = bf16[4,64,256]{2,1,0:T(8,128)(2,1)S(1)} collective-permute-done((bf16[4,64,256]{2,1,0:T(8,128)(2,1)S(1)}, bf16[4,64,256]{2,1,0:T(8,128)(2,1)S(1)}, u32[]{:S(2)}, u32[]{:S(2)}) %collective-permute-start.23) | collective-permute-done | bytes 131104 | tf_op jit(solution)/shard_map/ppermute | solution.py:291
  87.0 0.8 join.1
  (52 shorter events, 5.0 us)
Async XLA Ops:
  0.0 19.3 %copy-start = (bf16[1024,256]{1,0:T(8,128)(2,1)S(1)}, bf16[1024,256]{1,0:T(8,128)(2,1)}, u32[]{:S(2)}) copy-start(bf16[1024,256]{1,0:T(8,128)(2,1)} %refs_0_.4) | copy-start | bytes 1572868
  0.0 5.0 %collective-permute-start = (bf16[3,512,256]{2,1,0:T(8,128)(2,1)}, bf16[3,512,256]{2,1,0:T(8,128)(2,1)S(1)}, u32[]{:S(2)}, u32[]{:S(2)}) collective-permute-start(bf16[3,512,256]{2,1,0:T(8,128)(2,1)} %refs_0_.5), channel_id=1, source_target_pairs={{0,1},{1,0},{2,3},{3,2},{4,5},{5,4},{6,7},{7,6},{8,9},{9,8},{10,11... | collective-permute-start | bytes 2359304 | tf_op jit(solution)/shard_map/ppermute | solution.py:291
  0.5 4.6 %collective-permute-start.1 = (bf16[3,256,512]{2,1,0:T(8,128)(2,1)}, bf16[3,256,512]{2,1,0:T(8,128)(2,1)S(1)}, u32[]{:S(2)}, u32[]{:S(2)}) collective-permute-start(bf16[3,256,512]{2,1,0:T(8,128)(2,1)} %refs_2_.3), channel_id=1, source_target_pairs={{0,1},{1,0},{2,3},{3,2},{4,5},{5,4},{6,7},{7,6},{8,9},{9,8},{10,11... | collective-permute-start | bytes 2359304 | tf_op jit(solution)/shard_map/ppermute | solution.py:291
  0.5 15.8 %collective-permute-start.6 = (bf16[1024,256]{1,0:T(8,128)(2,1)}, bf16[1024,256]{1,0:T(8,128)(2,1)S(1)}, u32[]{:S(2)}, u32[]{:S(2)}) collective-permute-start(bf16[1024,256]{1,0:T(8,128)(2,1)} %refs_0_.4), channel_id=1, source_target_pairs={{0,2},{2,0},{4,6},{6,4},{8,10},{10,8},{12,14},{14,12},{16,18},{18,... | collective-permute-start | bytes 1572872 | tf_op jit(solution)/shard_map/ppermute | solution.py:285
  3.5 14.3 %collective-permute-start.8 = (bf16[1024,256]{1,0:T(8,128)(2,1)}, bf16[1024,256]{1,0:T(8,128)(2,1)S(1)}, u32[]{:S(2)}, u32[]{:S(2)}) collective-permute-start(bf16[1024,256]{1,0:T(8,128)(2,1)} %refs_0_.4), channel_id=1, source_target_pairs={{0,8},{2,10},{4,12},{6,14},{8,0},{10,2},{12,4},{14,6},{16,24},{18,... | collective-permute-start | bytes 1572872 | tf_op jit(solution)/shard_map/ppermute | solution.py:285
  5.0 1.9 %copy-start.1 = (bf16[96,128,128]{2,1,0:T(8,128)(2,1)S(1)}, bf16[96,128,128]{2,1,0:T(8,128)(2,1)}, u32[]{:S(2)}) copy-start(bf16[96,128,128]{2,1,0:T(8,128)(2,1)} %basis) | copy-start | bytes 9437188
  7.6 0.7 copy-start.6
  8.9 0.7 copy-start.8
  13.2 19.6 %collective-permute-start.3 = (bf16[1808,128]{1,0:T(8,128)(2,1)S(1)}, bf16[1808,128]{1,0:T(8,128)(2,1)S(1)}, u32[]{:S(2)}, u32[]{:S(2)}) collective-permute-start(bf16[1808,128]{1,0:T(8,128)(2,1)S(1)} %get-tuple-element.41), channel_id=1, source_target_pairs={{0,2},{2,0},{4,6},{6,4},{8,10},{10,8},{12,14},{14,12},{16,18},{18,... | collective-permute-start | bytes 1388552 | tf_op jit(solution)/shard_map/ppermute | solution.py:285
  14.8 18.1 %collective-permute-start.4 = (bf16[1808,128]{1,0:T(8,128)(2,1)S(1)}, bf16[1808,128]{1,0:T(8,128)(2,1)S(1)}, u32[]{:S(2)}, u32[]{:S(2)}) collective-permute-start(bf16[1808,128]{1,0:T(8,128)(2,1)S(1)} %get-tuple-element.42), channel_id=1, source_target_pairs={{0,8},{2,10},{4,12},{6,14},{8,0},{10,2},{12,4},{14,6},{16,24},{18,... | collective-permute-start | bytes 1388552 | tf_op jit(solution)/shard_map/ppermute | solution.py:285
  16.4 16.4 %collective-permute-start.7 = (bf16[512,256]{1,0:T(8,128)(2,1)S(1)}, bf16[512,256]{1,0:T(8,128)(2,1)S(1)}, u32[]{:S(2)}, u32[]{:S(2)}) collective-permute-start(bf16[512,256]{1,0:T(8,128)(2,1)S(1)} %slice.12), channel_id=1, source_target_pairs={{0,8},{2,10},{4,12},{6,14},{8,0},{10,2},{12,4},{14,6},{16,24},{18,... | collective-permute-start | bytes 786440 | tf_op jit(solution)/shard_map/ppermute | solution.py:285
  17.8 15.7 %collective-permute-start.9 = (bf16[512,256]{1,0:T(8,128)(2,1)S(1)}, bf16[512,256]{1,0:T(8,128)(2,1)S(1)}, u32[]{:S(2)}, u32[]{:S(2)}) collective-permute-start(bf16[512,256]{1,0:T(8,128)(2,1)S(1)} %slice.13), channel_id=1, source_target_pairs={{0,2},{2,0},{4,6},{6,4},{8,10},{10,8},{12,14},{14,12},{16,18},{18,... | collective-permute-start | bytes 786440 | tf_op jit(solution)/shard_map/ppermute | solution.py:285
  19.3 15.8 %collective-permute-start.2 = (bf16[1024,256]{1,0:T(8,128)(2,1)S(1)}, bf16[1024,256]{1,0:T(8,128)(2,1)S(1)}, u32[]{:S(2)}, u32[]{:S(2)}) collective-permute-start(bf16[1024,256]{1,0:T(8,128)(2,1)S(1)} %copy-done), channel_id=1, source_target_pairs={{0,1},{1,0},{2,3},{3,2},{4,5},{5,4},{6,7},{7,6},{8,9},{9,8},{10,11... | collective-permute-start | bytes 1572872 | tf_op jit(solution)/shard_map/ppermute | solution.py:291
  32.9 2.3 %collective-permute-start.11 = (bf16[1024,256]{1,0:T(8,128)(2,1)S(1)}, bf16[1024,256]{1,0:T(8,128)(2,1)S(1)}, u32[]{:S(2)}, u32[]{:S(2)}) collective-permute-start(bf16[1024,256]{1,0:T(8,128)(2,1)S(1)} %collective-permute-done.6.refs_4_), channel_id=1, source_target_pairs={{0,1},{1,0},{2,3},{3,2},{4,5},{5,4},{6,7},{7,6},{8,9},{9,8},{10,11... | collective-permute-start | bytes 1572872 | tf_op jit(solution)/shard_map/ppermute | solution.py:291
  32.9 2.6 %collective-permute-start.12 = (bf16[1024,256]{1,0:T(8,128)(2,1)S(1)}, bf16[1024,256]{1,0:T(8,128)(2,1)S(1)}, u32[]{:S(2)}, u32[]{:S(2)}) collective-permute-start(bf16[1024,256]{1,0:T(8,128)(2,1)S(1)} %collective-permute-done.8.refs_5_), channel_id=1, source_target_pairs={{0,1},{1,0},{2,3},{3,2},{4,5},{5,4},{6,7},{7,6},{8,9},{9,8},{10,11... | collective-permute-start | bytes 1572872 | tf_op jit(solution)/shard_map/ppermute | solution.py:291
  33.5 9.3 %collective-permute-start.10 = (bf16[1024,256]{1,0:T(8,128)(2,1)S(1)}, bf16[1024,256]{1,0:T(8,128)(2,1)S(1)}, u32[]{:S(2)}, u32[]{:S(2)}) collective-permute-start(bf16[1024,256]{1,0:T(8,128)(2,1)S(1)} %constant_dynamic-update-slice_fusion.mine), channel_id=1, source_target_pairs={{0,1},{1,0},{2,3},{3,2},{4,5},{5,4},{6,7},{7,6},{8,9},{9,8},{10,11... | collective-permute-start | bytes 1572872 | tf_op jit(solution)/shard_map/ppermute | solution.py:291
  33.6 9.1 %collective-permute-start.5 = (bf16[912,128]{1,0:T(8,128)(2,1)S(1)}, bf16[912,128]{1,0:T(8,128)(2,1)S(1)}, u32[]{:S(2)}, u32[]{:S(2)}) collective-permute-start(bf16[912,128]{1,0:T(8,128)(2,1)S(1)} %get-tuple-element.43), channel_id=1, source_target_pairs={{0,10},{2,8},{4,14},{6,12},{8,2},{10,0},{12,6},{14,4},{16,26},{18,... | collective-permute-start | bytes 700424 | tf_op jit(solution)/shard_map/ppermute | solution.py:285
  38.6 9.9 %collective-permute-start.13 = (bf16[1088,128]{1,0:T(8,128)(2,1)S(1)}, bf16[1088,128]{1,0:T(8,128)(2,1)S(1)}, u32[]{:S(2)}, u32[]{:S(2)}) collective-permute-start(bf16[1088,128]{1,0:T(8,128)(2,1)S(1)} %get-tuple-element.52), channel_id=1, source_target_pairs={{0,10},{2,8},{4,14},{6,12},{8,2},{10,0},{12,6},{14,4},{16,26},{18,... | collective-permute-start | bytes 835592 | tf_op jit(solution)/shard_map/ppermute | solution.py:285
  44.4 7.7 %collective-permute-start.16 = (bf16[1,8,32,512]{3,2,1,0:T(8,128)(2,1)S(1)}, bf16[1,8,32,512]{3,2,1,0:T(8,128)(2,1)S(1)}, u32[]{:S(2)}, u32[]{:S(2)}) collective-permute-start(bf16[1,8,32,512]{3,2,1,0:T(8,128)(2,1)S(1)} %get-tuple-element.56), channel_id=1, source_target_pairs={{0,4},{2,6},{4,0},{6,2},{8,12},{10,14},{12,8},{14,10},{16,20},{18,... | collective-permute-start | bytes 786440 | tf_op jit(solution)/shard_map/ppermute | solution.py:288
  50.1 30.8 %copy-start.2 = (bf16[3,512,256]{2,1,0:T(8,128)(2,1)S(1)}, bf16[3,512,256]{2,1,0:T(8,128)(2,1)}, u32[]{:S(2)}) copy-start(bf16[3,512,256]{2,1,0:T(8,128)(2,1)} %refs_0_.5) | copy-start | bytes 2359300
  50.1 30.8 %copy-start.3 = (bf16[3,256,512]{2,1,0:T(8,128)(2,1)S(1)}, bf16[3,256,512]{2,1,0:T(8,128)(2,1)}, u32[]{:S(2)}) copy-start(bf16[3,256,512]{2,1,0:T(8,128)(2,1)} %refs_2_.3) | copy-start | bytes 2359300
  50.2 30.8 %copy-start.4 = (s32[8]{0:T(128)S(1)}, s32[8]{0:T(128)}, u32[]{:S(2)}) copy-start(s32[8]{0:T(128)} %reverse.3) | copy-start | bytes 100
  50.2 7.8 %collective-permute-start.14 = (bf16[1,8,32,512]{3,2,1,0:T(8,128)(2,1)S(1)}, bf16[1,8,32,512]{3,2,1,0:T(8,128)(2,1)S(1)}, u32[]{:S(2)}, u32[]{:S(2)}) collective-permute-start(bf16[1,8,32,512]{3,2,1,0:T(8,128)(2,1)S(1)} %get-tuple-element.53), channel_id=1, source_target_pairs={{0,4},{2,6},{4,0},{6,2},{8,12},{10,14},{12,8},{14,10},{16,20},{18,... | collective-permute-start | bytes 786440 | tf_op jit(solution)/shard_map/ppermute | solution.py:288
  52.2 17.7 %collective-permute-start.17 = (bf16[1,8,32,512]{3,2,1,0:T(8,128)(2,1)S(1)}, bf16[1,8,32,512]{3,2,1,0:T(8,128)(2,1)S(1)}, u32[]{:S(2)}, u32[]{:S(2)}) collective-permute-start(bf16[1,8,32,512]{3,2,1,0:T(8,128)(2,1)S(1)} %add_convert_fusion.1), channel_id=1, source_target_pairs={{0,16},{2,18},{4,20},{6,22},{8,24},{10,26},{12,28},{14,30},{16,0},... | collective-permute-start | bytes 786440 | tf_op jit(solution)/shard_map/ppermute | solution.py:288
  58.0 13.8 %collective-permute-start.18 = (bf16[1,8,32,512]{3,2,1,0:T(8,128)(2,1)S(1)}, bf16[1,8,32,512]{3,2,1,0:T(8,128)(2,1)S(1)}, u32[]{:S(2)}, u32[]{:S(2)}) collective-permute-start(bf16[1,8,32,512]{3,2,1,0:T(8,128)(2,1)S(1)} %get-tuple-element.59), channel_id=1, source_target_pairs={{0,4},{2,6},{4,0},{6,2},{8,12},{10,14},{12,8},{14,10},{16,20},{18,... | collective-permute-start | bytes 786440 | tf_op jit(solution)/shard_map/ppermute | solution.py:288
  59.5 12.3 %collective-permute-start.15 = (bf16[1,8,32,512]{3,2,1,0:T(8,128)(2,1)S(1)}, bf16[1,8,32,512]{3,2,1,0:T(8,128)(2,1)S(1)}, u32[]{:S(2)}, u32[]{:S(2)}) collective-permute-start(bf16[1,8,32,512]{3,2,1,0:T(8,128)(2,1)S(1)} %get-tuple-element.54), channel_id=1, source_target_pairs={{0,4},{2,6},{4,0},{6,2},{8,12},{10,14},{12,8},{14,10},{16,20},{18,... | collective-permute-start | bytes 786440 | tf_op jit(solution)/shard_map/ppermute | solution.py:288
  60.1 11.7 %collective-permute-start.19 = (bf16[1,4,32,512]{3,2,1,0:T(8,128)(2,1)S(1)}, bf16[1,4,32,512]{3,2,1,0:T(8,128)(2,1)S(1)}, u32[]{:S(2)}, u32[]{:S(2)}) collective-permute-start(bf16[1,4,32,512]{3,2,1,0:T(8,128)(2,1)S(1)} %get-tuple-element.70), channel_id=1, source_target_pairs={{0,16},{2,18},{4,20},{6,22},{8,24},{10,26},{12,28},{14,30},{16,0},... | collective-permute-start | bytes 393224 | tf_op jit(solution)/shard_map/ppermute | solution.py:288
  69.9 10.9 %collective-permute-start.22 = (bf16[1,4,32,512]{3,2,1,0:T(8,128)(2,1)S(1)}, bf16[1,4,32,512]{3,2,1,0:T(8,128)(2,1)S(1)}, u32[]{:S(2)}, u32[]{:S(2)}) collective-permute-start(bf16[1,4,32,512]{3,2,1,0:T(8,128)(2,1)S(1)} %get-tuple-element.65), channel_id=1, source_target_pairs={{0,16},{2,18},{4,20},{6,22},{8,24},{10,26},{12,28},{14,30},{16,0},... | collective-permute-start | bytes 393224 | tf_op jit(solution)/shard_map/ppermute | solution.py:288
  72.0 11.2 %collective-permute-start.20 = (bf16[2,64,512]{2,1,0:T(8,128)(2,1)S(1)}, bf16[2,64,512]{2,1,0:T(8,128)(2,1)S(1)}, u32[]{:S(2)}, u32[]{:S(2)}) collective-permute-start(bf16[2,64,512]{2,1,0:T(8,128)(2,1)S(1)} %get-tuple-element.62), channel_id=1, source_target_pairs={{0,2},{2,0},{4,6},{6,4},{8,10},{10,8},{12,14},{14,12},{16,18},{18,... | collective-permute-start | bytes 393224 | tf_op jit(solution)/shard_map/ppermute | solution.py:417
  72.6 10.9 %collective-permute-start.21 = (bf16[2,64,512]{2,1,0:T(8,128)(2,1)S(1)}, bf16[2,64,512]{2,1,0:T(8,128)(2,1)S(1)}, u32[]{:S(2)}, u32[]{:S(2)}) collective-permute-start(bf16[2,64,512]{2,1,0:T(8,128)(2,1)S(1)} %get-tuple-element.63), channel_id=1, source_target_pairs={{0,30},{2,4},{4,2},{6,8},{8,6},{10,12},{12,10},{14,16},{16,14},{18... | collective-permute-start | bytes 393224 | tf_op jit(solution)/shard_map/ppermute | solution.py:416
  83.1 2.7 %collective-permute-start.24 = (bf16[4,64,256]{2,1,0:T(8,128)(2,1)S(1)}, bf16[4,64,256]{2,1,0:T(8,128)(2,1)S(1)}, u32[]{:S(2)}, u32[]{:S(2)}) collective-permute-start(bf16[4,64,256]{2,1,0:T(8,128)(2,1)S(1)} %get-tuple-element.68), channel_id=1, source_target_pairs={{0,1},{1,0},{2,3},{3,2},{4,5},{5,4},{6,7},{7,6},{8,9},{9,8},{10,11... | collective-permute-start | bytes 393224 | tf_op jit(solution)/shard_map/ppermute | solution.py:291
  85.6 1.4 %collective-permute-start.23 = (bf16[4,64,256]{2,1,0:T(8,128)(2,1)S(1)}, bf16[4,64,256]{2,1,0:T(8,128)(2,1)S(1)}, u32[]{:S(2)}, u32[]{:S(2)}) collective-permute-start(bf16[4,64,256]{2,1,0:T(8,128)(2,1)S(1)} %get-tuple-element.67), channel_id=1, source_target_pairs={{0,1},{1,0},{2,3},{3,2},{4,5},{5,4},{6,7},{7,6},{8,9},{9,8},{10,11... | collective-permute-start | bytes 393224 | tf_op jit(solution)/shard_map/ppermute | solution.py:291
  (2 other events, 1.3 us)
